TPU v7x, 128 devices: a whole 4x4x4 slice. The times are simulated.
128 devices in a mesh: row: 8 (over z, core), col: 16 (over y, x).
Axes of the slice: x: 4, y: 4, z: 4, core: 2. Of those that a mesh axis runs over, the one named last changes fastest.
Arguments:
- single: bfloat16 [65536, 384], P(('row', 'col')), may hold values from -20 to 20
- left_weight: bfloat16 [384, 128], replicated, may hold values from -0.3125 to 0.3125
- right_weight: bfloat16 [384, 128], replicated, may hold values from -0.3125 to 0.3125
- bin_weight: bfloat16 [128, 64], replicated, may hold values from -3 to 3
- bin_bias: float32 [64], replicated, may hold values from -4 to 4
- block_tiles: int32 [128, 8, 2], P(('row', 'col')), may hold values from 0 to 511, as said below
- block_count: int32 [128], P(('row', 'col')), may hold values from 1 to 8, as said below
- teacher: bfloat16 [128, 8, 64, 128, 128], P(('row', 'col')), may hold values from 0 to 1, as said below
Outputs:
- grad_single: bfloat16 [65536, 384], P(('row', 'col'))
- grad_left: float32 [384, 128], replicated
- grad_right: float32 [384, 128], replicated
- grad_bin: float32 [128, 64], replicated
- loss: float32 [], replicated
Inputs may be any that keep to these rules, and one draw needn't show every extreme that they name: `block_tiles`: for the device at mesh position (r, c), with tile t held by device t // 4 in row-major mesh order, each slot's row tile is held by a device of mesh row r and its column tile by a device of mesh column c. Slots 2m and 2m + 1 take their row tiles from one device and their column tiles from one device; different m take them from different devices, so at most two slots of a device name tiles of any one device on each side. Slots from block_count on are ignored. `block_count`: counts differ from device to device; some device holds 8 kept blocks. `teacher`: each pair's probabilities over the bins are positive and sum to one up to bfloat16 rounding.
All inputs are finite; a program needn't handle non-finite values.
Results may differ from a plain program's by a relative error of at most 0.011.
Values may be sent and summed in bfloat16 or wider, within the bound.
No kernel may reach another device: no remote copies, remote signals or barrier semaphores. Data moves between devices by JAX's collectives and lax.ppermute only.
A program may use at most 64 MiB of HBM per device.

v0:
```python
import jax
import jax.numpy as jnp
from jax import lax
from jax.sharding import PartitionSpec as P


def block_terms(left_tile, right_tile, bin_weight, bin_bias, target_block):
    weight_wide = bin_weight.astype(jnp.float32)
    scaled = (left_tile.astype(jnp.float32)[None, :, :] * weight_wide.T[:, None, :]).astype(
        jnp.bfloat16
    )
    logits = jnp.einsum("kpc,qc->kpq", scaled, right_tile, preferred_element_type=jnp.float32)
    logits = logits + bin_bias[:, None, None]
    highest = jnp.max(logits, axis=0, keepdims=True)
    shifted = logits - highest
    log_prob = shifted - jnp.log(jnp.sum(jnp.exp(shifted), axis=0, keepdims=True))
    target = target_block.astype(jnp.float32)
    cross_sum = -jnp.sum(target * log_prob)
    target_mass = jnp.sum(target, axis=0, keepdims=True)
    grad_logits = (target_mass * jnp.exp(log_prob) - target).astype(jnp.bfloat16)
    mixed_grad = jnp.einsum(
        "kpq,qc->kpc", grad_logits, right_tile, preferred_element_type=jnp.float32
    )
    grad_left_tile = jnp.sum(mixed_grad * weight_wide.T[:, None, :], axis=0)
    grad_right_tile = jnp.einsum(
        "kpq,kpc->qc", grad_logits, scaled, preferred_element_type=jnp.float32
    )
    grad_bin_tile = jnp.sum(mixed_grad * left_tile.astype(jnp.float32)[None, :, :], axis=1).T
    return (grad_left_tile, grad_right_tile, grad_bin_tile, cross_sum)


def per_device(
    single, left_weight, right_weight, bin_weight, bin_bias, block_tiles, block_count, teacher
):
    tile_size = teacher.shape[-1]
    col_count = lax.axis_size("col")
    devices = lax.axis_size(("row", "col"))
    tiles_dev = single.shape[0] // tile_size
    own_tiles = block_tiles[0]
    own_count = block_count[0]
    own_targets = teacher[0]
    left_wide = left_weight.astype(jnp.float32)
    right_wide = right_weight.astype(jnp.float32)
    left_local = jnp.dot(single, left_weight, preferred_element_type=jnp.float32).astype(
        jnp.bfloat16
    )
    right_local = jnp.dot(single, right_weight, preferred_element_type=jnp.float32).astype(
        jnp.bfloat16
    )
    width = left_local.shape[1]
    row_peer = own_tiles[:, 0] // tiles_dev % col_count
    col_peer = own_tiles[:, 1] // tiles_dev // col_count
    row_inner = own_tiles[:, 0] % tiles_dev
    col_inner = own_tiles[:, 1] % tiles_dev
    row_place = row_peer * tiles_dev + row_inner
    col_place = col_peer * tiles_dev + col_inner
    row_bank = lax.all_gather(left_local, "col", axis=0, tiled=True).reshape(-1, tile_size, width)
    col_bank = lax.all_gather(right_local, "row", axis=0, tiled=True).reshape(-1, tile_size, width)
    initial = (
        jnp.zeros(row_bank.shape, jnp.float32),
        jnp.zeros(col_bank.shape, jnp.float32),
        jnp.zeros(bin_weight.shape, jnp.float32),
        jnp.zeros((), jnp.float32),
    )

    def block_step(slot_index, carried):
        row_acc, col_acc, part_bin, cross_total = carried
        row_spot = row_place[slot_index]
        col_spot = col_place[slot_index]
        grad_left_tile, grad_right_tile, grad_bin_tile, cross_sum = block_terms(
            row_bank[row_spot], col_bank[col_spot], bin_weight, bin_bias, own_targets[slot_index]
        )
        row_acc = lax.dynamic_update_index_in_dim(
            row_acc, row_acc[row_spot] + grad_left_tile, row_spot, 0
        )
        col_acc = lax.dynamic_update_index_in_dim(
            col_acc, col_acc[col_spot] + grad_right_tile, col_spot, 0
        )
        return (row_acc, col_acc, part_bin + grad_bin_tile, cross_total + cross_sum)

    row_acc, col_acc, part_bin, cross_total = lax.fori_loop(0, own_count, block_step, initial)
    left_rows_grad = lax.psum_scatter(
        row_acc.reshape(-1, width), "col", scatter_dimension=0, tiled=True
    )
    right_rows_grad = lax.psum_scatter(
        col_acc.reshape(-1, width), "row", scatter_dimension=0, tiled=True
    )
    grad_single = (
        jnp.dot(left_rows_grad, left_wide.T, precision=lax.Precision.HIGHEST)
        + jnp.dot(right_rows_grad, right_wide.T, precision=lax.Precision.HIGHEST)
    ).astype(jnp.bfloat16)
    single_wide = single.astype(jnp.float32)
    part_left = jnp.dot(single_wide.T, left_rows_grad, precision=lax.Precision.HIGHEST)
    part_right = jnp.dot(single_wide.T, right_rows_grad, precision=lax.Precision.HIGHEST)
    totals = lax.psum(
        (part_left, part_right, part_bin, cross_total, own_count.astype(jnp.float32)),
        ("row", "col"),
    )
    grad_left = totals[0] / devices
    grad_right = totals[1] / devices
    grad_bin = totals[2] / devices
    loss_value = totals[3] / (totals[4] * (tile_size * tile_size))
    return (grad_single, grad_left, grad_right, grad_bin, loss_value)


def solution(mesh):
    return jax.shard_map(
        per_device,
        mesh=mesh,
        in_specs=(
            P(("row", "col"), None),
            P(),
            P(),
            P(),
            P(),
            P(("row", "col"), None, None),
            P(("row", "col")),
            P(("row", "col"), None, None, None, None),
        ),
        out_specs=(P(("row", "col"), None), P(), P(), P(), P()),
        check_vma=False,
    )
```

profile of v0, /device:TPU:1, one launch (start us, length us, event | category | flops | bytes accessed | tf_op | source)
XLA Modules:
  0.0 513.0 jit_solution(279906347958925368)
XLA Ops:
  7.2 0.9 copy-done
  8.2 1.8 convolution_convert_fusion
  10.1 1.8 convolution_convert_fusion.1
  11.9 0.8 fusion.24
  12.7 24.9 %all-gather.5.cloned.1.call-done = bf16[4096,128]{1,0:T(8,128)(2,1)} async-done(((bf16[512,128]{1,0:T(8,128)(2,1)}), bf16[4096,128]{1,0:T(8,128)(2,1)}) %all-gather.5.cloned.1.call-update) | async-done | bytes 1048592 | tf_op jit(solution)/shard_map/all_gather | solution.py:58
  37.6 46.2 %all-gather.3.cloned.1.call-done = bf16[8192,128]{1,0:T(8,128)(2,1)} async-done(((bf16[512,128]{1,0:T(8,128)(2,1)}), bf16[8192,128]{1,0:T(8,128)(2,1)}) %all-gather.3.cloned.1.call-update) | async-done | bytes 2097168 | tf_op jit(solution)/shard_map/all_gather | solution.py:57
  83.7 2.4 broadcast_in_dim.10
  86.5 20.0 %while.16 = (s32[]{:T(128)}, f32[64,128,128]{2,1,0:T(8,128)}, f32[32,128,128]{2,1,0:T(8,128)S(1)}, f32[128,64]{0,1:T(8,128)S(1)}, f32[]{:T(128)}, /*index=5*/s32...) while((s32[]{:T(128)}, f32[64,128,128]{2,1,0:T(8,128)}, ...), condition=%wide.region_7.8_spmd, body=%wide.region_0.7_spmd.sunk | while | flops 830464000 | bytes 24822876 | solution.py:81
  93.0 1.5 add_reduce_fusion.2
  95.3 1.9 convert_reduce_fusion.2
  97.2 4.1 fusion.49
  101.3 1.6 multiply_reduce_fusion.3
  102.9 1.5 fusion.50
  106.5 1.3 copy-done.1
  109.1 199.5 %all-reduce = (f32[128,64]{0,1:T(8,128)S(1)}, f32[]{:T(128)}, f32[]{:T(128)}) all-reduce(f32[128,64]{0,1:T(8,128)S(1)} %get-tuple-element.78, f32[]{:T(128)} %get-tuple-element.79, f32[]{:T(128)S(6)} %convert_element_type.40), channel_id=1, replica_groups=mesh['row'=8,'col'=16] {'row','col'}, use_global_device_ids=true, to_apply=%region_12.13 | all-reduce | flops 8194 | bytes 65552 | tf_op jit(solution)/shard_map/psum | solution.py:95
  310.5 2.1 convolution_bitcast_fusion
  312.6 38.8 %reduce-scatter.3.cloned.1.call-done = f32[512,128]{1,0:T(8,128)} async-done(((f32[8192,128]{1,0:T(8,128)}), f32[512,128]{1,0:T(8,128)}) %reduce-scatter.3.cloned.1.call-update) | async-done | bytes 262160 | tf_op jit(solution)/shard_map/reduce_scatter | solution.py:82
  351.4 2.1 convolution_bitcast_fusion.1
  353.5 1.4 fusion.27
  354.9 2.2 fusion.22
  357.1 145.6 %all-reduce.4.cloned.1.call-done = (f32[384,128]{0,1:T(8,128)}, f32[384,128]{0,1:T(8,128)}) async-done(((f32[384,128]{0,1:T(8,128)}, f32[384,128]{0,1:T(8,128)}), (f32[384,128]{0,1:T(8,128)}, f32[384,128]{0,1:T(8,128)})) %all-reduce.4.cloned.1.call-update) | async-done | bytes 393232 | tf_op jit(solution)/shard_map/psum | solution.py:95
  502.7 1.0 broadcast_multiply_fusion
  503.7 0.8 copy.18
  504.5 0.8 copy.19
  (32 shorter events, 5.1 us)
Async XLA Ops:
  7.2 1.0 copy-start
  7.2 79.3 %copy-start.2 = (bf16[128,64]{0,1:T(8,128)(2,1)S(1)}, bf16[128,64]{0,1:T(8,128)(2,1)}, u32[]{:S(2)}) copy-start(bf16[128,64]{0,1:T(8,128)(2,1)} %param.13) | copy-start | bytes 49156
  7.2 79.3 %copy-start.5 = (f32[64]{0:T(128)S(1)}, f32[64]{0:T(128)}, u32[]{:S(2)}) copy-start(f32[64]{0:T(128)} %param.14) | copy-start | bytes 772
  7.2 30.4 %all-gather.5.cloned.1.call-start = ((), (), s32[]{:S(2)}) async-start(), calls=%async_computation.3 | async-start | bytes 1179648 | tf_op jit(solution)/shard_map/all_gather | solution.py:58
  10.0 73.7 %all-gather.3.cloned.1.call-start = ((), (), s32[]{:S(2)}) async-start(), calls=%async_computation.2 | async-start | bytes 2228224 | tf_op jit(solution)/shard_map/all_gather | solution.py:57
  11.9 298.6 %reduce-scatter.5.cloned.1.call-start = ((), (), s32[]{:S(2)}) async-start(), calls=%async_computation.5 | async-start | bytes 2359296 | tf_op jit(solution)/shard_map/reduce_scatter | solution.py:85
  106.5 1.3 copy-start.1
  106.5 247.0 %copy-start.3 = (bf16[384,128]{1,0:T(8,128)(2,1)S(1)}, bf16[384,128]{1,0:T(8,128)(2,1)}, u32[]{:S(2)}) copy-start(bf16[384,128]{1,0:T(8,128)(2,1)} %param.11) | copy-start | bytes 294916
  107.8 247.1 %copy-start.4 = (bf16[384,128]{1,0:T(8,128)(2,1)S(1)}, bf16[384,128]{1,0:T(8,128)(2,1)}, u32[]{:S(2)}) copy-start(bf16[384,128]{1,0:T(8,128)(2,1)} %param.12) | copy-start | bytes 294916
  107.8 243.5 %reduce-scatter.3.cloned.1.call-start = ((), (), s32[]{:S(2)}) async-start(), calls=%async_computation.4 | async-start | bytes 4456448 | tf_op jit(solution)/shard_map/reduce_scatter | solution.py:82
  108.4 394.2 %all-reduce.4.cloned.1.call-start = ((), (), s32[]{:S(2)}) async-start(), calls=%async_computation.6 | async-start | bytes 786432 | tf_op jit(solution)/shard_map/psum | solution.py:95
Sparse Core Ops, SparseCore 0:
  10.3 27.2 all-gather.4
  40.3 43.4 all-gather.2
  108.0 162.4 reduce-scatter.4
  273.6 77.7 reduce-scatter.2
  357.3 145.3 all-reduce.3
where the time goes:
time: 517 us; the launch traced here: 513 us
  waiting for transfers between devices  256 us (50%)
  blocking collectives  199 us (38%)
  between operations  17 us (3%)
  matrix products  15.3 us (3%)
  other arithmetic  11.5 us (2%)
  local copies, waits for them, and re-layouts  7.74 us (1%)
  loops' own time  5.91 us (1%)
    psum x1, blocking collectives, per_device(): lax.psum((part_left, part_right, part_bin, cross_total, own_count.astype(...  199 us
    psum x1, waiting for transfers between devices, per_device(): lax.psum((part_left, part_right, part_bin, cross_total, own_count.astype(...  146 us
    all_gather x1, waiting for transfers between devices, per_device(): lax.all_gather(left_local, 'col', axis=0, tiled=True)  46.2 us
    reduce_scatter x1, waiting for transfers between devices, per_device(): lax.psum_scatter(row_acc.reshape(-1, width), 'col', scatter_dimension=0,...  38.8 us
    all_gather x1, waiting for transfers between devices, per_device(): lax.all_gather(right_local, 'row', axis=0, tiled=True)  24.9 us
  transfers between devices with their start and end apart: 5, of which 4 were waited for; matrix products, arithmetic and copies ran while one was open for 2% of the time, Pallas kernels for 0%

commit v1 on v0

v1 whole, which is shorter than its diff:
```python
import jax
import jax.numpy as jnp
from jax import lax
from jax.sharding import Mesh
from jax.sharding import PartitionSpec as P

AXES = ("z", "core", "y", "x")


def block_terms(left_tile, right_tile, bin_weight, bin_bias, target_block):
    weight_wide = bin_weight.astype(jnp.float32)
    scaled = (left_tile.astype(jnp.float32)[None, :, :] * weight_wide.T[:, None, :]).astype(
        jnp.bfloat16
    )
    logits = jnp.einsum("kpc,qc->kpq", scaled, right_tile, preferred_element_type=jnp.float32)
    logits = logits + bin_bias[:, None, None]
    highest = jnp.max(logits, axis=0, keepdims=True)
    shifted = logits - highest
    log_prob = shifted - jnp.log(jnp.sum(jnp.exp(shifted), axis=0, keepdims=True))
    target = target_block.astype(jnp.float32)
    cross_sum = -jnp.sum(target * log_prob)
    target_mass = jnp.sum(target, axis=0, keepdims=True)
    grad_logits = (target_mass * jnp.exp(log_prob) - target).astype(jnp.bfloat16)
    mixed_grad = jnp.einsum(
        "kpq,qc->kpc", grad_logits, right_tile, preferred_element_type=jnp.float32
    )
    grad_left_tile = jnp.sum(mixed_grad * weight_wide.T[:, None, :], axis=0)
    grad_right_tile = jnp.einsum(
        "kpq,kpc->qc", grad_logits, scaled, preferred_element_type=jnp.float32
    )
    grad_bin_tile = jnp.sum(mixed_grad * left_tile.astype(jnp.float32)[None, :, :], axis=1).T
    return (grad_left_tile, grad_right_tile, grad_bin_tile, cross_sum)


def shift(value, axis, step):
    size = lax.axis_size(axis)
    return lax.ppermute(value, axis, [(i, (i + step) % size) for i in range(size)])


def spread(value, axis):
    return jnp.stack([value] + [shift(value, axis, s) for s in range(1, lax.axis_size(axis))])


def collect(parts, axis):
    total = parts[0].astype(jnp.float32)
    for s in range(1, lax.axis_size(axis)):
        total = total + shift(parts[s].astype(jnp.bfloat16), axis, s).astype(jnp.float32)
    return total


def per_device(
    single, left_weight, right_weight, bin_weight, bin_bias, block_tiles, block_count, teacher
):
    tile = teacher.shape[-1]
    bins = bin_weight.shape[1]
    devices = lax.axis_size(AXES)
    tiles_dev = single.shape[0] // tile
    own_tiles = block_tiles[0]
    own_count = block_count[0]
    own_targets = teacher[0]
    left_wide = left_weight.astype(jnp.float32)
    right_wide = right_weight.astype(jnp.float32)
    left_local = jnp.dot(single, left_weight, preferred_element_type=jnp.float32).astype(
        jnp.bfloat16
    )
    right_local = jnp.dot(single, right_weight, preferred_element_type=jnp.float32).astype(
        jnp.bfloat16
    )
    width = left_local.shape[1]
    z, core, y, x = (lax.axis_index(a) for a in AXES)
    row_home = own_tiles[:, 0] // tiles_dev
    col_home = own_tiles[:, 1] // tiles_dev
    row_inner = own_tiles[:, 0] % tiles_dev
    col_inner = own_tiles[:, 1] % tiles_dev
    far_y = (row_home // 4 % 4 - y) % 4
    far_x = (row_home % 4 - x) % 4
    far_z = (col_home // 32 - z) % 4
    far_core = (col_home // 16 % 2 - core) % 2
    row_from = (((-far_y) % 4) * 4 + (-far_x) % 4) * tiles_dev + row_inner
    row_to = (far_y * 4 + far_x) * tiles_dev + row_inner
    col_from = (far_core * 4 + (-far_z) % 4) * tiles_dev + col_inner
    col_to = (far_core * 4 + far_z) * tiles_dev + col_inner
    row_bank = spread(spread(left_local, "x"), "y").reshape(-1, tile, width)
    col_bank = spread(spread(right_local, "z"), "core").reshape(-1, tile, width)
    initial = (
        jnp.zeros(row_bank.shape, jnp.float32),
        jnp.zeros(col_bank.shape, jnp.float32),
        jnp.zeros(bin_weight.shape, jnp.float32),
        jnp.zeros((), jnp.float32),
    )

    def block_step(slot_index, carried):
        row_acc, col_acc, part_bin, cross_total = carried
        row_spot = row_to[slot_index]
        col_spot = col_to[slot_index]
        grad_left_tile, grad_right_tile, grad_bin_tile, cross_sum = block_terms(
            row_bank[row_from[slot_index]],
            col_bank[col_from[slot_index]],
            bin_weight,
            bin_bias,
            own_targets[slot_index],
        )
        row_acc = lax.dynamic_update_index_in_dim(
            row_acc, row_acc[row_spot] + grad_left_tile, row_spot, 0
        )
        col_acc = lax.dynamic_update_index_in_dim(
            col_acc, col_acc[col_spot] + grad_right_tile, col_spot, 0
        )
        return (row_acc, col_acc, part_bin + grad_bin_tile, cross_total + cross_sum)

    row_acc, col_acc, part_bin, cross_total = lax.fori_loop(0, own_count, block_step, initial)
    rows_dev = single.shape[0]
    left_rows_grad = collect(
        collect(row_acc.reshape(4, 4, rows_dev, width), "y"), "x"
    )
    right_rows_grad = collect(
        collect(col_acc.reshape(2, 4, rows_dev, width), "core"), "z"
    )
    grad_single = (
        jnp.dot(left_rows_grad, left_wide.T, precision=lax.Precision.HIGHEST)
        + jnp.dot(right_rows_grad, right_wide.T, precision=lax.Precision.HIGHEST)
    ).astype(jnp.bfloat16)
    single_wide = single.astype(jnp.float32)
    part_left = jnp.dot(single_wide.T, left_rows_grad, precision=lax.Precision.HIGHEST)
    part_right = jnp.dot(single_wide.T, right_rows_grad, precision=lax.Precision.HIGHEST)
    depth = part_left.shape[0]
    rows_sum = 2 * depth + bins
    chunk = -(-(rows_sum + 1) // devices)
    scalars = jnp.stack([cross_total, own_count.astype(jnp.float32)])
    packed = jnp.concatenate(
        [
            part_left,
            part_right,
            part_bin.T,
            jnp.pad(scalars[None], ((0, chunk * devices - rows_sum - 1), (0, width - 2))),
        ]
    ).reshape(devices, chunk, width)
    mine = jnp.sum(lax.all_to_all(packed, AXES, 0, 0), axis=0)
    totals = lax.all_to_all(
        jnp.broadcast_to(mine[None], (devices, chunk, width)), AXES, 0, 0
    ).reshape(-1, width)
    grad_left = totals[:depth] / devices
    grad_right = totals[depth : 2 * depth] / devices
    grad_bin = totals[2 * depth : rows_sum].T / devices
    loss_value = totals[rows_sum, 0] / (totals[rows_sum, 1] * (tile * tile))
    return (grad_single, grad_left, grad_right, grad_bin, loss_value)


def solution(mesh):
    torus = Mesh(mesh.devices.reshape(4, 2, 4, 4), AXES)
    return jax.shard_map(
        per_device,
        mesh=torus,
        in_specs=(
            P(AXES, None),
            P(),
            P(),
            P(),
            P(),
            P(AXES, None, None),
            P(AXES),
            P(AXES, None, None, None, None),
        ),
        out_specs=(P(AXES, None), P(), P(), P(), P()),
        check_vma=False,
    )
```

time: 517 us -> 351 us (0.68); the launches traced: 513 us -> 352 us
  starting transfers between devices: 0.2 us -> 222 us
  waiting for transfers between devices: 256 us -> 43.3 us
  blocking collectives: 199 us -> 22.5 us
  between operations: 17 us -> 3.96 us
  local copies, waits for them, and re-layouts: 7.74 us -> 18.9 us
  other arithmetic: 11.5 us -> 20.2 us
    ppermute x0 -> x20, starting transfers between devices: none -> 218 us  [shift(): lax.ppermute(value, axis, [(i, (i + step) % size) for i in range(size)])]
    psum x1 -> x0, blocking collectives: 199 us -> none  [per_device(): lax.psum((part_left, part_right, part_bin, cross_total, own_count.astype(...]
    psum x1 -> x0, waiting for transfers between devices: 146 us -> none  [per_device(): lax.psum((part_left, part_right, part_bin, cross_total, own_count.astype(...]
    all_gather x2 -> x0, waiting for transfers between devices: 71 us -> none  [the longest x1 46.2 us: per_device(): lax.all_gather(left_local, 'col', axis=0, tiled=True)]
    reduce_scatter x2 -> x0, waiting for transfers between devices: 38.8 us -> none  [the longest x1 38.8 us: per_device(): lax.psum_scatter(row_acc.reshape(-1, width), 'col', scatter_dimension=0,...]
    ppermute x0 -> x20, waiting for transfers between devices: none -> 33.2 us  [shift(): lax.ppermute(value, axis, [(i, (i + step) % size) for i in range(size)])]
    all_to_all x0 -> x1, blocking collectives: none -> 22.5 us  [per_device(): mine = jnp.sum(lax.all_to_all(packed, AXES, 0, 0), axis=0)]
    all_to_all x0 -> x1, waiting for transfers between devices: none -> 10.1 us  [per_device(): lax.all_to_all(jnp.broadcast_to(mine[None], (devices, chunk, width)), AXE...]
  transfers between devices with their start and end apart: 5 -> 21, of which waited for: 4 -> 10; matrix products, arithmetic and copies ran while one was open for 2% -> 4% of each run, Pallas kernels for 0% -> 0%
where the time goes in v1:
time: 351 us; the launch traced here: 352 us
  starting transfers between devices  222 us (63%)
  waiting for transfers between devices  43.3 us (12%)
  blocking collectives  22.5 us (6%)
  other arithmetic  20.2 us (6%)
  local copies, waits for them, and re-layouts  18.9 us (5%)
  matrix products  11.6 us (3%)
  loops' own time  9.79 us (3%)
  between operations  3.96 us (1%)
    ppermute x20, starting transfers between devices, shift(): lax.ppermute(value, axis, [(i, (i + step) % size) for i in range(size)])  218 us
    ppermute x20, waiting for transfers between devices, shift(): lax.ppermute(value, axis, [(i, (i + step) % size) for i in range(size)])  33.2 us
    all_to_all x1, blocking collectives, per_device(): mine = jnp.sum(lax.all_to_all(packed, AXES, 0, 0), axis=0)  22.5 us
    all_to_all x1, waiting for transfers between devices, per_device(): lax.all_to_all(jnp.broadcast_to(mine[None], (devices, chunk, width)), AXE...  10.1 us
    another operation x1, loops' own time, per_device(): lax.fori_loop(0, own_count, block_step, initial)  9.79 us
  transfers between devices with their start and end apart: 21, of which 10 were waited for; matrix products, arithmetic and copies ran while one was open for 4% of the time, Pallas kernels for 0%

profile of v1, /device:TPU:1, one launch (start us, length us, event | category | flops | bytes accessed | tf_op | source)
XLA Modules:
  0.0 352.2 jit_solution(17868107000511840932)
XLA Ops:
  2.8 2.1 collective-permute-start
  4.9 2.5 collective-permute-start.1
  11.4 3.3 collective-permute-start.7
  20.3 4.2 %collective-permute-start.9 = (bf16[4,512,128]{2,1,0:T(8,128)(2,1)S(1)}, bf16[4,512,128]{2,1,0:T(8,128)(2,1)S(1)}, u32[]{:S(2)}, u32[]{:S(2)}) collective-permute-start(bf16[4,512,128]{2,1,0:T(8,128)(2,1)S(1)} %get-tuple-element.152), channel_id=1, source_target_pairs={{0,16},{16,0},{1,17},{17,1},{2,18},{18,2},{3,19},{19,3},{4,20},{20... | collective-permute-start | bytes 1572872 | tf_op jit(solution)/shard_map/ppermute | solution.py:37
  26.0 2.6 collective-permute-start.4
  30.9 8.7 %collective-permute-done.3 = bf16[4,512,128]{2,1,0:T(8,128)(2,1)S(1)} collective-permute-done((bf16[4,512,128]{2,1,0:T(8,128)(2,1)S(1)}, bf16[4,512,128]{2,1,0:T(8,128)(2,1)S(1)}, u32[]{:S(2)}, u32[]{:S(2)}) %collective-permute-start.3) | collective-permute-done | bytes 524320 | tf_op jit(solution)/shard_map/ppermute | solution.py:37
  39.6 12.3 %collective-permute-done.4 = bf16[4,512,128]{2,1,0:T(8,128)(2,1)S(1)} collective-permute-done((bf16[4,512,128]{2,1,0:T(8,128)(2,1)S(1)}, bf16[4,512,128]{2,1,0:T(8,128)(2,1)S(1)}, u32[]{:S(2)}, u32[]{:S(2)}) %collective-permute-start.4) | collective-permute-done | bytes 524320 | tf_op jit(solution)/shard_map/ppermute | solution.py:37
  53.5 2.5 broadcast_in_dim.24
  57.7 25.7 %while.16 = (s32[]{:T(128)}, f32[64,128,128]{2,1,0:T(8,128)}, f32[32,128,128]{2,1,0:T(8,128)}, f32[128,64]{0,1:T(8,128)S(1)}, f32[]{:T(128)}, /*index=5*/s32[]{:...) while((s32[]{:T(128)}, f32[64,128,128]{2,1,0:T(8,128)}, ...), condition=%wide.region_7.8_spmd, body=%wide.region_0.7_spmd.sunk | while | flops 830464000 | bytes 24822980 | solution.py:111
  68.4 4.1 %fusion.78 = (f32[]{:T(128)}, bf16[64,128,128]{2,1,0:T(8,128)(2,1)S(1)}) fusion(f32[64,128,128]{2,1,0:T(8,128)S(1)} %get-tuple-element.264, f32[128,128]{1,0:T(8,128)S(1)} %log.10, f32[128,128]{1,0:T(8,128)S(1)} %get-tuple-element.265, f32[64]{0:T(128)S(1)} %get-tuple-element.325, bf16[8,64,128,128]{3,2,1,0:T(8,128)(2,1)} %get-tuple-element.319, ...), kind=kLoop, calls=%fused_computation.5.clone.1 | loop fusion | flops 9437183 | bytes 8585480 | tf_op jit(solution)/shard_map/while/body/reduce_sum | solution.py:21
  84.0 2.6 convert.20
  87.8 125.8 %collective-permute-start.10 = (bf16[4,512,128]{2,1,0:T(8,128)(2,1)}, bf16[4,512,128]{2,1,0:T(8,128)(2,1)}, u32[]{:S(2)}, u32[]{:S(2)}) collective-permute-start(bf16[4,512,128]{2,1,0:T(8,128)(2,1)} %bitcast.36), channel_id=1, source_target_pairs={{0,4},{4,8},{8,12},{12,0},{1,5},{5,9},{9,13},{13,1},{2,6},{6,10},{... | collective-permute-start | bytes 1572872 | tf_op jit(solution)/shard_map/ppermute | solution.py:37
  213.6 2.4 collective-permute-start.12
  216.7 2.3 slice.83
  221.7 3.9 %collective-permute-done.11 = bf16[4,512,128]{2,1,0:T(8,128)(2,1)} collective-permute-done((bf16[4,512,128]{2,1,0:T(8,128)(2,1)}, bf16[4,512,128]{2,1,0:T(8,128)(2,1)}, u32[]{:S(2)}, u32[]{:S(2)}) %collective-permute-start.11) | collective-permute-done | bytes 524320 | tf_op jit(solution)/shard_map/ppermute | solution.py:37
  226.2 1.9 fusion.55
  228.3 2.6 collective-permute-start.15
  232.9 62.6 %collective-permute-start.17 = (bf16[512,128]{1,0:T(8,128)(2,1)S(1)}, bf16[512,128]{1,0:T(8,128)(2,1)S(1)}, u32[]{:S(2)}, u32[]{:S(2)}) collective-permute-start(bf16[512,128]{1,0:T(8,128)(2,1)S(1)} %get-tuple-element.148), channel_id=1, source_target_pairs={{0,32},{32,64},{64,96},{96,0},{1,33},{33,65},{65,97},{97,1},{2,34}... | collective-permute-start | bytes 393224 | tf_op jit(solution)/shard_map/ppermute | solution.py:37
  295.6 2.5 collective-permute-start.19
  298.5 2.8 collective-permute-done.18
  306.1 22.5 %all_to_all.10 = f32[128,7,128]{2,1,0:T(8,128)S(1)} all-to-all(f32[128,7,128]{2,1,0:T(8,128)S(1)} %reshape.62), channel_id=1, replica_groups=mesh['z'=4,'core'=2,'y'=4,'x'=4] {'z','core','y','x'}, dimensions={0} | all-to-all | bytes 917504 | tf_op jit(solution)/shard_map/all_to_all | solution.py:138
  329.5 4.2 %all-to-all-start.1 = ((f32[128,7,128]{2,1,0:T(8,128)}), f32[128,7,128]{2,1,0:T(8,128)S(1)}, u32[]{:S(2)}, u32[]{:S(2)}) async-start(f32[128,7,128]{2,1,0:T(8,128)} %broadcast_in_dim.36), calls=%async_computation.1 | async-start | bytes 1048576 | tf_op jit(solution)/shard_map/all_to_all | solution.py:139
  335.3 2.3 fusion.22
  337.6 10.1 %all-to-all-done.1 = f32[128,7,128]{2,1,0:T(8,128)S(1)} async-done(((f32[128,7,128]{2,1,0:T(8,128)}), f32[128,7,128]{2,1,0:T(8,128)S(1)}, u32[]{:S(2)}, u32[]{:S(2)}) %all-to-all-start.1) | async-done | bytes 458784 | tf_op jit(solution)/shard_map/all_to_all | solution.py:139
  (99 shorter events, 47.6 us)
Async XLA Ops:
  2.8 21.7 %collective-permute-start = (bf16[512,128]{1,0:T(8,128)(2,1)S(1)}, bf16[512,128]{1,0:T(8,128)(2,1)S(1)}, u32[]{:S(2)}, u32[]{:S(2)}) collective-permute-start(bf16[512,128]{1,0:T(8,128)(2,1)S(1)} %convolution_convert_fusion.1), channel_id=1, source_target_pairs={{0,1},{1,2},{2,3},{3,0},{4,5},{5,6},{6,7},{7,4},{8,9},{9,10},{10,1... | collective-permute-start | bytes 393224 | tf_op jit(solution)/shard_map/ppermute | solution.py:37
  4.9 19.6 %collective-permute-start.1 = (bf16[512,128]{1,0:T(8,128)(2,1)S(1)}, bf16[512,128]{1,0:T(8,128)(2,1)S(1)}, u32[]{:S(2)}, u32[]{:S(2)}) collective-permute-start(bf16[512,128]{1,0:T(8,128)(2,1)S(1)} %convolution_convert_fusion.1), channel_id=1, source_target_pairs={{0,2},{1,3},{2,0},{3,1},{4,6},{5,7},{6,4},{7,5},{8,10},{9,11},{10,... | collective-permute-start | bytes 393224 | tf_op jit(solution)/shard_map/ppermute | solution.py:37
  7.4 17.2 %collective-permute-start.2 = (bf16[512,128]{1,0:T(8,128)(2,1)S(1)}, bf16[512,128]{1,0:T(8,128)(2,1)S(1)}, u32[]{:S(2)}, u32[]{:S(2)}) collective-permute-start(bf16[512,128]{1,0:T(8,128)(2,1)S(1)} %convolution_convert_fusion.1), channel_id=1, source_target_pairs={{0,3},{1,0},{2,1},{3,2},{4,7},{5,4},{6,5},{7,6},{8,11},{9,8},{10,9... | collective-permute-start | bytes 393224 | tf_op jit(solution)/shard_map/ppermute | solution.py:37
  9.7 6.2 %collective-permute-start.6 = (bf16[512,128]{1,0:T(8,128)(2,1)S(1)}, bf16[512,128]{1,0:T(8,128)(2,1)S(1)}, u32[]{:S(2)}, u32[]{:S(2)}) collective-permute-start(bf16[512,128]{1,0:T(8,128)(2,1)S(1)} %convolution_convert_fusion), channel_id=1, source_target_pairs={{0,32},{32,64},{64,96},{96,0},{1,33},{33,65},{65,97},{97,1},{2,34}... | collective-permute-start | bytes 393224 | tf_op jit(solution)/shard_map/ppermute | solution.py:37
  11.4 7.8 %collective-permute-start.7 = (bf16[512,128]{1,0:T(8,128)(2,1)S(1)}, bf16[512,128]{1,0:T(8,128)(2,1)S(1)}, u32[]{:S(2)}, u32[]{:S(2)}) collective-permute-start(bf16[512,128]{1,0:T(8,128)(2,1)S(1)} %convolution_convert_fusion), channel_id=1, source_target_pairs={{0,64},{32,96},{64,0},{96,32},{1,65},{33,97},{65,1},{97,33},{2,66}... | collective-permute-start | bytes 393224 | tf_op jit(solution)/shard_map/ppermute | solution.py:37
  15.9 4.3 %collective-permute-start.8 = (bf16[512,128]{1,0:T(8,128)(2,1)S(1)}, bf16[512,128]{1,0:T(8,128)(2,1)S(1)}, u32[]{:S(2)}, u32[]{:S(2)}) collective-permute-start(bf16[512,128]{1,0:T(8,128)(2,1)S(1)} %convolution_convert_fusion), channel_id=1, source_target_pairs={{0,96},{32,0},{64,32},{96,64},{1,97},{33,1},{65,33},{97,65},{2,98}... | collective-permute-start | bytes 393224 | tf_op jit(solution)/shard_map/ppermute | solution.py:37
  20.3 9.4 %collective-permute-start.9 = (bf16[4,512,128]{2,1,0:T(8,128)(2,1)S(1)}, bf16[4,512,128]{2,1,0:T(8,128)(2,1)S(1)}, u32[]{:S(2)}, u32[]{:S(2)}) collective-permute-start(bf16[4,512,128]{2,1,0:T(8,128)(2,1)S(1)} %get-tuple-element.152), channel_id=1, source_target_pairs={{0,16},{16,0},{1,17},{17,1},{2,18},{18,2},{3,19},{19,3},{4,20},{20... | collective-permute-start | bytes 1572872 | tf_op jit(solution)/shard_map/ppermute | solution.py:37
  24.6 14.9 %collective-permute-start.3 = (bf16[4,512,128]{2,1,0:T(8,128)(2,1)S(1)}, bf16[4,512,128]{2,1,0:T(8,128)(2,1)S(1)}, u32[]{:S(2)}, u32[]{:S(2)}) collective-permute-start(bf16[4,512,128]{2,1,0:T(8,128)(2,1)S(1)} %get-tuple-element.154), channel_id=1, source_target_pairs={{0,4},{4,8},{8,12},{12,0},{1,5},{5,9},{9,13},{13,1},{2,6},{6,10},{... | collective-permute-start | bytes 1572872 | tf_op jit(solution)/shard_map/ppermute | solution.py:37
  26.0 25.9 %collective-permute-start.4 = (bf16[4,512,128]{2,1,0:T(8,128)(2,1)S(1)}, bf16[4,512,128]{2,1,0:T(8,128)(2,1)S(1)}, u32[]{:S(2)}, u32[]{:S(2)}) collective-permute-start(bf16[4,512,128]{2,1,0:T(8,128)(2,1)S(1)} %get-tuple-element.154), channel_id=1, source_target_pairs={{0,8},{4,12},{8,0},{12,4},{1,9},{5,13},{9,1},{13,5},{2,10},{6,14},... | collective-permute-start | bytes 1572872 | tf_op jit(solution)/shard_map/ppermute | solution.py:37
  28.6 23.3 %collective-permute-start.5 = (bf16[4,512,128]{2,1,0:T(8,128)(2,1)S(1)}, bf16[4,512,128]{2,1,0:T(8,128)(2,1)S(1)}, u32[]{:S(2)}, u32[]{:S(2)}) collective-permute-start(bf16[4,512,128]{2,1,0:T(8,128)(2,1)S(1)} %get-tuple-element.154), channel_id=1, source_target_pairs={{0,12},{4,0},{8,4},{12,8},{1,13},{5,1},{9,5},{13,9},{2,14},{6,2},{... | collective-permute-start | bytes 1572872 | tf_op jit(solution)/shard_map/ppermute | solution.py:37
  86.6 132.4 %copy-start.1 = (f32[32,128,128]{2,1,0:T(8,128)S(1)}, f32[32,128,128]{2,1,0:T(8,128)}, u32[]{:S(2)}) copy-start(f32[32,128,128]{2,1,0:T(8,128)} %get-tuple-element.87) | copy-start | bytes 6291460
  87.8 133.9 %collective-permute-start.10 = (bf16[4,512,128]{2,1,0:T(8,128)(2,1)}, bf16[4,512,128]{2,1,0:T(8,128)(2,1)}, u32[]{:S(2)}, u32[]{:S(2)}) collective-permute-start(bf16[4,512,128]{2,1,0:T(8,128)(2,1)} %bitcast.36), channel_id=1, source_target_pairs={{0,4},{4,8},{8,12},{12,0},{1,5},{5,9},{9,13},{13,1},{2,6},{6,10},{... | collective-permute-start | bytes 1572872 | tf_op jit(solution)/shard_map/ppermute | solution.py:37
  213.6 12.1 %collective-permute-start.11 = (bf16[4,512,128]{2,1,0:T(8,128)(2,1)}, bf16[4,512,128]{2,1,0:T(8,128)(2,1)}, u32[]{:S(2)}, u32[]{:S(2)}) collective-permute-start(bf16[4,512,128]{2,1,0:T(8,128)(2,1)} %bitcast.37), channel_id=1, source_target_pairs={{0,8},{4,12},{8,0},{12,4},{1,9},{5,13},{9,1},{13,5},{2,10},{6,14},... | collective-permute-start | bytes 1572872 | tf_op jit(solution)/shard_map/ppermute | solution.py:37
  213.6 12.5 %collective-permute-start.12 = (bf16[4,512,128]{2,1,0:T(8,128)(2,1)}, bf16[4,512,128]{2,1,0:T(8,128)(2,1)}, u32[]{:S(2)}, u32[]{:S(2)}) collective-permute-start(bf16[4,512,128]{2,1,0:T(8,128)(2,1)} %bitcast.38), channel_id=1, source_target_pairs={{0,12},{4,0},{8,4},{12,8},{1,13},{5,1},{9,5},{13,9},{2,14},{6,2},{... | collective-permute-start | bytes 1572872 | tf_op jit(solution)/shard_map/ppermute | solution.py:37
  220.0 10.9 %collective-permute-start.16 = (bf16[4,512,128]{2,1,0:T(8,128)(2,1)}, bf16[4,512,128]{2,1,0:T(8,128)(2,1)S(1)}, u32[]{:S(2)}, u32[]{:S(2)}) collective-permute-start(bf16[4,512,128]{2,1,0:T(8,128)(2,1)} %bitcast.44), channel_id=1, source_target_pairs={{0,16},{16,0},{1,17},{17,1},{2,18},{18,2},{3,19},{19,3},{4,20},{20... | collective-permute-start | bytes 1572872 | tf_op jit(solution)/shard_map/ppermute | solution.py:37
  228.1 75.8 %copy-start.11 = (f32[128,64]{1,0:T(8,128)S(1)}, f32[128,64]{1,0:T(8,128)}, u32[]{:S(2)}) copy-start(f32[128,64]{1,0:T(8,128)} %copy.19) | copy-start | bytes 98308
  228.1 67.4 %collective-permute-start.13 = (bf16[512,128]{1,0:T(8,128)(2,1)S(1)}, bf16[512,128]{1,0:T(8,128)(2,1)S(1)}, u32[]{:S(2)}, u32[]{:S(2)}) collective-permute-start(bf16[512,128]{1,0:T(8,128)(2,1)S(1)} %get-tuple-element.145), channel_id=1, source_target_pairs={{0,1},{1,2},{2,3},{3,0},{4,5},{5,6},{6,7},{7,4},{8,9},{9,10},{10,1... | collective-permute-start | bytes 393224 | tf_op jit(solution)/shard_map/ppermute | solution.py:37
  228.2 69.8 %collective-permute-start.14 = (bf16[512,128]{1,0:T(8,128)(2,1)S(1)}, bf16[512,128]{1,0:T(8,128)(2,1)S(1)}, u32[]{:S(2)}, u32[]{:S(2)}) collective-permute-start(bf16[512,128]{1,0:T(8,128)(2,1)S(1)} %get-tuple-element.147), channel_id=1, source_target_pairs={{0,2},{1,3},{2,0},{3,1},{4,6},{5,7},{6,4},{7,5},{8,10},{9,11},{10,... | collective-permute-start | bytes 393224 | tf_op jit(solution)/shard_map/ppermute | solution.py:37
  228.3 69.7 %collective-permute-start.15 = (bf16[512,128]{1,0:T(8,128)(2,1)S(1)}, bf16[512,128]{1,0:T(8,128)(2,1)S(1)}, u32[]{:S(2)}, u32[]{:S(2)}) collective-permute-start(bf16[512,128]{1,0:T(8,128)(2,1)S(1)} %get-tuple-element.146), channel_id=1, source_target_pairs={{0,3},{1,0},{2,1},{3,2},{4,7},{5,4},{6,5},{7,6},{8,11},{9,8},{10,9... | collective-permute-start | bytes 393224 | tf_op jit(solution)/shard_map/ppermute | solution.py:37
  232.9 65.6 %collective-permute-start.17 = (bf16[512,128]{1,0:T(8,128)(2,1)S(1)}, bf16[512,128]{1,0:T(8,128)(2,1)S(1)}, u32[]{:S(2)}, u32[]{:S(2)}) collective-permute-start(bf16[512,128]{1,0:T(8,128)(2,1)S(1)} %get-tuple-element.148), channel_id=1, source_target_pairs={{0,32},{32,64},{64,96},{96,0},{1,33},{33,65},{65,97},{97,1},{2,34}... | collective-permute-start | bytes 393224 | tf_op jit(solution)/shard_map/ppermute | solution.py:37
  295.6 5.8 %collective-permute-start.18 = (bf16[512,128]{1,0:T(8,128)(2,1)S(1)}, bf16[512,128]{1,0:T(8,128)(2,1)S(1)}, u32[]{:S(2)}, u32[]{:S(2)}) collective-permute-start(bf16[512,128]{1,0:T(8,128)(2,1)S(1)} %get-tuple-element.150), channel_id=1, source_target_pairs={{0,64},{32,96},{64,0},{96,32},{1,65},{33,97},{65,1},{97,33},{2,66}... | collective-permute-start | bytes 393224 | tf_op jit(solution)/shard_map/ppermute | solution.py:37
  295.6 8.2 %copy-start.7 = (bf16[512,128]{1,0:T(8,128)(2,1)}, bf16[512,128]{1,0:T(8,128)(2,1)S(1)}, u32[]{:S(2)}) copy-start(bf16[512,128]{1,0:T(8,128)(2,1)S(1)} %collective-permute-done.13) | copy-start | bytes 393220
  295.6 7.7 %collective-permute-start.19 = (bf16[512,128]{1,0:T(8,128)(2,1)S(1)}, bf16[512,128]{1,0:T(8,128)(2,1)S(1)}, u32[]{:S(2)}, u32[]{:S(2)}) collective-permute-start(bf16[512,128]{1,0:T(8,128)(2,1)S(1)} %get-tuple-element.149), channel_id=1, source_target_pairs={{0,96},{32,0},{64,32},{96,64},{1,97},{33,1},{65,33},{97,65},{2,98}... | collective-permute-start | bytes 393224 | tf_op jit(solution)/shard_map/ppermute | solution.py:37
  329.5 18.2 %all-to-all-start.1 = ((f32[128,7,128]{2,1,0:T(8,128)}), f32[128,7,128]{2,1,0:T(8,128)S(1)}, u32[]{:S(2)}, u32[]{:S(2)}) async-start(f32[128,7,128]{2,1,0:T(8,128)} %broadcast_in_dim.36), calls=%async_computation.1 | async-start | bytes 1048576 | tf_op jit(solution)/shard_map/all_to_all | solution.py:139
  (10 other events, 30.6 us)

commit v2 on v1

v2 whole, which is shorter than its diff:
```python
import jax
import jax.numpy as jnp
from jax import lax
from jax.experimental import pallas as pl
from jax.experimental.pallas import tpu as pltpu
from jax.sharding import Mesh
from jax.sharding import PartitionSpec as P

GROUP = 8


def blocks_kernel(
    place, count, bias, w_rows, w_wide, w_cols, left_bank, right_bank, teacher,
    row0, row1, row2, row3, col0, col1, bin_out, cross_out,
    left_tiles, right_tiles, target, logit, left_turn, right_turn, left_sum, right_sum,
    left_grads, right_grads, tile_sem, target_sem,
):
    rows_out = (row0, row1, row2, row3)
    cols_out = (col0, col1)
    slots, bins, tile, width = teacher.shape
    live = count[0]

    def target_copy(slot):
        return pltpu.make_async_copy(
            teacher.at[slot], target.at[lax.rem(slot, 2)], target_sem.at[lax.rem(slot, 2)]
        )

    def left_copy(slot):
        return pltpu.make_async_copy(
            left_bank.at[place[slot, 0]], left_tiles.at[slot], tile_sem.at[slot, 0]
        )

    def right_copy(slot):
        return pltpu.make_async_copy(
            right_bank.at[place[slot, 1]], right_tiles.at[slot], tile_sem.at[slot, 1]
        )

    for slot in range(slots):

        @pl.when(slot < live)
        def _():
            left_copy(slot).start()
            right_copy(slot).start()

    target_copy(0).start()
    for out in rows_out + cols_out:
        out[...] = jnp.zeros(out.shape, out.dtype)
    bin_out[...] = jnp.zeros(bin_out.shape, jnp.float32)
    cross_out[...] = jnp.zeros(cross_out.shape, jnp.float32)
    left_grads[...] = jnp.zeros(left_grads.shape, jnp.float32)
    right_grads[...] = jnp.zeros(right_grads.shape, jnp.float32)

    def block(slot, _):
        buf = lax.rem(slot, 2)

        @pl.when(slot + 1 < live)
        def _():
            target_copy(slot + 1).start()

        left_copy(slot).wait()
        right_copy(slot).wait()
        left = left_tiles[slot]
        right = right_tiles[slot]
        left_turn[...] = left.T
        right_turn[...] = right.T
        left_sum[...] = jnp.zeros(left_sum.shape, jnp.float32)
        right_sum[...] = jnp.zeros(right_sum.shape, jnp.float32)

        def scores(g, highest):
            left = left_tiles[slot].reshape(tile // 16, 16, width)
            for j in range(GROUP):
                k = g * GROUP + j
                scaled = (left * w_rows[k][None]).reshape(tile, width)
                value = jnp.dot(scaled, right_turn[...], preferred_element_type=jnp.float32)
                value = value + bias[k]
                logit[k] = value
                highest = jnp.maximum(highest, value)
            return highest

        highest = lax.fori_loop(
            0, bins // GROUP, scores, jnp.full((tile, tile), -jnp.inf, jnp.float32)
        )
        target_copy(slot).wait()

        STEP = 32
        ratios = []
        for p in range(0, tile, STEP):
            rows = pl.ds(p, STEP)
            top = highest[p : p + STEP]

            def soft(g, carried):
                total, mass, cross = carried
                for j in range(GROUP):
                    k = g * GROUP + j
                    value = logit[k, rows, :] - top
                    power = jnp.exp(value)
                    goal = target[buf, k, rows, :].astype(jnp.float32)
                    total = total + power
                    mass = mass + goal
                    cross = cross + goal * value
                    logit[k, rows, :] = power
                return total, mass, cross

            zero = jnp.zeros((STEP, tile), jnp.float32)
            total, mass, cross = lax.fori_loop(0, bins // GROUP, soft, (zero, zero, zero))
            cross = mass * jnp.log(total) - cross
            cross_out[...] += cross.reshape(STEP // 8, 8, tile).sum(0)
            ratios.append(mass / total)
        ratio = jnp.concatenate(ratios, 0)

        def grads(g, _):
            left_wide = left_tiles[slot].astype(jnp.float32)
            pieces, scales = [], []
            left_part = jnp.zeros((tile, width), jnp.float32)
            for j in range(GROUP):
                k = g * GROUP + j
                grad = logit[k] * ratio - target[buf, k].astype(jnp.float32)
                grad = grad.astype(jnp.bfloat16)
                mixed = jnp.dot(grad, right_tiles[slot], preferred_element_type=jnp.float32)
                left_part = left_part + (
                    mixed.reshape(tile // 8, 8, width) * w_wide[k][None]
                ).reshape(tile, width)
                bin_out[k] += (mixed * left_wide).reshape(tile // 8, 8, width).sum(0)
                pieces.append(grad)
                scales.append(left_turn[...] * w_cols[k])
            left_sum[...] += left_part
            right_sum[...] += jnp.dot(
                jnp.concatenate(scales, 1),
                jnp.concatenate(pieces, 0),
                preferred_element_type=jnp.float32,
            )
            return 0

        lax.fori_loop(0, bins // GROUP, grads, 0)
        left_grads[slot] = left_sum[...]
        right_grads[slot] = right_sum[...].T
        return 0

    lax.fori_loop(0, live, block, 0)

    def put(outs, spot, value):
        size = outs[0].shape[0]
        for n, out in enumerate(outs):

            @pl.when(spot // size == n)
            def _():
                out[lax.rem(spot, size)] = value.astype(jnp.bfloat16)

    for slot in range(0, slots, 2):
        for grads_ref, outs, field in ((left_grads, rows_out, 2), (right_grads, cols_out, 3)):
            first, second = place[slot, field], place[slot + 1, field]
            same = (slot + 1 < live) & (first == second)
            one, two = grads_ref[slot], grads_ref[slot + 1]

            @pl.when(slot < live)
            def _():
                put(outs, first, one + jnp.where(same, two, 0.0))

            @pl.when((slot + 1 < live) & (first != second))
            def _():
                put(outs, second, two)


def run_blocks(place, count, bin_weight, bin_bias, left_bank, right_bank, teacher):
    slots, bins, tile, _ = teacher.shape
    width = bin_weight.shape[0]
    turned = bin_weight.T
    w_rows = jnp.broadcast_to(turned[:, None, :], (bins, 16, width))
    w_wide = jnp.broadcast_to(turned[:, None, :].astype(jnp.float32), (bins, 8, width))
    w_cols = jnp.broadcast_to(turned[:, :, None], (bins, width, tile))
    smem = pl.BlockSpec(memory_space=pltpu.SMEM)
    vmem = pl.BlockSpec(memory_space=pltpu.VMEM)
    hbm = pl.BlockSpec(memory_space=pl.ANY)
    f32, bf16 = jnp.float32, jnp.bfloat16
    piece = jax.ShapeDtypeStruct((16, tile, width), bf16)
    return pl.pallas_call(
        blocks_kernel,
        out_shape=[piece] * 6
        + [
            jax.ShapeDtypeStruct((bins, 8, width), f32),
            jax.ShapeDtypeStruct((8, tile), f32),
        ],
        in_specs=[smem, smem, smem, vmem, vmem, vmem, hbm, hbm, hbm],
        out_specs=[vmem] * 8,
        scratch_shapes=[
            pltpu.VMEM((slots, tile, width), bf16),
            pltpu.VMEM((slots, tile, width), bf16),
            pltpu.VMEM((2, bins, tile, tile), bf16),
            pltpu.VMEM((bins, tile, tile), f32),
            pltpu.VMEM((width, tile), bf16),
            pltpu.VMEM((width, tile), bf16),
            pltpu.VMEM((tile, width), f32),
            pltpu.VMEM((width, tile), f32),
            pltpu.VMEM((slots, tile, width), f32),
            pltpu.VMEM((slots, tile, width), f32),
            pltpu.SemaphoreType.DMA((slots, 2)),
            pltpu.SemaphoreType.DMA((2,)),
        ],
        compiler_params=pltpu.CompilerParams(vmem_limit_bytes=48 * 1024 * 1024),
        cost_estimate=pl.CostEstimate(
            flops=6 * 8 * 64 * 128**3, bytes_accessed=20 * 2**20, transcendentals=8 * 2**20
        ),
    )(place, count, bin_bias, w_rows, w_wide, w_cols, left_bank, right_bank, teacher)


AXES = ("z", "core", "y", "x")


def shift(value, axis, step):
    size = lax.axis_size(axis)
    return lax.ppermute(value, axis, [(i, (i + step) % size) for i in range(size)])


def spread(value, axis):
    return jnp.stack([value] + [shift(value, axis, s) for s in range(1, lax.axis_size(axis))])


def collect(parts, axis):
    total = parts[0].astype(jnp.float32)
    for s in range(1, lax.axis_size(axis)):
        total = total + shift(parts[s].astype(jnp.bfloat16), axis, s).astype(jnp.float32)
    return total


def per_device(
    single, left_weight, right_weight, bin_weight, bin_bias, block_tiles, block_count, teacher
):
    tile = teacher.shape[-1]
    bins = bin_weight.shape[1]
    devices = lax.axis_size(AXES)
    tiles_dev = single.shape[0] // tile
    own_tiles = block_tiles[0]
    own_count = block_count[0]
    own_targets = teacher[0]
    left_wide = left_weight.astype(jnp.float32)
    right_wide = right_weight.astype(jnp.float32)
    left_local = jnp.dot(single, left_weight, preferred_element_type=jnp.float32).astype(
        jnp.bfloat16
    )
    right_local = jnp.dot(single, right_weight, preferred_element_type=jnp.float32).astype(
        jnp.bfloat16
    )
    width = left_local.shape[1]
    z, core, y, x = (lax.axis_index(a) for a in AXES)
    row_home = own_tiles[:, 0] // tiles_dev
    col_home = own_tiles[:, 1] // tiles_dev
    row_inner = own_tiles[:, 0] % tiles_dev
    col_inner = own_tiles[:, 1] % tiles_dev
    far_y = (row_home // 4 % 4 - y) % 4
    far_x = (row_home % 4 - x) % 4
    far_z = (col_home // 32 - z) % 4
    far_core = (col_home // 16 % 2 - core) % 2
    row_from = (((-far_y) % 4) * 4 + (-far_x) % 4) * tiles_dev + row_inner
    row_to = (far_y * 4 + far_x) * tiles_dev + row_inner
    col_from = (far_core * 4 + (-far_z) % 4) * tiles_dev + col_inner
    col_to = (far_core * 4 + far_z) * tiles_dev + col_inner
    row_bank = spread(spread(left_local, "x"), "y").reshape(-1, tile, width)
    col_bank = spread(spread(right_local, "z"), "core").reshape(-1, tile, width)
    place = jnp.stack([row_from, col_from, row_to, col_to], axis=1)
    row0, row1, row2, row3, col0, col1, bins_part, cross_part = run_blocks(
        place, block_count, bin_weight, bin_bias, row_bank, col_bank, own_targets
    )
    rows_dev = single.shape[0]
    left_near = collect((row0, row1, row2, row3), "y").reshape(4, rows_dev, width)
    right_near = collect((col0, col1), "core").reshape(4, rows_dev, width)
    left_rows_grad = collect(left_near, "x")
    right_rows_grad = collect(right_near, "z")
    grad_single = (
        jnp.dot(left_rows_grad, left_wide.T, precision=lax.Precision.HIGHEST)
        + jnp.dot(right_rows_grad, right_wide.T, precision=lax.Precision.HIGHEST)
    ).astype(jnp.bfloat16)
    single_wide = single.astype(jnp.float32)
    part_left = jnp.dot(single_wide.T, left_rows_grad, precision=lax.Precision.HIGHEST)
    part_right = jnp.dot(single_wide.T, right_rows_grad, precision=lax.Precision.HIGHEST)
    depth = part_left.shape[0]
    rows_sum = 2 * depth + bins
    chunk = -(-(rows_sum + 1) // devices)
    scalars = jnp.stack([jnp.sum(cross_part), own_count.astype(jnp.float32)])
    packed = jnp.concatenate(
        [
            part_left,
            part_right,
            jnp.sum(bins_part, axis=1),
            jnp.pad(scalars[None], ((0, chunk * devices - rows_sum - 1), (0, width - 2))),
        ]
    ).reshape(devices, chunk, width)
    mine = jnp.sum(lax.all_to_all(packed, AXES, 0, 0), axis=0)
    totals = lax.all_to_all(
        jnp.broadcast_to(mine[None], (devices, chunk, width)), AXES, 0, 0
    ).reshape(-1, width)
    grad_left = totals[:depth] / devices
    grad_right = totals[depth : 2 * depth] / devices
    grad_bin = totals[2 * depth : rows_sum].T / devices
    loss_value = totals[rows_sum, 0] / (totals[rows_sum, 1] * (tile * tile))
    return (grad_single, grad_left, grad_right, grad_bin, loss_value)


def solution(mesh):
    torus = Mesh(mesh.devices.reshape(4, 2, 4, 4), AXES)
    return jax.shard_map(
        per_device,
        mesh=torus,
        in_specs=(
            P(AXES, None),
            P(),
            P(),
            P(),
            P(),
            P(AXES, None, None),
            P(AXES),
            P(AXES, None, None, None, None),
        ),
        out_specs=(P(AXES, None), P(), P(), P(), P()),
        check_vma=False,
    )
```

time: 351 us -> 175 us (0.50)
  starting transfers between devices: 222 us -> 61.1 us
  Pallas kernels: 0 us -> 26.8 us
  local copies, waits for them, and re-layouts: 18.9 us -> 6.17 us
  other arithmetic: 20.2 us -> 7.97 us
  loops' own time: 9.79 us -> 0 us
  matrix products: 11.6 us -> 4.91 us
    ppermute x20, starting transfers between devices: 218 us -> 56.9 us  [shift(): lax.ppermute(value, axis, [(i, (i + step) % size) for i in range(size)])]
    pallas_call x0 -> x1, Pallas kernels: none -> 26.8 us  [run_blocks(): pl.pallas_call(blocks_kernel, out_shape=[piece] * 6 + [jax.ShapeDtypeStru...]
    another operation x1 -> x0, loops' own time: 9.79 us -> none  [per_device(): lax.fori_loop(0, own_count, block_step, initial)]
    reduce_sum x3 -> x2, other arithmetic: 6.79 us -> 0.67 us  [the longest x1 0.6 us: per_device(): scalars = jnp.stack([jnp.sum(cross_part), own_count.astype(jnp.float32)])]
    dot_general x3 -> x0, matrix products: 4.47 us -> none  [the longest x1 1.58 us: block_terms(): jnp.einsum('kpq,qc->kpc', grad_logits, right_tile, preferred_element_type...]
  transfers between devices with their start and end apart: 21 -> 21, of which waited for: 10 -> 10; matrix products, arithmetic and copies ran while one was open for 4% -> 5% of each run, Pallas kernels for 0% -> 0%
where the time goes in v2:
time: 175 us
  starting transfers between devices  61.1 us (35%)
  waiting for transfers between devices  42.4 us (24%)
  Pallas kernels  26.8 us (15%)
  blocking collectives  21.6 us (12%)
  other arithmetic  7.97 us (5%)
  local copies, waits for them, and re-layouts  6.17 us (4%)
  matrix products  4.91 us (3%)
  between operations  3.95 us (2%)
    ppermute x20, starting transfers between devices, shift(): lax.ppermute(value, axis, [(i, (i + step) % size) for i in range(size)])  56.9 us
    ppermute x20, waiting for transfers between devices, shift(): lax.ppermute(value, axis, [(i, (i + step) % size) for i in range(size)])  30.1 us
    pallas_call x1, Pallas kernels, run_blocks(): pl.pallas_call(blocks_kernel, out_shape=[piece] * 6 + [jax.ShapeDtypeStru...  26.8 us
    all_to_all x1, blocking collectives, per_device(): mine = jnp.sum(lax.all_to_all(packed, AXES, 0, 0), axis=0)  21.6 us
    all_to_all x1, waiting for transfers between devices, per_device(): lax.all_to_all(jnp.broadcast_to(mine[None], (devices, chunk, width)), AXE...  12.3 us
    all_to_all x1, starting transfers between devices, per_device(): lax.all_to_all(jnp.broadcast_to(mine[None], (devices, chunk, width)), AXE...  4.17 us
  transfers between devices with their start and end apart: 21, of which 10 were waited for; matrix products, arithmetic and copies ran while one was open for 5% of the time, Pallas kernels for 0%

profile of v2, /device:TPU:1, one launch (start us, length us, event | category | flops | bytes accessed | tf_op | source)
XLA Modules:
  0.0 175.0 jit_solution(12250646307437611836)
XLA Ops:
  2.8 2.1 %collective-permute-start = (bf16[512,128]{1,0:T(8,128)(2,1)S(1)}, bf16[512,128]{1,0:T(8,128)(2,1)S(1)}, u32[]{:S(2)}, u32[]{:S(2)}) collective-permute-start(bf16[512,128]{1,0:T(8,128)(2,1)S(1)} %convolution_convert_fusion.1), channel_id=1, source_target_pairs={{0,1},{1,2},{2,3},{3,0},{4,5},{5,6},{6,7},{7,4},{8,9},{9,10},{10,1... | collective-permute-start | bytes 393224 | tf_op jit(solution)/shard_map/ppermute | solution.py:211
  4.9 2.5 %collective-permute-start.1 = (bf16[512,128]{1,0:T(8,128)(2,1)S(1)}, bf16[512,128]{1,0:T(8,128)(2,1)S(1)}, u32[]{:S(2)}, u32[]{:S(2)}) collective-permute-start(bf16[512,128]{1,0:T(8,128)(2,1)S(1)} %convolution_convert_fusion.1), channel_id=1, source_target_pairs={{0,2},{1,3},{2,0},{3,1},{4,6},{5,7},{6,4},{7,5},{8,10},{9,11},{10,... | collective-permute-start | bytes 393224 | tf_op jit(solution)/shard_map/ppermute | solution.py:211
  9.7 1.7 collective-permute-start.6
  11.4 3.3 %collective-permute-start.7 = (bf16[512,128]{1,0:T(8,128)(2,1)S(1)}, bf16[512,128]{1,0:T(8,128)(2,1)S(1)}, u32[]{:S(2)}, u32[]{:S(2)}) collective-permute-start(bf16[512,128]{1,0:T(8,128)(2,1)S(1)} %convolution_convert_fusion), channel_id=1, source_target_pairs={{0,64},{32,96},{64,0},{96,32},{1,65},{33,97},{65,1},{97,33},{2,66}... | collective-permute-start | bytes 393224 | tf_op jit(solution)/shard_map/ppermute | solution.py:211
  17.8 2.6 %collective-permute-start.4 = (bf16[4,512,128]{2,1,0:T(8,128)(2,1)S(1)}, bf16[4,512,128]{2,1,0:T(8,128)(2,1)S(1)}, u32[]{:S(2)}, u32[]{:S(2)}) collective-permute-start(bf16[4,512,128]{2,1,0:T(8,128)(2,1)S(1)} %get-tuple-element.34), channel_id=1, source_target_pairs={{0,8},{4,12},{8,0},{12,4},{1,9},{5,13},{9,1},{13,5},{2,10},{6,14},... | collective-permute-start | bytes 1572872 | tf_op jit(solution)/shard_map/ppermute | solution.py:211
  21.6 3.3 %collective-permute-start.9 = (bf16[4,512,128]{2,1,0:T(8,128)(2,1)S(1)}, bf16[4,512,128]{2,1,0:T(8,128)(2,1)S(1)}, u32[]{:S(2)}, u32[]{:S(2)}) collective-permute-start(bf16[4,512,128]{2,1,0:T(8,128)(2,1)S(1)} %get-tuple-element.32), channel_id=1, source_target_pairs={{0,16},{16,0},{1,17},{17,1},{2,18},{18,2},{3,19},{19,3},{4,20},{20... | collective-permute-start | bytes 1572872 | tf_op jit(solution)/shard_map/ppermute | solution.py:211
  26.5 2.4 %collective-permute-done.3 = bf16[4,512,128]{2,1,0:T(8,128)(2,1)S(1)} collective-permute-done((bf16[4,512,128]{2,1,0:T(8,128)(2,1)S(1)}, bf16[4,512,128]{2,1,0:T(8,128)(2,1)S(1)}, u32[]{:S(2)}, u32[]{:S(2)}) %collective-permute-start.3) | collective-permute-done | bytes 524320 | tf_op jit(solution)/shard_map/ppermute | solution.py:211
  28.9 12.4 %collective-permute-done.4 = bf16[4,512,128]{2,1,0:T(8,128)(2,1)S(1)} collective-permute-done((bf16[4,512,128]{2,1,0:T(8,128)(2,1)S(1)}, bf16[4,512,128]{2,1,0:T(8,128)(2,1)S(1)}, u32[]{:S(2)}, u32[]{:S(2)}) %collective-permute-start.4) | collective-permute-done | bytes 524320 | tf_op jit(solution)/shard_map/ppermute | solution.py:211
  44.1 2.2 %broadcast_in_dim.12.w_cols = bf16[64,128,128]{2,1,0:T(8,128)(2,1)} broadcast(bf16[64,128]{1,0:T(8,128)(2,1)S(1)} %bitcast.70), dimensions={0,1} | broadcast | bytes 2113536 | tf_op jit(solution)/shard_map/broadcast_in_dim | solution.py:170
  46.3 26.8 %shard_map.119 = (bf16[16,128,128]{2,1,0:T(8,128)(2,1)S(1)}, bf16[16,128,128]{2,1,0:T(8,128)(2,1)}, bf16[16,128,128]{2,1,0:T(8,128)(2,1)S(1)}, bf16[16,128,128]{...) custom-call(s32[8,4]{1,0:T(8,128)S(1)} %pad_add_fusion.place, ...), custom_call_target="tpu_custom_call" | custom-call | flops 6442450944 | bytes 20971520 | tf_op jit(solution)/shard_map/pallas_call | solution.py:176
  73.1 13.5 %collective-permute-start.10 = (bf16[16,128,128]{2,1,0:T(8,128)(2,1)}, bf16[16,128,128]{2,1,0:T(8,128)(2,1)}, u32[]{:S(2)}, u32[]{:S(2)}) collective-permute-start(bf16[16,128,128]{2,1,0:T(8,128)(2,1)} %get-tuple-element.14), channel_id=1, source_target_pairs={{0,4},{4,8},{8,12},{12,0},{1,5},{5,9},{9,13},{13,1},{2,6},{6,10},{... | collective-permute-start | bytes 1572872 | tf_op jit(solution)/shard_map/ppermute | solution.py:211
  86.7 2.5 %collective-permute-start.12 = (bf16[16,128,128]{2,1,0:T(8,128)(2,1)S(1)}, bf16[16,128,128]{2,1,0:T(8,128)(2,1)}, u32[]{:S(2)}, u32[]{:S(2)}) collective-permute-start(bf16[16,128,128]{2,1,0:T(8,128)(2,1)S(1)} %get-tuple-element.16), channel_id=1, source_target_pairs={{0,12},{4,0},{8,4},{12,8},{1,13},{5,1},{9,5},{13,9},{2,14},{6,2},{... | collective-permute-start | bytes 1572872 | tf_op jit(solution)/shard_map/ppermute | solution.py:211
  90.7 2.4 %collective-permute-done.10 = bf16[16,128,128]{2,1,0:T(8,128)(2,1)} collective-permute-done((bf16[16,128,128]{2,1,0:T(8,128)(2,1)}, bf16[16,128,128]{2,1,0:T(8,128)(2,1)}, u32[]{:S(2)}, u32[]{:S(2)}) %collective-permute-start.10) | collective-permute-done | bytes 524320 | tf_op jit(solution)/shard_map/ppermute | solution.py:211
  93.1 5.5 %collective-permute-done.11 = bf16[16,128,128]{2,1,0:T(8,128)(2,1)} collective-permute-done((bf16[16,128,128]{2,1,0:T(8,128)(2,1)S(1)}, bf16[16,128,128]{2,1,0:T(8,128)(2,1)}, u32[]{:S(2)}, u32[]{:S(2)}) %collective-permute-start.11) | collective-permute-done | bytes 524320 | tf_op jit(solution)/shard_map/ppermute | solution.py:211
  99.1 1.7 fusion.40
  100.8 4.1 %collective-permute-start.13 = (bf16[512,128]{1,0:T(8,128)(2,1)S(1)}, bf16[512,128]{1,0:T(8,128)(2,1)S(1)}, u32[]{:S(2)}, u32[]{:S(2)}) collective-permute-start(bf16[512,128]{1,0:T(8,128)(2,1)S(1)} %bitcast.80), channel_id=1, source_target_pairs={{0,1},{1,2},{2,3},{3,0},{4,5},{5,6},{6,7},{7,4},{8,9},{9,10},{10,1... | collective-permute-start | bytes 393224 | tf_op jit(solution)/shard_map/ppermute | solution.py:211
  104.9 2.5 %collective-permute-start.15 = (bf16[512,128]{1,0:T(8,128)(2,1)S(1)}, bf16[512,128]{1,0:T(8,128)(2,1)S(1)}, u32[]{:S(2)}, u32[]{:S(2)}) collective-permute-start(bf16[512,128]{1,0:T(8,128)(2,1)S(1)} %bitcast.78), channel_id=1, source_target_pairs={{0,3},{1,0},{2,1},{3,2},{4,7},{5,4},{6,5},{7,6},{8,11},{9,8},{10,9... | collective-permute-start | bytes 393224 | tf_op jit(solution)/shard_map/ppermute | solution.py:211
  108.7 11.8 %collective-permute-start.17 = (bf16[512,128]{1,0:T(8,128)(2,1)S(1)}, bf16[512,128]{1,0:T(8,128)(2,1)S(1)}, u32[]{:S(2)}, u32[]{:S(2)}) collective-permute-start(bf16[512,128]{1,0:T(8,128)(2,1)S(1)} %bitcast.83), channel_id=1, source_target_pairs={{0,32},{32,64},{64,96},{96,0},{1,33},{33,65},{65,97},{97,1},{2,34}... | collective-permute-start | bytes 393224 | tf_op jit(solution)/shard_map/ppermute | solution.py:211
  120.5 2.2 %collective-permute-start.18 = (bf16[512,128]{1,0:T(8,128)(2,1)S(1)}, bf16[512,128]{1,0:T(8,128)(2,1)S(1)}, u32[]{:S(2)}, u32[]{:S(2)}) collective-permute-start(bf16[512,128]{1,0:T(8,128)(2,1)S(1)} %bitcast.82), channel_id=1, source_target_pairs={{0,64},{32,96},{64,0},{96,32},{1,65},{33,97},{65,1},{97,33},{2,66}... | collective-permute-start | bytes 393224 | tf_op jit(solution)/shard_map/ppermute | solution.py:211
  123.8 1.6 collective-permute-done.17
  125.4 3.4 %collective-permute-done.18 = bf16[512,128]{1,0:T(8,128)(2,1)S(1)} collective-permute-done((bf16[512,128]{1,0:T(8,128)(2,1)S(1)}, bf16[512,128]{1,0:T(8,128)(2,1)S(1)}, u32[]{:S(2)}, u32[]{:S(2)}) %collective-permute-start.18) | collective-permute-done | bytes 131104 | tf_op jit(solution)/shard_map/ppermute | solution.py:211
  129.7 21.6 %all_to_all.10 = f32[128,7,128]{2,1,0:T(8,128)S(1)} all-to-all(f32[128,7,128]{2,1,0:T(8,128)S(1)} %reshape.58), channel_id=1, replica_groups=mesh['z'=4,'core'=2,'y'=4,'x'=4] {'z','core','y','x'}, dimensions={0} | all-to-all | bytes 917504 | tf_op jit(solution)/shard_map/all_to_all | solution.py:287
  152.3 4.2 %all-to-all-start.1 = ((f32[128,7,128]{2,1,0:T(8,128)}), f32[128,7,128]{2,1,0:T(8,128)S(1)}, u32[]{:S(2)}, u32[]{:S(2)}) async-start(f32[128,7,128]{2,1,0:T(8,128)} %broadcast_in_dim.14), calls=%async_computation.1 | async-start | bytes 1048576 | tf_op jit(solution)/shard_map/all_to_all | solution.py:288
  158.3 12.3 %all-to-all-done.1 = f32[128,7,128]{2,1,0:T(8,128)S(1)} async-done(((f32[128,7,128]{2,1,0:T(8,128)}), f32[128,7,128]{2,1,0:T(8,128)S(1)}, u32[]{:S(2)}, u32[]{:S(2)}) %all-to-all-start.1) | async-done | bytes 458784 | tf_op jit(solution)/shard_map/all_to_all | solution.py:288
  (71 shorter events, 22.5 us)
Async XLA Ops:
  2.8 22.9 %copy-start.4 = (bf16[128,64]{0,1:T(8,128)(2,1)S(1)}, bf16[128,64]{0,1:T(8,128)(2,1)}, u32[]{:S(2)}) copy-start(bf16[128,64]{0,1:T(8,128)(2,1)} %param.11) | copy-start | bytes 49156
  2.8 11.9 %collective-permute-start = (bf16[512,128]{1,0:T(8,128)(2,1)S(1)}, bf16[512,128]{1,0:T(8,128)(2,1)S(1)}, u32[]{:S(2)}, u32[]{:S(2)}) collective-permute-start(bf16[512,128]{1,0:T(8,128)(2,1)S(1)} %convolution_convert_fusion.1), channel_id=1, source_target_pairs={{0,1},{1,2},{2,3},{3,0},{4,5},{5,6},{6,7},{7,4},{8,9},{9,10},{10,1... | collective-permute-start | bytes 393224 | tf_op jit(solution)/shard_map/ppermute | solution.py:211
  4.9 11.4 %collective-permute-start.1 = (bf16[512,128]{1,0:T(8,128)(2,1)S(1)}, bf16[512,128]{1,0:T(8,128)(2,1)S(1)}, u32[]{:S(2)}, u32[]{:S(2)}) collective-permute-start(bf16[512,128]{1,0:T(8,128)(2,1)S(1)} %convolution_convert_fusion.1), channel_id=1, source_target_pairs={{0,2},{1,3},{2,0},{3,1},{4,6},{5,7},{6,4},{7,5},{8,10},{9,11},{10,... | collective-permute-start | bytes 393224 | tf_op jit(solution)/shard_map/ppermute | solution.py:211
  7.4 9.0 %collective-permute-start.2 = (bf16[512,128]{1,0:T(8,128)(2,1)S(1)}, bf16[512,128]{1,0:T(8,128)(2,1)S(1)}, u32[]{:S(2)}, u32[]{:S(2)}) collective-permute-start(bf16[512,128]{1,0:T(8,128)(2,1)S(1)} %convolution_convert_fusion.1), channel_id=1, source_target_pairs={{0,3},{1,0},{2,1},{3,2},{4,7},{5,4},{6,5},{7,6},{8,11},{9,8},{10,9... | collective-permute-start | bytes 393224 | tf_op jit(solution)/shard_map/ppermute | solution.py:211
  9.7 10.7 %collective-permute-start.6 = (bf16[512,128]{1,0:T(8,128)(2,1)S(1)}, bf16[512,128]{1,0:T(8,128)(2,1)S(1)}, u32[]{:S(2)}, u32[]{:S(2)}) collective-permute-start(bf16[512,128]{1,0:T(8,128)(2,1)S(1)} %convolution_convert_fusion), channel_id=1, source_target_pairs={{0,32},{32,64},{64,96},{96,0},{1,33},{33,65},{65,97},{97,1},{2,34}... | collective-permute-start | bytes 393224 | tf_op jit(solution)/shard_map/ppermute | solution.py:211
  11.4 10.1 %collective-permute-start.7 = (bf16[512,128]{1,0:T(8,128)(2,1)S(1)}, bf16[512,128]{1,0:T(8,128)(2,1)S(1)}, u32[]{:S(2)}, u32[]{:S(2)}) collective-permute-start(bf16[512,128]{1,0:T(8,128)(2,1)S(1)} %convolution_convert_fusion), channel_id=1, source_target_pairs={{0,64},{32,96},{64,0},{96,32},{1,65},{33,97},{65,1},{97,33},{2,66}... | collective-permute-start | bytes 393224 | tf_op jit(solution)/shard_map/ppermute | solution.py:211
  14.7 6.8 %collective-permute-start.8 = (bf16[512,128]{1,0:T(8,128)(2,1)S(1)}, bf16[512,128]{1,0:T(8,128)(2,1)S(1)}, u32[]{:S(2)}, u32[]{:S(2)}) collective-permute-start(bf16[512,128]{1,0:T(8,128)(2,1)S(1)} %convolution_convert_fusion), channel_id=1, source_target_pairs={{0,96},{32,0},{64,32},{96,64},{1,97},{33,1},{65,33},{97,65},{2,98}... | collective-permute-start | bytes 393224 | tf_op jit(solution)/shard_map/ppermute | solution.py:211
  16.4 12.5 %collective-permute-start.3 = (bf16[4,512,128]{2,1,0:T(8,128)(2,1)S(1)}, bf16[4,512,128]{2,1,0:T(8,128)(2,1)S(1)}, u32[]{:S(2)}, u32[]{:S(2)}) collective-permute-start(bf16[4,512,128]{2,1,0:T(8,128)(2,1)S(1)} %get-tuple-element.34), channel_id=1, source_target_pairs={{0,4},{4,8},{8,12},{12,0},{1,5},{5,9},{9,13},{13,1},{2,6},{6,10},{... | collective-permute-start | bytes 1572872 | tf_op jit(solution)/shard_map/ppermute | solution.py:211
  17.8 23.4 %collective-permute-start.4 = (bf16[4,512,128]{2,1,0:T(8,128)(2,1)S(1)}, bf16[4,512,128]{2,1,0:T(8,128)(2,1)S(1)}, u32[]{:S(2)}, u32[]{:S(2)}) collective-permute-start(bf16[4,512,128]{2,1,0:T(8,128)(2,1)S(1)} %get-tuple-element.34), channel_id=1, source_target_pairs={{0,8},{4,12},{8,0},{12,4},{1,9},{5,13},{9,1},{13,5},{2,10},{6,14},... | collective-permute-start | bytes 1572872 | tf_op jit(solution)/shard_map/ppermute | solution.py:211
  20.4 22.1 %collective-permute-start.5 = (bf16[4,512,128]{2,1,0:T(8,128)(2,1)S(1)}, bf16[4,512,128]{2,1,0:T(8,128)(2,1)S(1)}, u32[]{:S(2)}, u32[]{:S(2)}) collective-permute-start(bf16[4,512,128]{2,1,0:T(8,128)(2,1)S(1)} %get-tuple-element.34), channel_id=1, source_target_pairs={{0,12},{4,0},{8,4},{12,8},{1,13},{5,1},{9,5},{13,9},{2,14},{6,2},{... | collective-permute-start | bytes 1572872 | tf_op jit(solution)/shard_map/ppermute | solution.py:211
  21.6 4.8 %collective-permute-start.9 = (bf16[4,512,128]{2,1,0:T(8,128)(2,1)S(1)}, bf16[4,512,128]{2,1,0:T(8,128)(2,1)S(1)}, u32[]{:S(2)}, u32[]{:S(2)}) collective-permute-start(bf16[4,512,128]{2,1,0:T(8,128)(2,1)S(1)} %get-tuple-element.32), channel_id=1, source_target_pairs={{0,16},{16,0},{1,17},{17,1},{2,18},{18,2},{3,19},{19,3},{4,20},{20... | collective-permute-start | bytes 1572872 | tf_op jit(solution)/shard_map/ppermute | solution.py:211
  73.1 19.9 %collective-permute-start.10 = (bf16[16,128,128]{2,1,0:T(8,128)(2,1)}, bf16[16,128,128]{2,1,0:T(8,128)(2,1)}, u32[]{:S(2)}, u32[]{:S(2)}) collective-permute-start(bf16[16,128,128]{2,1,0:T(8,128)(2,1)} %get-tuple-element.14), channel_id=1, source_target_pairs={{0,4},{4,8},{8,12},{12,0},{1,5},{5,9},{9,13},{13,1},{2,6},{6,10},{... | collective-permute-start | bytes 1572872 | tf_op jit(solution)/shard_map/ppermute | solution.py:211
  86.6 12.0 %collective-permute-start.11 = (bf16[16,128,128]{2,1,0:T(8,128)(2,1)S(1)}, bf16[16,128,128]{2,1,0:T(8,128)(2,1)}, u32[]{:S(2)}, u32[]{:S(2)}) collective-permute-start(bf16[16,128,128]{2,1,0:T(8,128)(2,1)S(1)} %get-tuple-element.15), channel_id=1, source_target_pairs={{0,8},{4,12},{8,0},{12,4},{1,9},{5,13},{9,1},{13,5},{2,10},{6,14},... | collective-permute-start | bytes 1572872 | tf_op jit(solution)/shard_map/ppermute | solution.py:211
  86.7 12.4 %collective-permute-start.12 = (bf16[16,128,128]{2,1,0:T(8,128)(2,1)S(1)}, bf16[16,128,128]{2,1,0:T(8,128)(2,1)}, u32[]{:S(2)}, u32[]{:S(2)}) collective-permute-start(bf16[16,128,128]{2,1,0:T(8,128)(2,1)S(1)} %get-tuple-element.16), channel_id=1, source_target_pairs={{0,12},{4,0},{8,4},{12,8},{1,13},{5,1},{9,5},{13,9},{2,14},{6,2},{... | collective-permute-start | bytes 1572872 | tf_op jit(solution)/shard_map/ppermute | solution.py:211
  89.1 18.3 %collective-permute-start.16 = (bf16[16,128,128]{2,1,0:T(8,128)(2,1)S(1)}, bf16[16,128,128]{2,1,0:T(8,128)(2,1)}, u32[]{:S(2)}, u32[]{:S(2)}) collective-permute-start(bf16[16,128,128]{2,1,0:T(8,128)(2,1)S(1)} %get-tuple-element.18), channel_id=1, source_target_pairs={{0,16},{16,0},{1,17},{17,1},{2,18},{18,2},{3,19},{19,3},{4,20},{20... | collective-permute-start | bytes 1572872 | tf_op jit(solution)/shard_map/ppermute | solution.py:211
  100.8 22.0 %collective-permute-start.13 = (bf16[512,128]{1,0:T(8,128)(2,1)S(1)}, bf16[512,128]{1,0:T(8,128)(2,1)S(1)}, u32[]{:S(2)}, u32[]{:S(2)}) collective-permute-start(bf16[512,128]{1,0:T(8,128)(2,1)S(1)} %bitcast.80), channel_id=1, source_target_pairs={{0,1},{1,2},{2,3},{3,0},{4,5},{5,6},{6,7},{7,4},{8,9},{9,10},{10,1... | collective-permute-start | bytes 393224 | tf_op jit(solution)/shard_map/ppermute | solution.py:211
  104.9 18.4 %collective-permute-start.14 = (bf16[512,128]{1,0:T(8,128)(2,1)S(1)}, bf16[512,128]{1,0:T(8,128)(2,1)S(1)}, u32[]{:S(2)}, u32[]{:S(2)}) collective-permute-start(bf16[512,128]{1,0:T(8,128)(2,1)S(1)} %bitcast.79), channel_id=1, source_target_pairs={{0,2},{1,3},{2,0},{3,1},{4,6},{5,7},{6,4},{7,5},{8,10},{9,11},{10,... | collective-permute-start | bytes 393224 | tf_op jit(solution)/shard_map/ppermute | solution.py:211
  104.9 18.4 %collective-permute-start.15 = (bf16[512,128]{1,0:T(8,128)(2,1)S(1)}, bf16[512,128]{1,0:T(8,128)(2,1)S(1)}, u32[]{:S(2)}, u32[]{:S(2)}) collective-permute-start(bf16[512,128]{1,0:T(8,128)(2,1)S(1)} %bitcast.78), channel_id=1, source_target_pairs={{0,3},{1,0},{2,1},{3,2},{4,7},{5,4},{6,5},{7,6},{8,11},{9,8},{10,9... | collective-permute-start | bytes 393224 | tf_op jit(solution)/shard_map/ppermute | solution.py:211
  108.7 16.7 %collective-permute-start.17 = (bf16[512,128]{1,0:T(8,128)(2,1)S(1)}, bf16[512,128]{1,0:T(8,128)(2,1)S(1)}, u32[]{:S(2)}, u32[]{:S(2)}) collective-permute-start(bf16[512,128]{1,0:T(8,128)(2,1)S(1)} %bitcast.83), channel_id=1, source_target_pairs={{0,32},{32,64},{64,96},{96,0},{1,33},{33,65},{65,97},{97,1},{2,34}... | collective-permute-start | bytes 393224 | tf_op jit(solution)/shard_map/ppermute | solution.py:211
  120.5 8.3 %collective-permute-start.18 = (bf16[512,128]{1,0:T(8,128)(2,1)S(1)}, bf16[512,128]{1,0:T(8,128)(2,1)S(1)}, u32[]{:S(2)}, u32[]{:S(2)}) collective-permute-start(bf16[512,128]{1,0:T(8,128)(2,1)S(1)} %bitcast.82), channel_id=1, source_target_pairs={{0,64},{32,96},{64,0},{96,32},{1,65},{33,97},{65,1},{97,33},{2,66}... | collective-permute-start | bytes 393224 | tf_op jit(solution)/shard_map/ppermute | solution.py:211
  122.8 6.0 %collective-permute-start.19 = (bf16[512,128]{1,0:T(8,128)(2,1)S(1)}, bf16[512,128]{1,0:T(8,128)(2,1)S(1)}, u32[]{:S(2)}, u32[]{:S(2)}) collective-permute-start(bf16[512,128]{1,0:T(8,128)(2,1)S(1)} %bitcast.81), channel_id=1, source_target_pairs={{0,96},{32,0},{64,32},{96,64},{1,97},{33,1},{65,33},{97,65},{2,98}... | collective-permute-start | bytes 393224 | tf_op jit(solution)/shard_map/ppermute | solution.py:211
  129.6 26.9 %copy-start.2 = (bf16[384,128]{1,0:T(8,128)(2,1)S(1)}, bf16[384,128]{1,0:T(8,128)(2,1)}, u32[]{:S(2)}) copy-start(bf16[384,128]{1,0:T(8,128)(2,1)} %param.10) | copy-start | bytes 294916
  129.7 27.3 %copy-start.3 = (bf16[384,128]{1,0:T(8,128)(2,1)S(1)}, bf16[384,128]{1,0:T(8,128)(2,1)}, u32[]{:S(2)}) copy-start(bf16[384,128]{1,0:T(8,128)(2,1)} %param.9) | copy-start | bytes 294916
  152.3 18.2 %all-to-all-start.1 = ((f32[128,7,128]{2,1,0:T(8,128)}), f32[128,7,128]{2,1,0:T(8,128)S(1)}, u32[]{:S(2)}, u32[]{:S(2)}) async-start(f32[128,7,128]{2,1,0:T(8,128)} %broadcast_in_dim.14), calls=%async_computation.1 | async-start | bytes 1048576 | tf_op jit(solution)/shard_map/all_to_all | solution.py:288
  (2 other events, 3.2 us)

commit v3 on v2

v3 whole, which is shorter than its diff:
```python
import functools
import jax
import jax.numpy as jnp
from jax import lax
from jax.experimental import pallas as pl
from jax.experimental.pallas import tpu as pltpu
from jax.sharding import Mesh
from jax.sharding import PartitionSpec as P

GROUP_SCORES = 32
GROUP_SOFT = 16
GROUP_GRADS = 32


def blocks_kernel(
    place, count, bias, w_rows, w_wide, w_cols, left0, left1, left2, left3, right0, right1, teacher,
    left_grads, right_grads, bin_out, cross_out,
    left_tiles, right_tiles, target, logit, left_turn, right_turn, left_sum, right_sum,
    tile_sem, target_sem,
):
    left_from = (left0, left1, left2, left3)
    right_from = (right0, right1)
    slots, bins, tile, width = teacher.shape
    live = count[0]

    def target_copy(slot):
        return pltpu.make_async_copy(
            teacher.at[slot], target.at[lax.rem(slot, 2)], target_sem.at[lax.rem(slot, 2)]
        )

    def left_copy(slot, n):
        return pltpu.make_async_copy(
            left_from[n].at[slot], left_tiles.at[slot], tile_sem.at[slot, 0]
        )

    def right_copy(slot, n):
        return pltpu.make_async_copy(
            right_from[n].at[place[slot, 2]], right_tiles.at[slot], tile_sem.at[slot, 1]
        )

    for slot in range(slots):
        for n in range(len(left_from)):

            @pl.when((slot < live) & (place[slot, 0] == n))
            def _():
                left_copy(slot, n).start()

        for n in range(len(right_from)):

            @pl.when((slot < live) & (place[slot, 1] == n))
            def _():
                right_copy(slot, n).start()

    target_copy(0).start()
    bin_out[...] = jnp.zeros(bin_out.shape, jnp.float32)
    cross_out[...] = jnp.zeros(cross_out.shape, jnp.float32)

    def block(slot, _):
        buf = lax.rem(slot, 2)

        @pl.when(slot + 1 < live)
        def _():
            target_copy(slot + 1).start()

        left_copy(slot, 0).wait()
        right_copy(slot, 0).wait()
        left = left_tiles[slot]
        right = right_tiles[slot]
        left_turn[...] = left.T
        right_turn[...] = right.T
        left_sum[...] = jnp.zeros(left_sum.shape, jnp.float32)
        right_sum[...] = jnp.zeros(right_sum.shape, jnp.float32)

        def scores(g, highest):
            left = left_tiles[slot].reshape(tile // 16, 16, width)
            for j in range(GROUP_SCORES):
                k = g * GROUP_SCORES + j
                scaled = (left * w_rows[k][None]).reshape(tile, width)
                value = jnp.dot(scaled, right_turn[...], preferred_element_type=jnp.float32)
                value = value + bias[k]
                logit[k] = value
                highest = jnp.maximum(highest, value)
            return highest

        highest = lax.fori_loop(
            0, bins // GROUP_SCORES, scores, jnp.full((tile, tile), -jnp.inf, jnp.float32)
        )
        target_copy(slot).wait()

        STEP = 32
        ratios = []
        for p in range(0, tile, STEP):
            rows = pl.ds(p, STEP)
            top = highest[p : p + STEP]

            def soft(g, carried):
                total, mass, cross = carried
                for j in range(GROUP_SOFT):
                    k = g * GROUP_SOFT + j
                    value = logit[k, rows, :] - top
                    power = jnp.exp(value)
                    goal = target[buf, k, rows, :].astype(jnp.float32)
                    total = total + power
                    mass = mass + goal
                    cross = cross + goal * value
                    logit[k, rows, :] = power
                return total, mass, cross

            zero = jnp.zeros((STEP, tile), jnp.float32)
            total, mass, cross = lax.fori_loop(0, bins // GROUP_SOFT, soft, (zero, zero, zero))
            cross = mass * jnp.log(total) - cross
            cross_out[...] += cross.reshape(STEP // 8, 8, tile).sum(0)
            ratios.append(mass / total)
        ratio = jnp.concatenate(ratios, 0)

        def grads(g, _):
            left_wide = left_tiles[slot].astype(jnp.float32)
            pieces, scales = [], []
            left_part = jnp.zeros((tile, width), jnp.float32)
            for j in range(GROUP_GRADS):
                k = g * GROUP_GRADS + j
                grad = logit[k] * ratio - target[buf, k].astype(jnp.float32)
                grad = grad.astype(jnp.bfloat16)
                mixed = jnp.dot(grad, right_tiles[slot], preferred_element_type=jnp.float32)
                left_part = left_part + (
                    mixed.reshape(tile // 8, 8, width) * w_wide[k][None]
                ).reshape(tile, width)
                bin_out[k] += (mixed * left_wide).reshape(tile // 8, 8, width).sum(0)
                pieces.append(grad)
                scales.append(left_turn[...] * w_cols[k])
            left_sum[...] += left_part
            right_sum[...] += jnp.dot(
                jnp.concatenate(scales, 1),
                jnp.concatenate(pieces, 0),
                preferred_element_type=jnp.float32,
            )
            return 0

        lax.fori_loop(0, bins // GROUP_GRADS, grads, 0)
        left_grads[slot] = left_sum[...].astype(jnp.bfloat16)
        right_grads[slot] = right_sum[...].T.astype(jnp.bfloat16)
        return 0

    lax.fori_loop(0, live, block, 0)


def run_blocks(place, count, bin_weight, bin_bias, left_from, right_from, teacher):
    slots, bins, tile, _ = teacher.shape
    width = bin_weight.shape[0]
    turned = bin_weight.T
    w_rows = jnp.broadcast_to(turned[:, None, :], (bins, 16, width))
    w_wide = jnp.broadcast_to(turned[:, None, :].astype(jnp.float32), (bins, 8, width))
    w_cols = jnp.broadcast_to(turned[:, :, None], (bins, width, tile))
    smem = pl.BlockSpec(memory_space=pltpu.SMEM)
    vmem = pl.BlockSpec(memory_space=pltpu.VMEM)
    hbm = pl.BlockSpec(memory_space=pl.ANY)
    f32, bf16 = jnp.float32, jnp.bfloat16
    piece = jax.ShapeDtypeStruct((slots, tile, width), bf16)
    return pl.pallas_call(
        blocks_kernel,
        out_shape=[piece] * 2
        + [
            jax.ShapeDtypeStruct((bins, 8, width), f32),
            jax.ShapeDtypeStruct((8, tile), f32),
        ],
        in_specs=[smem] * 3 + [vmem] * 3 + [hbm] * 7,
        out_specs=[vmem] * 4,
        scratch_shapes=[
            pltpu.VMEM((slots, tile, width), bf16),
            pltpu.VMEM((slots, tile, width), bf16),
            pltpu.VMEM((2, bins, tile, tile), bf16),
            pltpu.VMEM((bins, tile, tile), f32),
            pltpu.VMEM((width, tile), bf16),
            pltpu.VMEM((width, tile), bf16),
            pltpu.VMEM((tile, width), f32),
            pltpu.VMEM((width, tile), f32),
            pltpu.SemaphoreType.DMA((slots, 2)),
            pltpu.SemaphoreType.DMA((2,)),
        ],
        compiler_params=pltpu.CompilerParams(vmem_limit_bytes=48 * 1024 * 1024),
        cost_estimate=pl.CostEstimate(
            flops=6 * 8 * 64 * 128**3, bytes_accessed=20 * 2**20, transcendentals=8 * 2**20
        ),
    )(place, count, bin_bias, w_rows, w_wide, w_cols, *left_from, *right_from, teacher)


AXES = ("z", "core", "y", "x")
TILES_DEV = 4


def own_spot(info, s, slot):
    row = info[s, 2 * slot]
    col = info[s, 2 * slot + 1]
    return (
        (lax.rem(row // 16, 4), lax.rem(row // 4, 4), lax.rem(row, 4)),
        (lax.rem(col // 128, 4), lax.rem(col // 64, 2), lax.rem(col, 4)),
    )


def pick_kernel(info, here, near0, near1, near2, near3, out0, out1, out2, out3, bank):
    outs = (out0, out1, out2, out3)
    for n, near in enumerate((near0, near1, near2, near3)):
        bank[pl.ds(4 * n, 4)] = near[...]
    slots = out0.shape[0]
    for s in range(4):
        for slot in range(slots):
            (_, x, t), _ = own_spot(info, s, slot)
            spot = lax.rem(here[3] - x + 4, 4) * 4 + t
            outs[(4 - s) % 4][slot] = bank[spot]


def pick_tiles(info, here, near):
    slots = (info.shape[1] - 1) // 2
    _, tile, width = near[0].shape
    smem = pl.BlockSpec(memory_space=pltpu.SMEM)
    vmem = pl.BlockSpec(memory_space=pltpu.VMEM)
    return pl.pallas_call(
        pick_kernel,
        out_shape=[jax.ShapeDtypeStruct((slots, tile, width), near[0].dtype)] * 4,
        in_specs=[smem] * 2 + [vmem] * 4,
        out_specs=[vmem] * 4,
        scratch_shapes=[pltpu.VMEM((16, tile, width), near[0].dtype)],
        compiler_params=pltpu.CompilerParams(vmem_limit_bytes=16 * 1024 * 1024),
    )(info, here, *near)


def fold_kernel(side, info, here, *refs):
    sources, (own, far1, far2, far3, total) = refs[:-5], refs[-5:]
    total[...] = jnp.zeros(total.shape, jnp.float32)
    slots = sources[0].shape[0]
    for s, source in enumerate(sources):
        live = info[s, 2 * slots]
        for slot in range(slots):
            (y, x, t), (z, core, u) = own_spot(info, s, slot)
            if side == 0:
                mine, spot = y == here[2], lax.rem(x - here[3] + 4, 4) * 4 + t
            else:
                mine, spot = core == here[1], lax.rem(z - here[0] + 4, 4) * 4 + u

            @pl.when((slot < live) & mine)
            def _():
                total[spot] += source[slot].astype(jnp.float32)

    own[...] = total[pl.ds(0, 4)]
    for n, far in enumerate((far1, far2, far3)):
        far[...] = total[pl.ds(4 * n + 4, 4)].astype(jnp.bfloat16)


def fold_slots(side, info, here, sources):
    _, tile, width = sources[0].shape
    smem = pl.BlockSpec(memory_space=pltpu.SMEM)
    vmem = pl.BlockSpec(memory_space=pltpu.VMEM)
    far = jax.ShapeDtypeStruct((4, tile, width), jnp.bfloat16)
    return pl.pallas_call(
        functools.partial(fold_kernel, side),
        out_shape=[jax.ShapeDtypeStruct((4, tile, width), jnp.float32)] + [far] * 3,
        in_specs=[smem] * 2 + [vmem] * len(sources),
        out_specs=[vmem] * 4,
        scratch_shapes=[pltpu.VMEM((16, tile, width), jnp.float32)],
        compiler_params=pltpu.CompilerParams(vmem_limit_bytes=16 * 1024 * 1024),
    )(info, here, *sources)


def shift(value, axis, step):
    size = lax.axis_size(axis)
    return lax.ppermute(value, axis, [(i, (i + step) % size) for i in range(size)])


def ring(value, axis):
    return [shift(value, axis, s) for s in range(1, lax.axis_size(axis))]


SCALARS = 16


def split_rows(value):
    body, tail = value[:-SCALARS], value[-SCALARS:]
    high = tail.astype(jnp.bfloat16)
    low = (tail - high.astype(jnp.float32)).astype(jnp.bfloat16)
    return jnp.concatenate([body.astype(jnp.bfloat16), high, low])


def join_rows(sent):
    sent = sent.astype(jnp.float32)
    body, high, low = sent[: -2 * SCALARS], sent[-2 * SCALARS : -SCALARS], sent[-SCALARS:]
    return jnp.concatenate([body, high + low])


def add_kernel(value, sent1, sent2, sent3, out, send):
    total = value[...]
    for sent in (sent1, sent2, sent3):
        total = total + join_rows(sent[...])
    out[...] = total
    send[...] = split_rows(total)


def add_sent(value, sent):
    vmem = pl.BlockSpec(memory_space=pltpu.VMEM)
    return pl.pallas_call(
        add_kernel,
        out_shape=[
            jax.ShapeDtypeStruct(value.shape, jnp.float32),
            jax.ShapeDtypeStruct(sent[0].shape, jnp.bfloat16),
        ],
        in_specs=[vmem] * 4,
        out_specs=[vmem] * 2,
    )(value, *sent)


def per_device(
    single, left_weight, right_weight, bin_weight, bin_bias, block_tiles, block_count, teacher
):
    slots, bins, tile = teacher.shape[1:4]
    devices = lax.axis_size(AXES)
    own_tiles = block_tiles[0]
    left_wide = left_weight.astype(jnp.float32)
    right_wide = right_weight.astype(jnp.float32)
    info = jnp.concatenate([own_tiles.reshape(1, -1), block_count[None]], axis=1)
    info_y = jnp.concatenate([info] + ring(info, "y"))
    info_core = jnp.concatenate([info] + ring(info, "core"))
    left_local = jnp.dot(single, left_weight, preferred_element_type=jnp.float32).astype(
        jnp.bfloat16
    )
    right_local = jnp.dot(single, right_weight, preferred_element_type=jnp.float32).astype(
        jnp.bfloat16
    )
    rows_dev, width = left_local.shape
    left_local = left_local.reshape(-1, tile, width)
    right_local = right_local.reshape(-1, tile, width)
    here = jnp.stack([lax.axis_index(a) for a in AXES]).astype(jnp.int32)
    z, core, y = here[0], here[1], here[2]
    picked = pick_tiles(info_y, here, [left_local] + ring(left_local, "x"))
    left_from = [picked[0]] + [shift(picked[s], "y", s) for s in (1, 2, 3)]
    right_near = jnp.concatenate([right_local] + ring(right_local, "z"))
    right_from = [right_near, shift(right_near, "core", 1)]
    row, col = own_tiles[:, 0], own_tiles[:, 1]
    place = jnp.stack(
        [
            (y - row // 16 % 4) % 4,
            (core - col // 64 % 2) % 2,
            (z - col // 128 % 4) % 4 * TILES_DEV + col % TILES_DEV,
        ],
        axis=1,
    )
    left_slots, right_slots, bins_part, cross_part = run_blocks(
        place, block_count, bin_weight, bin_bias, left_from, right_from, teacher[0]
    )
    left_own, *left_far = fold_slots(0, info_y, here, [left_slots] + ring(left_slots, "y"))
    right_own, *right_far = fold_slots(
        1, info_core, here, [right_slots] + ring(right_slots, "core")
    )
    left_rows_grad, right_rows_grad = left_own, right_own
    for s in (1, 2, 3):
        left_rows_grad = left_rows_grad + shift(left_far[s - 1], "x", s).astype(jnp.float32)
        right_rows_grad = right_rows_grad + shift(right_far[s - 1], "z", s).astype(jnp.float32)
    left_rows_grad = left_rows_grad.reshape(rows_dev, width)
    right_rows_grad = right_rows_grad.reshape(rows_dev, width)
    single_wide = single.astype(jnp.float32)
    part_left = jnp.dot(single_wide.T, left_rows_grad, precision=lax.Precision.HIGHEST)
    part_right = jnp.dot(single_wide.T, right_rows_grad, precision=lax.Precision.HIGHEST)
    depth = part_left.shape[0]
    scalars = jnp.stack([jnp.sum(cross_part), block_count[0].astype(jnp.float32)])
    scalars = jnp.pad(scalars[None], ((0, SCALARS - 1), (0, width - 2)))
    part_bin = jnp.sum(bins_part, axis=1)
    first = jnp.concatenate([part_left, part_bin, jnp.zeros_like(scalars)])
    second = jnp.concatenate([part_right, jnp.zeros_like(part_bin), scalars])
    low_core = core == 0
    total = jnp.where(low_core, first, second) + shift(
        jnp.where(low_core, second, first), "core", 1
    )
    send = split_rows(total)
    for axis in ("z", "y", "x"):
        total, send = add_sent(total, ring(send, axis))
    other = shift(total, "core", 1)
    first = jnp.where(low_core, total, other)
    second = jnp.where(low_core, other, total)
    grad_single = (
        jnp.dot(left_rows_grad, left_wide.T, precision=lax.Precision.HIGHEST)
        + jnp.dot(right_rows_grad, right_wide.T, precision=lax.Precision.HIGHEST)
    ).astype(jnp.bfloat16)
    grad_left = first[:depth] / devices
    grad_right = second[:depth] / devices
    grad_bin = first[depth : depth + bins].T / devices
    loss_value = second[depth + bins, 0] / (second[depth + bins, 1] * (tile * tile))
    return (grad_single, grad_left, grad_right, grad_bin, loss_value)


def solution(mesh):
    torus = Mesh(mesh.devices.reshape(4, 2, 4, 4), AXES)
    return jax.shard_map(
        per_device,
        mesh=torus,
        in_specs=(
            P(AXES, None),
            P(),
            P(),
            P(),
            P(),
            P(AXES, None, None),
            P(AXES),
            P(AXES, None, None, None, None),
        ),
        out_specs=(P(AXES, None), P(), P(), P(), P()),
        check_vma=False,
    )
```

time: 175 us -> 157 us (0.90)
  blocking collectives: 21.6 us -> 0 us
  starting transfers between devices: 61.1 us -> 75 us
  waiting for transfers between devices: 42.4 us -> 33.5 us
  Pallas kernels: 26.8 us -> 23.8 us
  other arithmetic: 7.97 us -> 5.48 us
  local copies, waits for them, and re-layouts: 6.17 us -> 8.47 us
    all_to_all x1 -> x0, blocking collectives: 21.6 us -> none  [per_device(): mine = jnp.sum(lax.all_to_all(packed, AXES, 0, 0), axis=0)]
    ppermute x20 -> x35, starting transfers between devices: 56.9 us -> 75 us  [shift(): lax.ppermute(value, axis, [(i, (i + step) % size) for i in range(size)])]
    all_to_all x1 -> x0, waiting for transfers between devices: 12.3 us -> none  [per_device(): lax.all_to_all(jnp.broadcast_to(mine[None], (devices, chunk, width)), AXE...]
    another operation x7 -> x2, other arithmetic: 4.82 us -> 0.15 us  [the longest x1 0.08 us: per_device(): here = jnp.stack([lax.axis_index(a) for a in AXES]).astype(jnp.int32)]
    all_to_all x1 -> x0, starting transfers between devices: 4.17 us -> none  [per_device(): lax.all_to_all(jnp.broadcast_to(mine[None], (devices, chunk, width)), AXE...]
    ppermute x20 -> x35, waiting for transfers between devices: 30.1 us -> 33.5 us  [shift(): lax.ppermute(value, axis, [(i, (i + step) % size) for i in range(size)])]
    unnamed x12 -> x31, local copies, waits for them, and re-layouts: 1.18 us -> 4.19 us
    pallas_call x1 -> x7, Pallas kernels: 26.8 us -> 23.8 us  [the longest x1 14.8 us: run_blocks(): pl.pallas_call(blocks_kernel, out_shape=[piece] * 2 + [jax.ShapeDtypeStru...]
  transfers between devices with their start and end apart: 21 -> 35, of which waited for: 10 -> 19; matrix products, arithmetic and copies ran while one was open for 5% -> 5% of each run, Pallas kernels for 0% -> 2%
where the time goes in v3:
time: 157 us; the launch traced here: 155 us
  starting transfers between devices  75 us (48%)
  waiting for transfers between devices  33.5 us (21%)
  Pallas kernels  23.8 us (15%)
  local copies, waits for them, and re-layouts  8.47 us (5%)
  other arithmetic  5.48 us (3%)
  matrix products  5.15 us (3%)
  between operations  4.07 us (3%)
    ppermute x35, starting transfers between devices, shift(): lax.ppermute(value, axis, [(i, (i + step) % size) for i in range(size)])  75 us
    ppermute x35, waiting for transfers between devices, shift(): lax.ppermute(value, axis, [(i, (i + step) % size) for i in range(size)])  33.5 us
    pallas_call x1, Pallas kernels, run_blocks(): pl.pallas_call(blocks_kernel, out_shape=[piece] * 2 + [jax.ShapeDtypeStru...  14.8 us
    pallas_call x3, Pallas kernels, add_sent(): pl.pallas_call(add_kernel, out_shape=[jax.ShapeDtypeStruct(value.shape, j...  5.74 us
    unnamed x31, local copies, waits for them, and re-layouts  4.19 us
  transfers between devices with their start and end apart: 35, of which 19 were waited for; matrix products, arithmetic and copies ran while one was open for 5% of the time, Pallas kernels for 2%

profile of v3, /device:TPU:1, one launch (start us, length us, event | category | flops | bytes accessed | tf_op | source)
XLA Modules:
  0.0 155.5 jit_solution(2371538366363724851)
XLA Ops:
  2.3 2.1 %collective-permute-start = (s32[1,17]{1,0:T(1,128)S(1)}, s32[1,17]{1,0:T(1,128)S(1)}, u32[]{:S(2)}, u32[]{:S(2)}) collective-permute-start(s32[1,17]{1,0:T(1,128)S(1)} %pad_add_fusion.3), channel_id=1, source_target_pairs={{0,4},{4,8},{8,12},{12,0},{1,5},{5,9},{9,13},{13,1},{2,6},{6,10},{... | collective-permute-start | bytes 212 | tf_op jit(solution)/shard_map/ppermute | solution.py:266
  4.4 2.6 %collective-permute-start.1 = (s32[1,17]{1,0:T(1,128)S(1)}, s32[1,17]{1,0:T(1,128)S(1)}, u32[]{:S(2)}, u32[]{:S(2)}) collective-permute-start(s32[1,17]{1,0:T(1,128)S(1)} %pad_add_fusion.3), channel_id=1, source_target_pairs={{0,8},{4,12},{8,0},{12,4},{1,9},{5,13},{9,1},{13,5},{2,10},{6,14},... | collective-permute-start | bytes 212 | tf_op jit(solution)/shard_map/ppermute | solution.py:266
  8.2 3.7 %collective-permute-start.10 = (bf16[4,128,128]{2,1,0:T(8,128)(2,1)S(1)}, bf16[4,128,128]{2,1,0:T(8,128)(2,1)S(1)}, u32[]{:S(2)}, u32[]{:S(2)}) collective-permute-start(bf16[4,128,128]{2,1,0:T(8,128)(2,1)S(1)} %bitcast.46), channel_id=1, source_target_pairs={{0,64},{32,96},{64,0},{96,32},{1,65},{33,97},{65,1},{97,33},{2,66}... | collective-permute-start | bytes 393224 | tf_op jit(solution)/shard_map/ppermute | solution.py:266
  18.9 2.5 %collective-permute-start.4 = (bf16[4,128,128]{2,1,0:T(8,128)(2,1)S(1)}, bf16[4,128,128]{2,1,0:T(8,128)(2,1)S(1)}, u32[]{:S(2)}, u32[]{:S(2)}) collective-permute-start(bf16[4,128,128]{2,1,0:T(8,128)(2,1)S(1)} %bitcast.39), channel_id=1, source_target_pairs={{0,2},{1,3},{2,0},{3,1},{4,6},{5,7},{6,4},{7,5},{8,10},{9,11},{10,... | collective-permute-start | bytes 393224 | tf_op jit(solution)/shard_map/ppermute | solution.py:266
  22.7 3.0 %collective-permute-start.12 = (bf16[16,128,128]{2,1,0:T(8,128)(2,1)S(1)}, bf16[16,128,128]{2,1,0:T(8,128)(2,1)S(1)}, u32[]{:S(2)}, u32[]{:S(2)}) collective-permute-start(bf16[16,128,128]{2,1,0:T(8,128)(2,1)S(1)} %pad_maximum_fusion.right0), channel_id=1, source_target_pairs={{0,16},{16,0},{1,17},{17,1},{2,18},{18,2},{3,19},{19,3},{4,20},{20... | collective-permute-start | bytes 1572872 | tf_op jit(solution)/shard_map/ppermute | solution.py:266
  27.2 2.2 %collective-permute-start.7 = (bf16[8,128,128]{2,1,0:T(8,128)(2,1)S(1)}, bf16[8,128,128]{2,1,0:T(8,128)(2,1)S(1)}, u32[]{:S(2)}, u32[]{:S(2)}) collective-permute-start(bf16[8,128,128]{2,1,0:T(8,128)(2,1)S(1)} %get-tuple-element.28), channel_id=1, source_target_pairs={{0,8},{4,12},{8,0},{12,4},{1,9},{5,13},{9,1},{13,5},{2,10},{6,14},... | collective-permute-start | bytes 786440 | tf_op jit(solution)/shard_map/ppermute | solution.py:266
  30.7 4.8 %collective-permute-done.6.left1 = bf16[8,128,128]{2,1,0:T(8,128)(2,1)S(1)} collective-permute-done((bf16[8,128,128]{2,1,0:T(8,128)(2,1)S(1)}, bf16[8,128,128]{2,1,0:T(8,128)(2,1)S(1)}, u32[]{:S(2)}, u32[]{:S(2)}) %collective-permute-start.6) | collective-permute-done | bytes 262176 | tf_op jit(solution)/shard_map/ppermute | solution.py:266
  35.5 2.6 %collective-permute-done.7.left2 = bf16[8,128,128]{2,1,0:T(8,128)(2,1)S(1)} collective-permute-done((bf16[8,128,128]{2,1,0:T(8,128)(2,1)S(1)}, bf16[8,128,128]{2,1,0:T(8,128)(2,1)S(1)}, u32[]{:S(2)}, u32[]{:S(2)}) %collective-permute-start.7) | collective-permute-done | bytes 262176 | tf_op jit(solution)/shard_map/ppermute | solution.py:266
  38.0 2.4 %collective-permute-done.8.left3 = bf16[8,128,128]{2,1,0:T(8,128)(2,1)S(1)} collective-permute-done((bf16[8,128,128]{2,1,0:T(8,128)(2,1)S(1)}, bf16[8,128,128]{2,1,0:T(8,128)(2,1)S(1)}, u32[]{:S(2)}, u32[]{:S(2)}) %collective-permute-start.8) | collective-permute-done | bytes 262176 | tf_op jit(solution)/shard_map/ppermute | solution.py:266
  43.9 14.8 %shard_map.120 = (bf16[8,128,128]{2,1,0:T(8,128)(2,1)S(1)}, bf16[8,128,128]{2,1,0:T(8,128)(2,1)S(1)}, f32[64,8,128]{2,1,0:T(8,128)S(1)}, f32[8,128]{1,0:T(8,128)S(1)}) custom-call(s32[8,3]{1,0:T(8,128)S(1)} %pad_add_fusion.place, s32[1]{0:T(128)} %copy.27.count, f32[64]{0:T(128)S(1)} %copy-done.1, bf16[64,16,128]{2,1,0:T(8,128)(2,1)S(1)} %broadcast_in_dim.15.w_rows, ...), custom_call_target="tpu_custom_call" | custom-call | flops 6442450944 | bytes 20971520 | tf_op jit(solution)/shard_map/pallas_call | solution.py:159
  58.7 13.8 %collective-permute-start.13 = (bf16[8,128,128]{2,1,0:T(8,128)(2,1)S(1)}, bf16[8,128,128]{2,1,0:T(8,128)(2,1)S(1)}, u32[]{:S(2)}, u32[]{:S(2)}) collective-permute-start(bf16[8,128,128]{2,1,0:T(8,128)(2,1)S(1)} %get-tuple-element.30.refs_0_), channel_id=1, source_target_pairs={{0,4},{4,8},{8,12},{12,0},{1,5},{5,9},{9,13},{13,1},{2,6},{6,10},{... | collective-permute-start | bytes 786440 | tf_op jit(solution)/shard_map/ppermute | solution.py:266
  72.5 2.5 %collective-permute-start.15 = (bf16[8,128,128]{2,1,0:T(8,128)(2,1)S(1)}, bf16[8,128,128]{2,1,0:T(8,128)(2,1)S(1)}, u32[]{:S(2)}, u32[]{:S(2)}) collective-permute-start(bf16[8,128,128]{2,1,0:T(8,128)(2,1)S(1)} %get-tuple-element.30.refs_0_), channel_id=1, source_target_pairs={{0,12},{4,0},{8,4},{12,8},{1,13},{5,1},{9,5},{13,9},{2,14},{6,2},{... | collective-permute-start | bytes 786440 | tf_op jit(solution)/shard_map/ppermute | solution.py:266
  75.6 3.1 %collective-permute-done.13.refs_1_ = bf16[8,128,128]{2,1,0:T(8,128)(2,1)S(1)} collective-permute-done((bf16[8,128,128]{2,1,0:T(8,128)(2,1)S(1)}, bf16[8,128,128]{2,1,0:T(8,128)(2,1)S(1)}, u32[]{:S(2)}, u32[]{:S(2)}) %collective-permute-start.13) | collective-permute-done | bytes 262176 | tf_op jit(solution)/shard_map/ppermute | solution.py:266
  78.7 3.9 %collective-permute-done.14.refs_2_ = bf16[8,128,128]{2,1,0:T(8,128)(2,1)S(1)} collective-permute-done((bf16[8,128,128]{2,1,0:T(8,128)(2,1)S(1)}, bf16[8,128,128]{2,1,0:T(8,128)(2,1)S(1)}, u32[]{:S(2)}, u32[]{:S(2)}) %collective-permute-start.14) | collective-permute-done | bytes 262176 | tf_op jit(solution)/shard_map/ppermute | solution.py:266
  84.2 4.1 %collective-permute-start.17 = (bf16[4,128,128]{2,1,0:T(8,128)(2,1)S(1)}, bf16[4,128,128]{2,1,0:T(8,128)(2,1)S(1)}, u32[]{:S(2)}, u32[]{:S(2)}) collective-permute-start(bf16[4,128,128]{2,1,0:T(8,128)(2,1)S(1)} %get-tuple-element.33), channel_id=1, source_target_pairs={{0,2},{1,3},{2,0},{3,1},{4,6},{5,7},{6,4},{7,5},{8,10},{9,11},{10,... | collective-permute-start | bytes 393224 | tf_op jit(solution)/shard_map/ppermute | solution.py:266
  90.8 4.6 %collective-permute-start.21 = (bf16[4,128,128]{2,1,0:T(8,128)(2,1)S(1)}, bf16[4,128,128]{2,1,0:T(8,128)(2,1)S(1)}, u32[]{:S(2)}, u32[]{:S(2)}) collective-permute-start(bf16[4,128,128]{2,1,0:T(8,128)(2,1)S(1)} %get-tuple-element.37), channel_id=1, source_target_pairs={{0,32},{32,64},{64,96},{96,0},{1,33},{33,65},{65,97},{97,1},{2,34}... | collective-permute-start | bytes 393224 | tf_op jit(solution)/shard_map/ppermute | solution.py:266
  97.3 2.1 %collective-permute-start.23 = (bf16[4,128,128]{2,1,0:T(8,128)(2,1)S(1)}, bf16[4,128,128]{2,1,0:T(8,128)(2,1)S(1)}, u32[]{:S(2)}, u32[]{:S(2)}) collective-permute-start(bf16[4,128,128]{2,1,0:T(8,128)(2,1)S(1)} %get-tuple-element.39), channel_id=1, source_target_pairs={{0,96},{32,0},{64,32},{96,64},{1,97},{33,1},{65,33},{97,65},{2,98}... | collective-permute-start | bytes 393224 | tf_op jit(solution)/shard_map/ppermute | solution.py:266
  102.2 8.6 %collective-permute-start.24 = (f32[464,128]{1,0:T(8,128)S(1)}, f32[464,128]{1,0:T(8,128)S(1)}, u32[]{:S(2)}, u32[]{:S(2)}) collective-permute-start(f32[464,128]{1,0:T(8,128)S(1)} %fusion.1), channel_id=1, source_target_pairs={{0,16},{16,0},{1,17},{17,1},{2,18},{18,2},{3,19},{19,3},{4,20},{20... | collective-permute-start | bytes 712712 | tf_op jit(solution)/shard_map/ppermute | solution.py:266
  113.5 2.2 %collective-permute-start.26 = (bf16[480,128]{1,0:T(8,128)(2,1)S(1)}, bf16[480,128]{1,0:T(8,128)(2,1)S(1)}, u32[]{:S(2)}, u32[]{:S(2)}) collective-permute-start(bf16[480,128]{1,0:T(8,128)(2,1)S(1)} %pad_maximum_fusion.1), channel_id=1, source_target_pairs={{0,64},{32,96},{64,0},{96,32},{1,65},{33,97},{65,1},{97,33},{2,66}... | collective-permute-start | bytes 368648 | tf_op jit(solution)/shard_map/ppermute | solution.py:266
  118.0 3.3 %collective-permute-done.26.sent2 = bf16[480,128]{1,0:T(8,128)(2,1)S(1)} collective-permute-done((bf16[480,128]{1,0:T(8,128)(2,1)S(1)}, bf16[480,128]{1,0:T(8,128)(2,1)S(1)}, u32[]{:S(2)}, u32[]{:S(2)}) %collective-permute-start.26) | collective-permute-done | bytes 122912 | tf_op jit(solution)/shard_map/ppermute | solution.py:266
  124.9 2.9 %collective-permute-start.29 = (bf16[480,128]{1,0:T(8,128)(2,1)}, bf16[480,128]{1,0:T(8,128)(2,1)S(1)}, u32[]{:S(2)}, u32[]{:S(2)}) collective-permute-start(bf16[480,128]{1,0:T(8,128)(2,1)} %get-tuple-element.43), channel_id=1, source_target_pairs={{0,8},{4,12},{8,0},{12,4},{1,9},{5,13},{9,1},{13,5},{2,10},{6,14},... | collective-permute-start | bytes 368648 | tf_op jit(solution)/shard_map/ppermute | solution.py:266
  129.7 2.8 %collective-permute-done.29.sent2 = bf16[480,128]{1,0:T(8,128)(2,1)S(1)} collective-permute-done((bf16[480,128]{1,0:T(8,128)(2,1)}, bf16[480,128]{1,0:T(8,128)(2,1)S(1)}, u32[]{:S(2)}, u32[]{:S(2)}) %collective-permute-start.29) | collective-permute-done | bytes 122912 | tf_op jit(solution)/shard_map/ppermute | solution.py:266
  136.1 2.1 %collective-permute-start.32 = (bf16[480,128]{1,0:T(8,128)(2,1)}, bf16[480,128]{1,0:T(8,128)(2,1)S(1)}, u32[]{:S(2)}, u32[]{:S(2)}) collective-permute-start(bf16[480,128]{1,0:T(8,128)(2,1)} %get-tuple-element.45), channel_id=1, source_target_pairs={{0,2},{1,3},{2,0},{3,1},{4,6},{5,7},{6,4},{7,5},{8,10},{9,11},{10,... | collective-permute-start | bytes 368648 | tf_op jit(solution)/shard_map/ppermute | solution.py:266
  145.4 3.3 %collective-permute-start.34 = (f32[464,128]{1,0:T(8,128)}, f32[464,128]{1,0:T(8,128)S(1)}, u32[]{:S(2)}, u32[]{:S(2)}) collective-permute-start(f32[464,128]{1,0:T(8,128)} %get-tuple-element.46), channel_id=1, source_target_pairs={{0,16},{16,0},{1,17},{17,1},{2,18},{18,2},{3,19},{19,3},{4,20},{20... | collective-permute-start | bytes 712712 | tf_op jit(solution)/shard_map/ppermute | solution.py:266
  (122 shorter events, 51.4 us)
Async XLA Ops:
  2.3 19.2 %collective-permute-start = (s32[1,17]{1,0:T(1,128)S(1)}, s32[1,17]{1,0:T(1,128)S(1)}, u32[]{:S(2)}, u32[]{:S(2)}) collective-permute-start(s32[1,17]{1,0:T(1,128)S(1)} %pad_add_fusion.3), channel_id=1, source_target_pairs={{0,4},{4,8},{8,12},{12,0},{1,5},{5,9},{9,13},{13,1},{2,6},{6,10},{... | collective-permute-start | bytes 212 | tf_op jit(solution)/shard_map/ppermute | solution.py:266
  4.4 18.3 %collective-permute-start.1 = (s32[1,17]{1,0:T(1,128)S(1)}, s32[1,17]{1,0:T(1,128)S(1)}, u32[]{:S(2)}, u32[]{:S(2)}) collective-permute-start(s32[1,17]{1,0:T(1,128)S(1)} %pad_add_fusion.3), channel_id=1, source_target_pairs={{0,8},{4,12},{8,0},{12,4},{1,9},{5,13},{9,1},{13,5},{2,10},{6,14},... | collective-permute-start | bytes 212 | tf_op jit(solution)/shard_map/ppermute | solution.py:266
  8.2 7.3 %collective-permute-start.10 = (bf16[4,128,128]{2,1,0:T(8,128)(2,1)S(1)}, bf16[4,128,128]{2,1,0:T(8,128)(2,1)S(1)}, u32[]{:S(2)}, u32[]{:S(2)}) collective-permute-start(bf16[4,128,128]{2,1,0:T(8,128)(2,1)S(1)} %bitcast.46), channel_id=1, source_target_pairs={{0,64},{32,96},{64,0},{96,32},{1,65},{33,97},{65,1},{97,33},{2,66}... | collective-permute-start | bytes 393224 | tf_op jit(solution)/shard_map/ppermute | solution.py:266
  12.3 6.7 %collective-permute-start.9 = (bf16[4,128,128]{2,1,0:T(8,128)(2,1)S(1)}, bf16[4,128,128]{2,1,0:T(8,128)(2,1)S(1)}, u32[]{:S(2)}, u32[]{:S(2)}) collective-permute-start(bf16[4,128,128]{2,1,0:T(8,128)(2,1)S(1)} %bitcast.48), channel_id=1, source_target_pairs={{0,32},{32,64},{64,96},{96,0},{1,33},{33,65},{65,97},{97,1},{2,34}... | collective-permute-start | bytes 393224 | tf_op jit(solution)/shard_map/ppermute | solution.py:266
  15.5 10.3 %collective-permute-start.2 = (s32[1,17]{1,0:T(1,128)S(1)}, s32[1,17]{1,0:T(1,128)S(1)}, u32[]{:S(2)}, u32[]{:S(2)}) collective-permute-start(s32[1,17]{1,0:T(1,128)S(1)} %pad_add_fusion.3), channel_id=1, source_target_pairs={{0,12},{4,0},{8,4},{12,8},{1,13},{5,1},{9,5},{13,9},{2,14},{6,2},{... | collective-permute-start | bytes 212 | tf_op jit(solution)/shard_map/ppermute | solution.py:266
  17.7 8.1 %collective-permute-start.3 = (bf16[4,128,128]{2,1,0:T(8,128)(2,1)S(1)}, bf16[4,128,128]{2,1,0:T(8,128)(2,1)S(1)}, u32[]{:S(2)}, u32[]{:S(2)}) collective-permute-start(bf16[4,128,128]{2,1,0:T(8,128)(2,1)S(1)} %bitcast.38), channel_id=1, source_target_pairs={{0,1},{1,2},{2,3},{3,0},{4,5},{5,6},{6,7},{7,4},{8,9},{9,10},{10,1... | collective-permute-start | bytes 393224 | tf_op jit(solution)/shard_map/ppermute | solution.py:266
  18.9 6.9 %collective-permute-start.4 = (bf16[4,128,128]{2,1,0:T(8,128)(2,1)S(1)}, bf16[4,128,128]{2,1,0:T(8,128)(2,1)S(1)}, u32[]{:S(2)}, u32[]{:S(2)}) collective-permute-start(bf16[4,128,128]{2,1,0:T(8,128)(2,1)S(1)} %bitcast.39), channel_id=1, source_target_pairs={{0,2},{1,3},{2,0},{3,1},{4,6},{5,7},{6,4},{7,5},{8,10},{9,11},{10,... | collective-permute-start | bytes 393224 | tf_op jit(solution)/shard_map/ppermute | solution.py:266
  22.7 17.7 %collective-permute-start.12 = (bf16[16,128,128]{2,1,0:T(8,128)(2,1)S(1)}, bf16[16,128,128]{2,1,0:T(8,128)(2,1)S(1)}, u32[]{:S(2)}, u32[]{:S(2)}) collective-permute-start(bf16[16,128,128]{2,1,0:T(8,128)(2,1)S(1)} %pad_maximum_fusion.right0), channel_id=1, source_target_pairs={{0,16},{16,0},{1,17},{17,1},{2,18},{18,2},{3,19},{19,3},{4,20},{20... | collective-permute-start | bytes 1572872 | tf_op jit(solution)/shard_map/ppermute | solution.py:266
  27.1 8.4 %collective-permute-start.6 = (bf16[8,128,128]{2,1,0:T(8,128)(2,1)S(1)}, bf16[8,128,128]{2,1,0:T(8,128)(2,1)S(1)}, u32[]{:S(2)}, u32[]{:S(2)}) collective-permute-start(bf16[8,128,128]{2,1,0:T(8,128)(2,1)S(1)} %get-tuple-element.27), channel_id=1, source_target_pairs={{0,4},{4,8},{8,12},{12,0},{1,5},{5,9},{9,13},{13,1},{2,6},{6,10},{... | collective-permute-start | bytes 786440 | tf_op jit(solution)/shard_map/ppermute | solution.py:266
  27.2 10.9 %collective-permute-start.7 = (bf16[8,128,128]{2,1,0:T(8,128)(2,1)S(1)}, bf16[8,128,128]{2,1,0:T(8,128)(2,1)S(1)}, u32[]{:S(2)}, u32[]{:S(2)}) collective-permute-start(bf16[8,128,128]{2,1,0:T(8,128)(2,1)S(1)} %get-tuple-element.28), channel_id=1, source_target_pairs={{0,8},{4,12},{8,0},{12,4},{1,9},{5,13},{9,1},{13,5},{2,10},{6,14},... | collective-permute-start | bytes 786440 | tf_op jit(solution)/shard_map/ppermute | solution.py:266
  29.4 11.0 %collective-permute-start.8 = (bf16[8,128,128]{2,1,0:T(8,128)(2,1)S(1)}, bf16[8,128,128]{2,1,0:T(8,128)(2,1)S(1)}, u32[]{:S(2)}, u32[]{:S(2)}) collective-permute-start(bf16[8,128,128]{2,1,0:T(8,128)(2,1)S(1)} %get-tuple-element.29), channel_id=1, source_target_pairs={{0,12},{4,0},{8,4},{12,8},{1,13},{5,1},{9,5},{13,9},{2,14},{6,2},{... | collective-permute-start | bytes 786440 | tf_op jit(solution)/shard_map/ppermute | solution.py:266
  58.7 20.0 %collective-permute-start.13 = (bf16[8,128,128]{2,1,0:T(8,128)(2,1)S(1)}, bf16[8,128,128]{2,1,0:T(8,128)(2,1)S(1)}, u32[]{:S(2)}, u32[]{:S(2)}) collective-permute-start(bf16[8,128,128]{2,1,0:T(8,128)(2,1)S(1)} %get-tuple-element.30.refs_0_), channel_id=1, source_target_pairs={{0,4},{4,8},{8,12},{12,0},{1,5},{5,9},{9,13},{13,1},{2,6},{6,10},{... | collective-permute-start | bytes 786440 | tf_op jit(solution)/shard_map/ppermute | solution.py:266
  72.5 10.0 %collective-permute-start.14 = (bf16[8,128,128]{2,1,0:T(8,128)(2,1)S(1)}, bf16[8,128,128]{2,1,0:T(8,128)(2,1)S(1)}, u32[]{:S(2)}, u32[]{:S(2)}) collective-permute-start(bf16[8,128,128]{2,1,0:T(8,128)(2,1)S(1)} %get-tuple-element.30.refs_0_), channel_id=1, source_target_pairs={{0,8},{4,12},{8,0},{12,4},{1,9},{5,13},{9,1},{13,5},{2,10},{6,14},... | collective-permute-start | bytes 786440 | tf_op jit(solution)/shard_map/ppermute | solution.py:266
  72.5 10.3 %collective-permute-start.15 = (bf16[8,128,128]{2,1,0:T(8,128)(2,1)S(1)}, bf16[8,128,128]{2,1,0:T(8,128)(2,1)S(1)}, u32[]{:S(2)}, u32[]{:S(2)}) collective-permute-start(bf16[8,128,128]{2,1,0:T(8,128)(2,1)S(1)} %get-tuple-element.30.refs_0_), channel_id=1, source_target_pairs={{0,12},{4,0},{8,4},{12,8},{1,13},{5,1},{9,5},{13,9},{2,14},{6,2},{... | collective-permute-start | bytes 786440 | tf_op jit(solution)/shard_map/ppermute | solution.py:266
  75.0 14.8 %collective-permute-start.20 = (bf16[8,128,128]{2,1,0:T(8,128)(2,1)S(1)}, bf16[8,128,128]{2,1,0:T(8,128)(2,1)S(1)}, u32[]{:S(2)}, u32[]{:S(2)}) collective-permute-start(bf16[8,128,128]{2,1,0:T(8,128)(2,1)S(1)} %get-tuple-element.35.refs_0_), channel_id=1, source_target_pairs={{0,16},{16,0},{1,17},{17,1},{2,18},{18,2},{3,19},{19,3},{4,20},{20... | collective-permute-start | bytes 786440 | tf_op jit(solution)/shard_map/ppermute | solution.py:266
  75.0 13.4 %collective-permute-start.19 = (s32[1,17]{1,0:T(1,128)S(1)}, s32[1,17]{1,0:T(1,128)S(1)}, u32[]{:S(2)}, u32[]{:S(2)}) collective-permute-start(s32[1,17]{1,0:T(1,128)S(1)} %pad_add_fusion.3), channel_id=1, source_target_pairs={{0,16},{16,0},{1,17},{17,1},{2,18},{18,2},{3,19},{19,3},{4,20},{20... | collective-permute-start | bytes 212 | tf_op jit(solution)/shard_map/ppermute | solution.py:266
  84.2 13.1 %collective-permute-start.16 = (bf16[4,128,128]{2,1,0:T(8,128)(2,1)S(1)}, bf16[4,128,128]{2,1,0:T(8,128)(2,1)S(1)}, u32[]{:S(2)}, u32[]{:S(2)}) collective-permute-start(bf16[4,128,128]{2,1,0:T(8,128)(2,1)S(1)} %get-tuple-element.32), channel_id=1, source_target_pairs={{0,1},{1,2},{2,3},{3,0},{4,5},{5,6},{6,7},{7,4},{8,9},{9,10},{10,1... | collective-permute-start | bytes 393224 | tf_op jit(solution)/shard_map/ppermute | solution.py:266
  84.2 15.2 %collective-permute-start.17 = (bf16[4,128,128]{2,1,0:T(8,128)(2,1)S(1)}, bf16[4,128,128]{2,1,0:T(8,128)(2,1)S(1)}, u32[]{:S(2)}, u32[]{:S(2)}) collective-permute-start(bf16[4,128,128]{2,1,0:T(8,128)(2,1)S(1)} %get-tuple-element.33), channel_id=1, source_target_pairs={{0,2},{1,3},{2,0},{3,1},{4,6},{5,7},{6,4},{7,5},{8,10},{9,11},{10,... | collective-permute-start | bytes 393224 | tf_op jit(solution)/shard_map/ppermute | solution.py:266
  88.4 11.1 %collective-permute-start.18 = (bf16[4,128,128]{2,1,0:T(8,128)(2,1)S(1)}, bf16[4,128,128]{2,1,0:T(8,128)(2,1)S(1)}, u32[]{:S(2)}, u32[]{:S(2)}) collective-permute-start(bf16[4,128,128]{2,1,0:T(8,128)(2,1)S(1)} %get-tuple-element.34), channel_id=1, source_target_pairs={{0,3},{1,0},{2,1},{3,2},{4,7},{5,4},{6,5},{7,6},{8,11},{9,8},{10,9... | collective-permute-start | bytes 393224 | tf_op jit(solution)/shard_map/ppermute | solution.py:266
  90.8 9.2 %collective-permute-start.21 = (bf16[4,128,128]{2,1,0:T(8,128)(2,1)S(1)}, bf16[4,128,128]{2,1,0:T(8,128)(2,1)S(1)}, u32[]{:S(2)}, u32[]{:S(2)}) collective-permute-start(bf16[4,128,128]{2,1,0:T(8,128)(2,1)S(1)} %get-tuple-element.37), channel_id=1, source_target_pairs={{0,32},{32,64},{64,96},{96,0},{1,33},{33,65},{65,97},{97,1},{2,34}... | collective-permute-start | bytes 393224 | tf_op jit(solution)/shard_map/ppermute | solution.py:266
  102.2 9.7 %collective-permute-start.24 = (f32[464,128]{1,0:T(8,128)S(1)}, f32[464,128]{1,0:T(8,128)S(1)}, u32[]{:S(2)}, u32[]{:S(2)}) collective-permute-start(f32[464,128]{1,0:T(8,128)S(1)} %fusion.1), channel_id=1, source_target_pairs={{0,16},{16,0},{1,17},{17,1},{2,18},{18,2},{3,19},{19,3},{4,20},{20... | collective-permute-start | bytes 712712 | tf_op jit(solution)/shard_map/ppermute | solution.py:266
  113.5 7.9 %collective-permute-start.26 = (bf16[480,128]{1,0:T(8,128)(2,1)S(1)}, bf16[480,128]{1,0:T(8,128)(2,1)S(1)}, u32[]{:S(2)}, u32[]{:S(2)}) collective-permute-start(bf16[480,128]{1,0:T(8,128)(2,1)S(1)} %pad_maximum_fusion.1), channel_id=1, source_target_pairs={{0,64},{32,96},{64,0},{96,32},{1,65},{33,97},{65,1},{97,33},{2,66}... | collective-permute-start | bytes 368648 | tf_op jit(solution)/shard_map/ppermute | solution.py:266
  124.9 7.6 %collective-permute-start.29 = (bf16[480,128]{1,0:T(8,128)(2,1)}, bf16[480,128]{1,0:T(8,128)(2,1)S(1)}, u32[]{:S(2)}, u32[]{:S(2)}) collective-permute-start(bf16[480,128]{1,0:T(8,128)(2,1)} %get-tuple-element.43), channel_id=1, source_target_pairs={{0,8},{4,12},{8,0},{12,4},{1,9},{5,13},{9,1},{13,5},{2,10},{6,14},... | collective-permute-start | bytes 368648 | tf_op jit(solution)/shard_map/ppermute | solution.py:266
  136.1 6.1 %collective-permute-start.32 = (bf16[480,128]{1,0:T(8,128)(2,1)}, bf16[480,128]{1,0:T(8,128)(2,1)S(1)}, u32[]{:S(2)}, u32[]{:S(2)}) collective-permute-start(bf16[480,128]{1,0:T(8,128)(2,1)} %get-tuple-element.45), channel_id=1, source_target_pairs={{0,2},{1,3},{2,0},{3,1},{4,6},{5,7},{6,4},{7,5},{8,10},{9,11},{10,... | collective-permute-start | bytes 368648 | tf_op jit(solution)/shard_map/ppermute | solution.py:266
  (25 other events, 288.2 us)

commit v4 on v3

--- a/solution.py
+++ b/solution.py
@@ -13,9 +13,9 @@
 
 
 def blocks_kernel(
-    place, count, bias, w_rows, w_wide, w_cols, left0, left1, left2, left3, right0, right1, teacher,
+    place, count, bias, w_turned, w_plain, left0, left1, left2, left3, right0, right1, teacher,
     left_grads, right_grads, bin_out, cross_out,
-    left_tiles, right_tiles, target, logit, left_turn, right_turn, left_sum, right_sum,
+    w_rows, w_wide, w_cols, left_tiles, right_tiles, target, logit, left_turn, right_turn, left_sum, right_sum,
     tile_sem, target_sem,
 ):
     left_from = (left0, left1, left2, left3)
@@ -52,6 +52,11 @@
                 right_copy(slot, n).start()
 
     target_copy(0).start()
+    for k in range(bins):
+        row = w_turned[k : k + 1, :]
+        w_wide[k] = jnp.broadcast_to(row, (8, width))
+        w_rows[k] = jnp.broadcast_to(row, (16, width)).astype(jnp.bfloat16)
+        w_cols[k] = jnp.broadcast_to(w_plain[:, k : k + 1], (width, tile)).astype(jnp.bfloat16)
     bin_out[...] = jnp.zeros(bin_out.shape, jnp.float32)
     cross_out[...] = jnp.zeros(cross_out.shape, jnp.float32)
 
@@ -147,10 +152,7 @@
 def run_blocks(place, count, bin_weight, bin_bias, left_from, right_from, teacher):
     slots, bins, tile, _ = teacher.shape
     width = bin_weight.shape[0]
-    turned = bin_weight.T
-    w_rows = jnp.broadcast_to(turned[:, None, :], (bins, 16, width))
-    w_wide = jnp.broadcast_to(turned[:, None, :].astype(jnp.float32), (bins, 8, width))
-    w_cols = jnp.broadcast_to(turned[:, :, None], (bins, width, tile))
+    wide = bin_weight.astype(jnp.float32)
     smem = pl.BlockSpec(memory_space=pltpu.SMEM)
     vmem = pl.BlockSpec(memory_space=pltpu.VMEM)
     hbm = pl.BlockSpec(memory_space=pl.ANY)
@@ -163,9 +165,12 @@
             jax.ShapeDtypeStruct((bins, 8, width), f32),
             jax.ShapeDtypeStruct((8, tile), f32),
         ],
-        in_specs=[smem] * 3 + [vmem] * 3 + [hbm] * 7,
+        in_specs=[smem] * 3 + [vmem] * 2 + [hbm] * 7,
         out_specs=[vmem] * 4,
         scratch_shapes=[
+            pltpu.VMEM((bins, 16, width), bf16),
+            pltpu.VMEM((bins, 8, width), f32),
+            pltpu.VMEM((bins, width, tile), bf16),
             pltpu.VMEM((slots, tile, width), bf16),
             pltpu.VMEM((slots, tile, width), bf16),
             pltpu.VMEM((2, bins, tile, tile), bf16),
@@ -181,7 +186,7 @@
         cost_estimate=pl.CostEstimate(
             flops=6 * 8 * 64 * 128**3, bytes_accessed=20 * 2**20, transcendentals=8 * 2**20
         ),
-    )(place, count, bin_bias, w_rows, w_wide, w_cols, *left_from, *right_from, teacher)
+    )(place, count, bin_bias, wide.T, wide, *left_from, *right_from, teacher)
 
 
 AXES = ("z", "core", "y", "x")
@@ -224,10 +229,11 @@
     )(info, here, *near)
 
 
-def fold_kernel(side, info, here, *refs):
-    sources, (own, far1, far2, far3, total) = refs[:-5], refs[-5:]
+def fold_kernel(side, count, info, here, *refs):
+    sources, rows = refs[:count], refs[count : count + 4]
+    own, far1, far2, far3, product, total = refs[count + 4 :]
     total[...] = jnp.zeros(total.shape, jnp.float32)
-    slots = sources[0].shape[0]
+    slots, tile, width = sources[0].shape
     for s, source in enumerate(sources):
         live = info[s, 2 * slots]
         for slot in range(slots):
@@ -244,21 +250,36 @@
     own[...] = total[pl.ds(0, 4)]
     for n, far in enumerate((far1, far2, far3)):
         far[...] = total[pl.ds(4 * n + 4, 4)].astype(jnp.bfloat16)
-
-
-def fold_slots(side, info, here, sources):
+    result = jnp.zeros(product.shape, jnp.float32)
+    for n in range(4):
+        value = total[pl.ds(4 * n, 4)].reshape(4 * tile, width)
+        high = value.astype(jnp.bfloat16)
+        low = (value - high.astype(jnp.float32)).astype(jnp.bfloat16)
+        for part in (high, low):
+            result = result + lax.dot_general(
+                rows[n][...],
+                part,
+                (((0,), (0,)), ((), ())),
+                preferred_element_type=jnp.float32,
+            )
+    product[...] = result
+
+
+def fold_slots(side, info, here, sources, rows):
     _, tile, width = sources[0].shape
     smem = pl.BlockSpec(memory_space=pltpu.SMEM)
     vmem = pl.BlockSpec(memory_space=pltpu.VMEM)
     far = jax.ShapeDtypeStruct((4, tile, width), jnp.bfloat16)
     return pl.pallas_call(
-        functools.partial(fold_kernel, side),
-        out_shape=[jax.ShapeDtypeStruct((4, tile, width), jnp.float32)] + [far] * 3,
-        in_specs=[smem] * 2 + [vmem] * len(sources),
-        out_specs=[vmem] * 4,
+        functools.partial(fold_kernel, side, len(sources)),
+        out_shape=[jax.ShapeDtypeStruct((4, tile, width), jnp.float32)]
+        + [far] * 3
+        + [jax.ShapeDtypeStruct((rows[0].shape[1], width), jnp.float32)],
+        in_specs=[smem] * 2 + [vmem] * (len(sources) + 4),
+        out_specs=[vmem] * 5,
         scratch_shapes=[pltpu.VMEM((16, tile, width), jnp.float32)],
-        compiler_params=pltpu.CompilerParams(vmem_limit_bytes=16 * 1024 * 1024),
-    )(info, here, *sources)
+        compiler_params=pltpu.CompilerParams(vmem_limit_bytes=24 * 1024 * 1024),
+    )(info, here, *sources, *rows)
 
 
 def shift(value, axis, step):
@@ -270,41 +291,48 @@
     return [shift(value, axis, s) for s in range(1, lax.axis_size(axis))]
 
 
-SCALARS = 16
-
-
-def split_rows(value):
-    body, tail = value[:-SCALARS], value[-SCALARS:]
-    high = tail.astype(jnp.bfloat16)
-    low = (tail - high.astype(jnp.float32)).astype(jnp.bfloat16)
-    return jnp.concatenate([body.astype(jnp.bfloat16), high, low])
-
-
-def join_rows(sent):
-    sent = sent.astype(jnp.float32)
-    body, high, low = sent[: -2 * SCALARS], sent[-2 * SCALARS : -SCALARS], sent[-SCALARS:]
-    return jnp.concatenate([body, high + low])
-
-
-def add_kernel(value, sent1, sent2, sent3, out, send):
-    total = value[...]
-    for sent in (sent1, sent2, sent3):
-        total = total + join_rows(sent[...])
-    out[...] = total
-    send[...] = split_rows(total)
-
-
-def add_sent(value, sent):
+def after(value, *others):
+    return lax.optimization_barrier((value,) + others)[0]
+
+
+def cut_kernel(here, one, two, own, far1, far2, far3):
+    rows = own.shape[0]
+    for n, out in enumerate((own, far1, far2, far3)):
+        spot = pl.ds(pl.multiple_of(lax.rem(here[0] + n, 4) * rows, 8), rows)
+        out[...] = one[spot, :] + two[spot, :]
+
+
+def paste_kernel(here, part0, part1, part2, part3, out):
+    rows = part0.shape[0]
+    for n, part in enumerate((part0, part1, part2, part3)):
+        spot = pl.ds(pl.multiple_of(lax.rem(here[0] - n + 4, 4) * rows, 8), rows)
+        out[spot, :] = part[...]
+
+
+def small_call(kernel, here, values, outs):
+    smem = pl.BlockSpec(memory_space=pltpu.SMEM)
     vmem = pl.BlockSpec(memory_space=pltpu.VMEM)
     return pl.pallas_call(
-        add_kernel,
-        out_shape=[
-            jax.ShapeDtypeStruct(value.shape, jnp.float32),
-            jax.ShapeDtypeStruct(sent[0].shape, jnp.bfloat16),
-        ],
-        in_specs=[vmem] * 4,
-        out_specs=[vmem] * 2,
-    )(value, *sent)
+        kernel,
+        out_shape=[jax.ShapeDtypeStruct(shape, jnp.float32) for shape in outs],
+        in_specs=[smem] + [vmem] * len(values),
+        out_specs=[vmem] * len(outs),
+    )(here, *values)
+
+
+def sum_everywhere(here, mine, other, in_z_step, in_y_step):
+    rows, width = mine.shape
+    part = (rows // 4, width)
+    own, *far = small_call(cut_kernel, here, [mine, shift(other, "core", 1)], [part] * 4)
+    in_z_step = after(in_z_step, own)
+    for s in (1, 2, 3):
+        own = own + shift(far[s - 1], "z", s)
+    in_y_step = after(in_y_step, own)
+    for axis in ("y", "x"):
+        sent = ring(own, axis)
+        own = own + sent[0] + sent[1] + sent[2]
+    total = small_call(paste_kernel, here, [own] + ring(own, "z"), [(rows, width)])[0]
+    return total, in_z_step, in_y_step
 
 
 def per_device(
@@ -316,12 +344,10 @@
     left_wide = left_weight.astype(jnp.float32)
     right_wide = right_weight.astype(jnp.float32)
     info = jnp.concatenate([own_tiles.reshape(1, -1), block_count[None]], axis=1)
-    info_y = jnp.concatenate([info] + ring(info, "y"))
-    info_core = jnp.concatenate([info] + ring(info, "core"))
     left_local = jnp.dot(single, left_weight, preferred_element_type=jnp.float32).astype(
         jnp.bfloat16
     )
-    right_local = jnp.dot(single, right_weight, preferred_element_type=jnp.float32).astype(
+    right_local = jnp.dot(after(single, left_local), right_weight, preferred_element_type=jnp.float32).astype(
         jnp.bfloat16
     )
     rows_dev, width = left_local.shape
@@ -329,10 +355,21 @@
     right_local = right_local.reshape(-1, tile, width)
     here = jnp.stack([lax.axis_index(a) for a in AXES]).astype(jnp.int32)
     z, core, y = here[0], here[1], here[2]
-    picked = pick_tiles(info_y, here, [left_local] + ring(left_local, "x"))
+    left_near = [left_local] + ring(left_local, "x")
+    right_ring = ring(right_local, "z")
+    left_near = after(left_near, *right_ring)
+    info_first = after(info, right_local)
+    info_y = jnp.concatenate([info_first] + ring(info_first, "y"))
+    picked = pick_tiles(info_y, here, left_near)
     left_from = [picked[0]] + [shift(picked[s], "y", s) for s in (1, 2, 3)]
-    right_near = jnp.concatenate([right_local] + ring(right_local, "z"))
+    right_near = jnp.concatenate([right_local] + right_ring)
     right_from = [right_near, shift(right_near, "core", 1)]
+    near_x = shift(after(single, right_from[1]), "x", 3)
+    left_from[0] = after(picked[0], near_x)
+    single_x = after(single, near_x)
+    single_z = after(single, right_near)
+    rows_x = [single, near_x] + [shift(single_x, "x", 4 - s) for s in (2, 3)]
+    rows_z = [single] + [shift(single_z, "z", 4 - s) for s in (1, 2, 3)]
     row, col = own_tiles[:, 0], own_tiles[:, 1]
     place = jnp.stack(
         [
@@ -345,9 +382,31 @@
     left_slots, right_slots, bins_part, cross_part = run_blocks(
         place, block_count, bin_weight, bin_bias, left_from, right_from, teacher[0]
     )
-    left_own, *left_far = fold_slots(0, info_y, here, [left_slots] + ring(left_slots, "y"))
-    right_own, *right_far = fold_slots(
-        1, info_core, here, [right_slots] + ring(right_slots, "core")
+    left_slots, right_slots = after((left_slots, right_slots), *rows_x, *rows_z)
+    left_ring = ring(left_slots, "y")
+    right_slots = after(right_slots, left_ring[0])
+    info_last = after(info, right_slots)
+    info_core = jnp.concatenate([info_last] + ring(info_last, "core"))
+    right_own, *right_far, part_right = fold_slots(
+        1, info_core, here, [right_slots] + ring(right_slots, "core"), rows_z
+    )
+    left_own, *left_far, part_left = fold_slots(
+        0, info_y, here, [left_slots] + left_ring, rows_x
+    )
+    depth = part_left.shape[0]
+    scalars = jnp.stack([jnp.sum(cross_part), block_count[0].astype(jnp.float32)])
+    part_bin = jnp.sum(bins_part, axis=1)
+    first = jnp.concatenate([part_left, part_bin])
+    second = jnp.concatenate(
+        [part_right, jnp.pad(scalars[None], ((0, bins - 1), (0, width - 2)))]
+    )
+    low_core = core == 0
+    total, left_far, right_far = sum_everywhere(
+        here,
+        jnp.where(low_core, first, second),
+        jnp.where(low_core, second, first),
+        left_far,
+        right_far,
     )
     left_rows_grad, right_rows_grad = left_own, right_own
     for s in (1, 2, 3):
@@ -355,22 +414,6 @@
         right_rows_grad = right_rows_grad + shift(right_far[s - 1], "z", s).astype(jnp.float32)
     left_rows_grad = left_rows_grad.reshape(rows_dev, width)
     right_rows_grad = right_rows_grad.reshape(rows_dev, width)
-    single_wide = single.astype(jnp.float32)
-    part_left = jnp.dot(single_wide.T, left_rows_grad, precision=lax.Precision.HIGHEST)
-    part_right = jnp.dot(single_wide.T, right_rows_grad, precision=lax.Precision.HIGHEST)
-    depth = part_left.shape[0]
-    scalars = jnp.stack([jnp.sum(cross_part), block_count[0].astype(jnp.float32)])
-    scalars = jnp.pad(scalars[None], ((0, SCALARS - 1), (0, width - 2)))
-    part_bin = jnp.sum(bins_part, axis=1)
-    first = jnp.concatenate([part_left, part_bin, jnp.zeros_like(scalars)])
-    second = jnp.concatenate([part_right, jnp.zeros_like(part_bin), scalars])
-    low_core = core == 0
-    total = jnp.where(low_core, first, second) + shift(
-        jnp.where(low_core, second, first), "core", 1
-    )
-    send = split_rows(total)
-    for axis in ("z", "y", "x"):
-        total, send = add_sent(total, ring(send, axis))
     other = shift(total, "core", 1)
     first = jnp.where(low_core, total, other)
     second = jnp.where(low_core, other, total)
@@ -381,7 +424,7 @@
     grad_left = first[:depth] / devices
     grad_right = second[:depth] / devices
     grad_bin = first[depth : depth + bins].T / devices
-    loss_value = second[depth + bins, 0] / (second[depth + bins, 1] * (tile * tile))
+    loss_value = second[depth, 0] / (second[depth, 1] * (tile * tile))
     return (grad_single, grad_left, grad_right, grad_bin, loss_value)
 
 

time: 157 us -> 162 us (1.032); the launches traced: 155 us -> 162 us
  local copies, waits for them, and re-layouts: 8.47 us -> 14.7 us
  waiting for transfers between devices: 33.5 us -> 30.3 us
  other arithmetic: 5.48 us -> 7.43 us
    unnamed x31 -> x50, local copies, waits for them, and re-layouts: 4.19 us -> 13.2 us
    ppermute x35 -> x44, waiting for transfers between devices: 33.5 us -> 30.3 us  [shift(): lax.ppermute(value, axis, [(i, (i + step) % size) for i in range(size)])]
    broadcast_in_dim x5 -> x0, local copies, waits for them, and re-layouts: 2.75 us -> none  [the longest x1 1.94 us: run_blocks(): w_cols = jnp.broadcast_to(turned[:, :, None], (bins, width, tile))]
    ppermute x35 -> x44, starting transfers between devices: 75 us -> 76.5 us  [shift(): lax.ppermute(value, axis, [(i, (i + step) % size) for i in range(size)])]
    pallas_call x5 -> x4, Pallas kernels: 8.08 us -> 8.58 us  [the longest x2 5.16 us: fold_slots(): pl.pallas_call(functools.partial(fold_kernel, side, len(sources)), out_sh...]
  transfers between devices with their start and end apart: 35 -> 44, of which waited for: 19 -> 23; matrix products, arithmetic and copies ran while one was open for 5% -> 6% of each run, Pallas kernels for 2% -> 12%
where the time goes in v4:
time: 162 us
  starting transfers between devices  76.5 us (47%)
  waiting for transfers between devices  30.3 us (19%)
  Pallas kernels  25 us (15%)
  local copies, waits for them, and re-layouts  14.7 us (9%)
  other arithmetic  7.43 us (5%)
  matrix products  4.31 us (3%)
  between operations  3.99 us (2%)
    ppermute x44, starting transfers between devices, shift(): lax.ppermute(value, axis, [(i, (i + step) % size) for i in range(size)])  76.5 us
    ppermute x44, waiting for transfers between devices, shift(): lax.ppermute(value, axis, [(i, (i + step) % size) for i in range(size)])  30.3 us
    pallas_call x1, Pallas kernels, run_blocks(): pl.pallas_call(blocks_kernel, out_shape=[piece] * 2 + [jax.ShapeDtypeStru...  15.5 us
    unnamed x50, local copies, waits for them, and re-layouts  13.2 us
    pallas_call x2, Pallas kernels, fold_slots(): pl.pallas_call(functools.partial(fold_kernel, side, len(sources)), out_sh...  5.16 us
    pallas_call x2, Pallas kernels, small_call(): pl.pallas_call(kernel, out_shape=[jax.ShapeDtypeStruct(shape, jnp.float32...  3.41 us
  transfers between devices with their start and end apart: 44, of which 23 were waited for; matrix products, arithmetic and copies ran while one was open for 6% of the time, Pallas kernels for 12%

profile of v4, /device:TPU:1, one launch (start us, length us, event | category | flops | bytes accessed | tf_op | source)
XLA Modules:
  0.0 162.2 jit_solution(10497645759237200666)
XLA Ops:
  2.0 2.1 %collective-permute-start.3 = (bf16[4,128,128]{2,1,0:T(8,128)(2,1)S(1)}, bf16[4,128,128]{2,1,0:T(8,128)(2,1)S(1)}, u32[]{:S(2)}, u32[]{:S(2)}) collective-permute-start(bf16[4,128,128]{2,1,0:T(8,128)(2,1)S(1)} %bitcast.28), channel_id=1, source_target_pairs={{0,1},{1,2},{2,3},{3,0},{4,5},{5,6},{6,7},{7,4},{8,9},{9,10},{10,1... | collective-permute-start | bytes 393224 | tf_op jit(solution)/shard_map/ppermute | solution.py:287
  4.1 2.5 %collective-permute-start.4 = (bf16[4,128,128]{2,1,0:T(8,128)(2,1)S(1)}, bf16[4,128,128]{2,1,0:T(8,128)(2,1)S(1)}, u32[]{:S(2)}, u32[]{:S(2)}) collective-permute-start(bf16[4,128,128]{2,1,0:T(8,128)(2,1)S(1)} %bitcast.29), channel_id=1, source_target_pairs={{0,2},{1,3},{2,0},{3,1},{4,6},{5,7},{6,4},{7,5},{8,10},{9,11},{10,... | collective-permute-start | bytes 393224 | tf_op jit(solution)/shard_map/ppermute | solution.py:287
  7.8 1.7 %collective-permute-start.6 = (bf16[4,128,128]{2,1,0:T(8,128)(2,1)S(1)}, bf16[4,128,128]{2,1,0:T(8,128)(2,1)S(1)}, u32[]{:S(2)}, u32[]{:S(2)}) collective-permute-start(bf16[4,128,128]{2,1,0:T(8,128)(2,1)S(1)} %bitcast.34), channel_id=1, source_target_pairs={{0,32},{32,64},{64,96},{96,0},{1,33},{33,65},{65,97},{97,1},{2,34}... | collective-permute-start | bytes 393224 | tf_op jit(solution)/shard_map/ppermute | solution.py:287
  9.5 3.3 %collective-permute-start.7 = (bf16[4,128,128]{2,1,0:T(8,128)(2,1)S(1)}, bf16[4,128,128]{2,1,0:T(8,128)(2,1)S(1)}, u32[]{:S(2)}, u32[]{:S(2)}) collective-permute-start(bf16[4,128,128]{2,1,0:T(8,128)(2,1)S(1)} %bitcast.35), channel_id=1, source_target_pairs={{0,64},{32,96},{64,0},{96,32},{1,65},{33,97},{65,1},{97,33},{2,66}... | collective-permute-start | bytes 393224 | tf_op jit(solution)/shard_map/ppermute | solution.py:287
  18.0 2.7 %collective-permute-start.2 = (s32[1,17]{1,0:T(1,128)S(1)}, s32[1,17]{1,0:T(1,128)S(1)}, u32[]{:S(2)}, u32[]{:S(2)}) collective-permute-start(s32[1,17]{1,0:T(1,128)S(1)} %pad_add_fusion.3), channel_id=1, source_target_pairs={{0,12},{4,0},{8,4},{12,8},{1,13},{5,1},{9,5},{13,9},{2,14},{6,2},{... | collective-permute-start | bytes 212 | tf_op jit(solution)/shard_map/ppermute | solution.py:287
  20.8 2.7 %collective-permute-start.9 = (bf16[16,128,128]{2,1,0:T(8,128)(2,1)S(1)}, bf16[16,128,128]{2,1,0:T(8,128)(2,1)S(1)}, u32[]{:S(2)}, u32[]{:S(2)}) collective-permute-start(bf16[16,128,128]{2,1,0:T(8,128)(2,1)S(1)} %pad_maximum_fusion.right0), channel_id=1, source_target_pairs={{0,16},{16,0},{1,17},{17,1},{2,18},{18,2},{3,19},{19,3},{4,20},{20... | collective-permute-start | bytes 1572872 | tf_op jit(solution)/shard_map/ppermute | solution.py:287
  26.1 2.9 %collective-permute-done.1 = s32[1,17]{1,0:T(1,128)S(1)} collective-permute-done((s32[1,17]{1,0:T(1,128)S(1)}, s32[1,17]{1,0:T(1,128)S(1)}, u32[]{:S(2)}, u32[]{:S(2)}) %collective-permute-start.1) | collective-permute-done | bytes 100 | tf_op jit(solution)/shard_map/ppermute | solution.py:287
  30.9 1.6 %collective-permute-start.12 = (bf16[8,128,128]{2,1,0:T(8,128)(2,1)S(1)}, bf16[8,128,128]{2,1,0:T(8,128)(2,1)S(1)}, u32[]{:S(2)}, u32[]{:S(2)}) collective-permute-start(bf16[8,128,128]{2,1,0:T(8,128)(2,1)S(1)} %get-tuple-element.57), channel_id=1, source_target_pairs={{0,8},{4,12},{8,0},{12,4},{1,9},{5,13},{9,1},{13,5},{2,10},{6,14},... | collective-permute-start | bytes 786440 | tf_op jit(solution)/shard_map/ppermute | solution.py:287
  34.9 3.3 %collective-permute-done.10.refs_5_ = bf16[512,384]{1,0:T(8,128)(2,1)S(1)} collective-permute-done((bf16[512,384]{1,0:T(8,128)(2,1)}, bf16[512,384]{1,0:T(8,128)(2,1)S(1)}, u32[]{:S(2)}, u32[]{:S(2)}) %collective-permute-start.10) | collective-permute-done | bytes 393248 | tf_op jit(solution)/shard_map/ppermute | solution.py:287
  39.1 3.6 %collective-permute-done.12.left2 = bf16[8,128,128]{2,1,0:T(8,128)(2,1)S(1)} collective-permute-done((bf16[8,128,128]{2,1,0:T(8,128)(2,1)S(1)}, bf16[8,128,128]{2,1,0:T(8,128)(2,1)S(1)}, u32[]{:S(2)}, u32[]{:S(2)}) %collective-permute-start.12) | collective-permute-done | bytes 262176 | tf_op jit(solution)/shard_map/ppermute | solution.py:287
  47.9 15.5 %shard_map.120 = (bf16[8,128,128]{2,1,0:T(8,128)(2,1)}, bf16[8,128,128]{2,1,0:T(8,128)(2,1)}, f32[64,8,128]{2,1,0:T(8,128)S(1)}, f32[8,128]{1,0:T(8,128)S(1)}) custom-call(s32[8,3]{1,0:T(8,128)S(1)} %pad_add_fusion.place, s32[1]{0:T(128)} %copy.25.count, f32[64]{0:T(128)S(1)} %copy-done.16, f32[64,128]{1,0:T(8,128)S(1)} %copy.22.w_turned, ...), custom_call_target="tpu_custom_call" | custom-call | flops 6442450944 | bytes 20971520 | tf_op jit(solution)/shard_map/pallas_call | solution.py:161
  64.3 5.1 %collective-permute-start.20 = (bf16[8,128,128]{2,1,0:T(8,128)(2,1)}, bf16[8,128,128]{2,1,0:T(8,128)(2,1)S(1)}, u32[]{:S(2)}, u32[]{:S(2)}) collective-permute-start(bf16[8,128,128]{2,1,0:T(8,128)(2,1)} %get-tuple-element.63.refs_0_), channel_id=1, source_target_pairs={{0,8},{4,12},{8,0},{12,4},{1,9},{5,13},{9,1},{13,5},{2,10},{6,14},... | collective-permute-start | bytes 786440 | tf_op jit(solution)/shard_map/ppermute | solution.py:287
  69.3 2.0 %collective-permute-start.21 = (bf16[8,128,128]{2,1,0:T(8,128)(2,1)}, bf16[8,128,128]{2,1,0:T(8,128)(2,1)}, u32[]{:S(2)}, u32[]{:S(2)}) collective-permute-start(bf16[8,128,128]{2,1,0:T(8,128)(2,1)} %get-tuple-element.63.refs_0_), channel_id=1, source_target_pairs={{0,12},{4,0},{8,4},{12,8},{1,13},{5,1},{9,5},{13,9},{2,14},{6,2},{... | collective-permute-start | bytes 786440 | tf_op jit(solution)/shard_map/ppermute | solution.py:287
  71.3 2.2 %collective-permute-done.19.refs_1_ = bf16[8,128,128]{2,1,0:T(8,128)(2,1)S(1)} collective-permute-done((bf16[8,128,128]{2,1,0:T(8,128)(2,1)}, bf16[8,128,128]{2,1,0:T(8,128)(2,1)S(1)}, u32[]{:S(2)}, u32[]{:S(2)}) %collective-permute-start.19) | collective-permute-done | bytes 262176 | tf_op jit(solution)/shard_map/ppermute | solution.py:287
  74.3 13.7 %collective-permute-start.23 = (bf16[8,128,128]{2,1,0:T(8,128)(2,1)}, bf16[8,128,128]{2,1,0:T(8,128)(2,1)S(1)}, u32[]{:S(2)}, u32[]{:S(2)}) collective-permute-start(bf16[8,128,128]{2,1,0:T(8,128)(2,1)} %get-tuple-element.71.refs_0_), channel_id=1, source_target_pairs={{0,16},{16,0},{1,17},{17,1},{2,18},{18,2},{3,19},{19,3},{4,20},{20... | collective-permute-start | bytes 786440 | tf_op jit(solution)/shard_map/ppermute | solution.py:287
  93.0 2.8 %shard_map.121 = (f32[4,128,128]{2,1,0:T(8,128)S(1)}, bf16[4,128,128]{2,1,0:T(8,128)(2,1)S(1)}, bf16[4,128,128]{2,1,0:T(8,128)(2,1)S(1)}, bf16[4,128,128]{2,1,0:T(8,128)(2,1)S(1)}, f32[384,128]{1,0:T(8,128)S(1)}) custom-call(s32[4,17]{1,0:T(4,128)S(1)} %pad_add_fusion.1.info, s32[4]{0:T(128)S(1)} %pad_add_fusion.4.here, ...), custom_call_target="tpu_custom_call" | custom-call | tf_op jit(solution)/shard_map/pallas_call | solution.py:273
  99.4 2.4 %shard_map.122 = (f32[4,128,128]{2,1,0:T(8,128)S(1)}, bf16[4,128,128]{2,1,0:T(8,128)(2,1)S(1)}, bf16[4,128,128]{2,1,0:T(8,128)(2,1)S(1)}, bf16[4,128,128]{2,1,0:T(8,128)(2,1)S(1)}, f32[384,128]{1,0:T(8,128)S(1)}) custom-call(s32[2,17]{1,0:T(2,128)S(1)} %pad_add_fusion.2.info, s32[4]{0:T(128)S(1)} %pad_add_fusion.4.here, ...), custom_call_target="tpu_custom_call" | custom-call | tf_op jit(solution)/shard_map/pallas_call | solution.py:273
  102.5 1.7 %collective-permute-start.24 = (f32[448,128]{1,0:T(8,128)S(1)}, f32[448,128]{1,0:T(8,128)S(1)}, u32[]{:S(2)}, u32[]{:S(2)}) collective-permute-start(f32[448,128]{1,0:T(8,128)S(1)} %get-tuple-element.91), channel_id=1, source_target_pairs={{0,16},{16,0},{1,17},{17,1},{2,18},{18,2},{3,19},{19,3},{4,20},{20... | collective-permute-start | bytes 688136 | tf_op jit(solution)/shard_map/ppermute | solution.py:287
  106.0 1.8 %shard_map.123 = (f32[112,128]{1,0:T(8,128)}, f32[112,128]{1,0:T(8,128)}, f32[112,128]{1,0:T(8,128)}, f32[112,128]{1,0:T(8,128)}) custom-call(s32[4]{0:T(128)} %copy-done.10, f32[448,128]{1,0:T(8,128)} %get-tuple-element.92.one, f32[448,128]{1,0:T(8,128)} %copy-done.18), custom_call_target="tpu_custom_call" | custom-call | tf_op jit(solution)/shard_map/pallas_call | solution.py:315
  107.8 13.3 %collective-permute-start.30 = (f32[112,128]{1,0:T(8,128)}, f32[112,128]{1,0:T(8,128)S(1)}, u32[]{:S(2)}, u32[]{:S(2)}) collective-permute-start(f32[112,128]{1,0:T(8,128)} %get-tuple-element.85), channel_id=1, source_target_pairs={{0,96},{32,0},{64,32},{96,64},{1,97},{33,1},{65,33},{97,65},{2,98}... | collective-permute-start | bytes 172040 | tf_op jit(solution)/shard_map/ppermute | solution.py:287
  123.2 2.7 %collective-permute-done.29 = f32[112,128]{1,0:T(8,128)S(1)} collective-permute-done((f32[112,128]{1,0:T(8,128)}, f32[112,128]{1,0:T(8,128)S(1)}, u32[]{:S(2)}, u32[]{:S(2)}) %collective-permute-start.29) | collective-permute-done | bytes 57376 | tf_op jit(solution)/shard_map/ppermute | solution.py:287
  138.1 1.8 %collective-permute-done.38 = f32[112,128]{1,0:T(8,128)S(1)} collective-permute-done((f32[112,128]{1,0:T(8,128)S(1)}, f32[112,128]{1,0:T(8,128)S(1)}, u32[]{:S(2)}, u32[]{:S(2)}) %collective-permute-start.38) | collective-permute-done | bytes 57376 | tf_op jit(solution)/shard_map/ppermute | solution.py:287
  141.2 2.7 %collective-permute-start.41 = (f32[112,128]{1,0:T(8,128)S(1)}, f32[112,128]{1,0:T(8,128)S(1)}, u32[]{:S(2)}, u32[]{:S(2)}) collective-permute-start(f32[112,128]{1,0:T(8,128)S(1)} %add_add_fusion.part0), channel_id=1, source_target_pairs={{0,64},{32,96},{64,0},{96,32},{1,65},{33,97},{65,1},{97,33},{2,66}... | collective-permute-start | bytes 172040 | tf_op jit(solution)/shard_map/ppermute | solution.py:287
  149.5 6.1 %collective-permute-start.43 = (f32[448,128]{1,0:T(8,128)}, f32[448,128]{1,0:T(8,128)S(1)}, u32[]{:S(2)}, u32[]{:S(2)}) collective-permute-start(f32[448,128]{1,0:T(8,128)} %shard_map.124), channel_id=1, source_target_pairs={{0,16},{16,0},{1,17},{17,1},{2,18},{18,2},{3,19},{19,3},{4,20},{20... | collective-permute-start | bytes 688136 | tf_op jit(solution)/shard_map/ppermute | solution.py:287
  (149 shorter events, 58.1 us)
Async XLA Ops:
  2.0 27.9 %collective-permute-start.3 = (bf16[4,128,128]{2,1,0:T(8,128)(2,1)S(1)}, bf16[4,128,128]{2,1,0:T(8,128)(2,1)S(1)}, u32[]{:S(2)}, u32[]{:S(2)}) collective-permute-start(bf16[4,128,128]{2,1,0:T(8,128)(2,1)S(1)} %bitcast.28), channel_id=1, source_target_pairs={{0,1},{1,2},{2,3},{3,0},{4,5},{5,6},{6,7},{7,4},{8,9},{9,10},{10,1... | collective-permute-start | bytes 393224 | tf_op jit(solution)/shard_map/ppermute | solution.py:287
  4.1 25.8 %collective-permute-start.4 = (bf16[4,128,128]{2,1,0:T(8,128)(2,1)S(1)}, bf16[4,128,128]{2,1,0:T(8,128)(2,1)S(1)}, u32[]{:S(2)}, u32[]{:S(2)}) collective-permute-start(bf16[4,128,128]{2,1,0:T(8,128)(2,1)S(1)} %bitcast.29), channel_id=1, source_target_pairs={{0,2},{1,3},{2,0},{3,1},{4,6},{5,7},{6,4},{7,5},{8,10},{9,11},{10,... | collective-permute-start | bytes 393224 | tf_op jit(solution)/shard_map/ppermute | solution.py:287
  7.8 9.0 %collective-permute-start.6 = (bf16[4,128,128]{2,1,0:T(8,128)(2,1)S(1)}, bf16[4,128,128]{2,1,0:T(8,128)(2,1)S(1)}, u32[]{:S(2)}, u32[]{:S(2)}) collective-permute-start(bf16[4,128,128]{2,1,0:T(8,128)(2,1)S(1)} %bitcast.34), channel_id=1, source_target_pairs={{0,32},{32,64},{64,96},{96,0},{1,33},{33,65},{65,97},{97,1},{2,34}... | collective-permute-start | bytes 393224 | tf_op jit(solution)/shard_map/ppermute | solution.py:287
  9.5 8.4 %collective-permute-start.7 = (bf16[4,128,128]{2,1,0:T(8,128)(2,1)S(1)}, bf16[4,128,128]{2,1,0:T(8,128)(2,1)S(1)}, u32[]{:S(2)}, u32[]{:S(2)}) collective-permute-start(bf16[4,128,128]{2,1,0:T(8,128)(2,1)S(1)} %bitcast.35), channel_id=1, source_target_pairs={{0,64},{32,96},{64,0},{96,32},{1,65},{33,97},{65,1},{97,33},{2,66}... | collective-permute-start | bytes 393224 | tf_op jit(solution)/shard_map/ppermute | solution.py:287
  12.8 7.9 %collective-permute-start.8 = (bf16[4,128,128]{2,1,0:T(8,128)(2,1)S(1)}, bf16[4,128,128]{2,1,0:T(8,128)(2,1)S(1)}, u32[]{:S(2)}, u32[]{:S(2)}) collective-permute-start(bf16[4,128,128]{2,1,0:T(8,128)(2,1)S(1)} %bitcast.36), channel_id=1, source_target_pairs={{0,96},{32,0},{64,32},{96,64},{1,97},{33,1},{65,33},{97,65},{2,98}... | collective-permute-start | bytes 393224 | tf_op jit(solution)/shard_map/ppermute | solution.py:287
  16.8 13.1 %collective-permute-start.5 = (bf16[4,128,128]{2,1,0:T(8,128)(2,1)S(1)}, bf16[4,128,128]{2,1,0:T(8,128)(2,1)S(1)}, u32[]{:S(2)}, u32[]{:S(2)}) collective-permute-start(bf16[4,128,128]{2,1,0:T(8,128)(2,1)S(1)} %bitcast.30), channel_id=1, source_target_pairs={{0,3},{1,0},{2,1},{3,2},{4,7},{5,4},{6,5},{7,6},{8,11},{9,8},{10,9... | collective-permute-start | bytes 393224 | tf_op jit(solution)/shard_map/ppermute | solution.py:287
  18.0 7.4 %collective-permute-start.2 = (s32[1,17]{1,0:T(1,128)S(1)}, s32[1,17]{1,0:T(1,128)S(1)}, u32[]{:S(2)}, u32[]{:S(2)}) collective-permute-start(s32[1,17]{1,0:T(1,128)S(1)} %pad_add_fusion.3), channel_id=1, source_target_pairs={{0,12},{4,0},{8,4},{12,8},{1,13},{5,1},{9,5},{13,9},{2,14},{6,2},{... | collective-permute-start | bytes 212 | tf_op jit(solution)/shard_map/ppermute | solution.py:287
  28.9 9.3 %collective-permute-start.10 = (bf16[512,384]{1,0:T(8,128)(2,1)}, bf16[512,384]{1,0:T(8,128)(2,1)S(1)}, u32[]{:S(2)}, u32[]{:S(2)}) collective-permute-start(bf16[512,384]{1,0:T(8,128)(2,1)} %refs_2_.1), channel_id=1, source_target_pairs={{0,3},{1,0},{2,1},{3,2},{4,7},{5,4},{6,5},{7,6},{8,11},{9,8},{10,9... | collective-permute-start | bytes 1179656 | tf_op jit(solution)/shard_map/ppermute | solution.py:287
  30.8 8.3 %collective-permute-start.11 = (bf16[8,128,128]{2,1,0:T(8,128)(2,1)S(1)}, bf16[8,128,128]{2,1,0:T(8,128)(2,1)S(1)}, u32[]{:S(2)}, u32[]{:S(2)}) collective-permute-start(bf16[8,128,128]{2,1,0:T(8,128)(2,1)S(1)} %get-tuple-element.56), channel_id=1, source_target_pairs={{0,4},{4,8},{8,12},{12,0},{1,5},{5,9},{9,13},{13,1},{2,6},{6,10},{... | collective-permute-start | bytes 786440 | tf_op jit(solution)/shard_map/ppermute | solution.py:287
  30.9 11.8 %collective-permute-start.12 = (bf16[8,128,128]{2,1,0:T(8,128)(2,1)S(1)}, bf16[8,128,128]{2,1,0:T(8,128)(2,1)S(1)}, u32[]{:S(2)}, u32[]{:S(2)}) collective-permute-start(bf16[8,128,128]{2,1,0:T(8,128)(2,1)S(1)} %get-tuple-element.57), channel_id=1, source_target_pairs={{0,8},{4,12},{8,0},{12,4},{1,9},{5,13},{9,1},{13,5},{2,10},{6,14},... | collective-permute-start | bytes 786440 | tf_op jit(solution)/shard_map/ppermute | solution.py:287
  32.5 12.3 %collective-permute-start.13 = (bf16[8,128,128]{2,1,0:T(8,128)(2,1)S(1)}, bf16[8,128,128]{2,1,0:T(8,128)(2,1)S(1)}, u32[]{:S(2)}, u32[]{:S(2)}) collective-permute-start(bf16[8,128,128]{2,1,0:T(8,128)(2,1)S(1)} %get-tuple-element.58), channel_id=1, source_target_pairs={{0,12},{4,0},{8,4},{12,8},{1,13},{5,1},{9,5},{13,9},{2,14},{6,2},{... | collective-permute-start | bytes 786440 | tf_op jit(solution)/shard_map/ppermute | solution.py:287
  33.6 30.5 %collective-permute-start.16 = (bf16[512,384]{1,0:T(8,128)(2,1)}, bf16[512,384]{1,0:T(8,128)(2,1)S(1)}, u32[]{:S(2)}, u32[]{:S(2)}) collective-permute-start(bf16[512,384]{1,0:T(8,128)(2,1)} %refs_2_.1), channel_id=1, source_target_pairs={{0,96},{32,0},{64,32},{96,64},{1,97},{33,1},{65,33},{97,65},{2,98}... | collective-permute-start | bytes 1179656 | tf_op jit(solution)/shard_map/ppermute | solution.py:287
  38.2 25.9 %collective-permute-start.17 = (bf16[512,384]{1,0:T(8,128)(2,1)}, bf16[512,384]{1,0:T(8,128)(2,1)S(1)}, u32[]{:S(2)}, u32[]{:S(2)}) collective-permute-start(bf16[512,384]{1,0:T(8,128)(2,1)} %refs_2_.1), channel_id=1, source_target_pairs={{0,64},{32,96},{64,0},{96,32},{1,65},{33,97},{65,1},{97,33},{2,66}... | collective-permute-start | bytes 1179656 | tf_op jit(solution)/shard_map/ppermute | solution.py:287
  39.1 25.1 %collective-permute-start.18 = (bf16[512,384]{1,0:T(8,128)(2,1)}, bf16[512,384]{1,0:T(8,128)(2,1)S(1)}, u32[]{:S(2)}, u32[]{:S(2)}) collective-permute-start(bf16[512,384]{1,0:T(8,128)(2,1)} %refs_2_.1), channel_id=1, source_target_pairs={{0,32},{32,64},{64,96},{96,0},{1,33},{33,65},{65,97},{97,1},{2,34}... | collective-permute-start | bytes 1179656 | tf_op jit(solution)/shard_map/ppermute | solution.py:287
  42.7 21.5 %collective-permute-start.14 = (bf16[512,384]{1,0:T(8,128)(2,1)}, bf16[512,384]{1,0:T(8,128)(2,1)S(1)}, u32[]{:S(2)}, u32[]{:S(2)}) collective-permute-start(bf16[512,384]{1,0:T(8,128)(2,1)} %refs_2_.1), channel_id=1, source_target_pairs={{0,2},{1,3},{2,0},{3,1},{4,6},{5,7},{6,4},{7,5},{8,10},{9,11},{10,... | collective-permute-start | bytes 1179656 | tf_op jit(solution)/shard_map/ppermute | solution.py:287
  44.8 19.3 %collective-permute-start.15 = (bf16[512,384]{1,0:T(8,128)(2,1)}, bf16[512,384]{1,0:T(8,128)(2,1)S(1)}, u32[]{:S(2)}, u32[]{:S(2)}) collective-permute-start(bf16[512,384]{1,0:T(8,128)(2,1)} %refs_2_.1), channel_id=1, source_target_pairs={{0,1},{1,2},{2,3},{3,0},{4,5},{5,6},{6,7},{7,4},{8,9},{9,10},{10,1... | collective-permute-start | bytes 1179656 | tf_op jit(solution)/shard_map/ppermute | solution.py:287
  64.2 9.4 %collective-permute-start.19 = (bf16[8,128,128]{2,1,0:T(8,128)(2,1)}, bf16[8,128,128]{2,1,0:T(8,128)(2,1)S(1)}, u32[]{:S(2)}, u32[]{:S(2)}) collective-permute-start(bf16[8,128,128]{2,1,0:T(8,128)(2,1)} %get-tuple-element.63.refs_0_), channel_id=1, source_target_pairs={{0,4},{4,8},{8,12},{12,0},{1,5},{5,9},{9,13},{13,1},{2,6},{6,10},{... | collective-permute-start | bytes 786440 | tf_op jit(solution)/shard_map/ppermute | solution.py:287
  64.3 26.1 %collective-permute-start.20 = (bf16[8,128,128]{2,1,0:T(8,128)(2,1)}, bf16[8,128,128]{2,1,0:T(8,128)(2,1)S(1)}, u32[]{:S(2)}, u32[]{:S(2)}) collective-permute-start(bf16[8,128,128]{2,1,0:T(8,128)(2,1)} %get-tuple-element.63.refs_0_), channel_id=1, source_target_pairs={{0,8},{4,12},{8,0},{12,4},{1,9},{5,13},{9,1},{13,5},{2,10},{6,14},... | collective-permute-start | bytes 786440 | tf_op jit(solution)/shard_map/ppermute | solution.py:287
  69.3 21.7 %collective-permute-start.21 = (bf16[8,128,128]{2,1,0:T(8,128)(2,1)}, bf16[8,128,128]{2,1,0:T(8,128)(2,1)}, u32[]{:S(2)}, u32[]{:S(2)}) collective-permute-start(bf16[8,128,128]{2,1,0:T(8,128)(2,1)} %get-tuple-element.63.refs_0_), channel_id=1, source_target_pairs={{0,12},{4,0},{8,4},{12,8},{1,13},{5,1},{9,5},{13,9},{2,14},{6,2},{... | collective-permute-start | bytes 786440 | tf_op jit(solution)/shard_map/ppermute | solution.py:287
  74.3 23.5 %collective-permute-start.23 = (bf16[8,128,128]{2,1,0:T(8,128)(2,1)}, bf16[8,128,128]{2,1,0:T(8,128)(2,1)S(1)}, u32[]{:S(2)}, u32[]{:S(2)}) collective-permute-start(bf16[8,128,128]{2,1,0:T(8,128)(2,1)} %get-tuple-element.71.refs_0_), channel_id=1, source_target_pairs={{0,16},{16,0},{1,17},{17,1},{2,18},{18,2},{3,19},{19,3},{4,20},{20... | collective-permute-start | bytes 786440 | tf_op jit(solution)/shard_map/ppermute | solution.py:287
  90.3 7.4 %collective-permute-start.22 = (s32[1,17]{1,0:T(1,128)S(1)}, s32[1,17]{1,0:T(1,128)S(1)}, u32[]{:S(2)}, u32[]{:S(2)}) collective-permute-start(s32[1,17]{1,0:T(1,128)S(1)} %pad_add_fusion.3), channel_id=1, source_target_pairs={{0,16},{16,0},{1,17},{17,1},{2,18},{18,2},{3,19},{19,3},{4,20},{20... | collective-permute-start | bytes 212 | tf_op jit(solution)/shard_map/ppermute | solution.py:287
  107.8 15.4 %collective-permute-start.30 = (f32[112,128]{1,0:T(8,128)}, f32[112,128]{1,0:T(8,128)S(1)}, u32[]{:S(2)}, u32[]{:S(2)}) collective-permute-start(f32[112,128]{1,0:T(8,128)} %get-tuple-element.85), channel_id=1, source_target_pairs={{0,96},{32,0},{64,32},{96,64},{1,97},{33,1},{65,33},{97,65},{2,98}... | collective-permute-start | bytes 172040 | tf_op jit(solution)/shard_map/ppermute | solution.py:287
  132.1 11.8 %collective-permute-start.33 = (bf16[4,128,128]{2,1,0:T(8,128)(2,1)S(1)}, bf16[4,128,128]{2,1,0:T(8,128)(2,1)S(1)}, u32[]{:S(2)}, u32[]{:S(2)}) collective-permute-start(bf16[4,128,128]{2,1,0:T(8,128)(2,1)S(1)} %get-tuple-element.88), channel_id=1, source_target_pairs={{0,96},{32,0},{64,32},{96,64},{1,97},{33,1},{65,33},{97,65},{2,98}... | collective-permute-start | bytes 393224 | tf_op jit(solution)/shard_map/ppermute | solution.py:287
  132.9 11.6 %collective-permute-start.32 = (bf16[4,128,128]{2,1,0:T(8,128)(2,1)S(1)}, bf16[4,128,128]{2,1,0:T(8,128)(2,1)S(1)}, u32[]{:S(2)}, u32[]{:S(2)}) collective-permute-start(bf16[4,128,128]{2,1,0:T(8,128)(2,1)S(1)} %get-tuple-element.87), channel_id=1, source_target_pairs={{0,64},{32,96},{64,0},{96,32},{1,65},{33,97},{65,1},{97,33},{2,66}... | collective-permute-start | bytes 393224 | tf_op jit(solution)/shard_map/ppermute | solution.py:287
  (43 other events, 411.3 us)

commit v5 on v3

--- a/solution.py
+++ b/solution.py
@@ -13,13 +13,14 @@
 
 
 def blocks_kernel(
-    place, count, bias, w_rows, w_wide, w_cols, left0, left1, left2, left3, right0, right1, teacher,
+    place, count, bias, w_turned, w_plain, left0, left1, left2, left3, right0, right1,
+    right2, right3, teacher,
     left_grads, right_grads, bin_out, cross_out,
-    left_tiles, right_tiles, target, logit, left_turn, right_turn, left_sum, right_sum,
+    w_rows, w_wide, w_cols, left_tiles, right_tiles, target, logit, left_turn, right_turn, left_sum, right_sum,
     tile_sem, target_sem,
 ):
     left_from = (left0, left1, left2, left3)
-    right_from = (right0, right1)
+    right_from = (right0, right1, right2, right3)
     slots, bins, tile, width = teacher.shape
     live = count[0]
 
@@ -52,6 +53,11 @@
                 right_copy(slot, n).start()
 
     target_copy(0).start()
+    for k in range(bins):
+        row = w_turned[k : k + 1, :]
+        w_wide[k] = jnp.broadcast_to(row, (8, width))
+        w_rows[k] = jnp.broadcast_to(row, (16, width)).astype(jnp.bfloat16)
+        w_cols[k] = jnp.broadcast_to(w_plain[:, k : k + 1], (width, tile)).astype(jnp.bfloat16)
     bin_out[...] = jnp.zeros(bin_out.shape, jnp.float32)
     cross_out[...] = jnp.zeros(cross_out.shape, jnp.float32)
 
@@ -147,10 +153,7 @@
 def run_blocks(place, count, bin_weight, bin_bias, left_from, right_from, teacher):
     slots, bins, tile, _ = teacher.shape
     width = bin_weight.shape[0]
-    turned = bin_weight.T
-    w_rows = jnp.broadcast_to(turned[:, None, :], (bins, 16, width))
-    w_wide = jnp.broadcast_to(turned[:, None, :].astype(jnp.float32), (bins, 8, width))
-    w_cols = jnp.broadcast_to(turned[:, :, None], (bins, width, tile))
+    wide = bin_weight.astype(jnp.float32)
     smem = pl.BlockSpec(memory_space=pltpu.SMEM)
     vmem = pl.BlockSpec(memory_space=pltpu.VMEM)
     hbm = pl.BlockSpec(memory_space=pl.ANY)
@@ -163,9 +166,12 @@
             jax.ShapeDtypeStruct((bins, 8, width), f32),
             jax.ShapeDtypeStruct((8, tile), f32),
         ],
-        in_specs=[smem] * 3 + [vmem] * 3 + [hbm] * 7,
+        in_specs=[smem] * 3 + [vmem] * 2 + [hbm] * 9,
         out_specs=[vmem] * 4,
         scratch_shapes=[
+            pltpu.VMEM((bins, 16, width), bf16),
+            pltpu.VMEM((bins, 8, width), f32),
+            pltpu.VMEM((bins, width, tile), bf16),
             pltpu.VMEM((slots, tile, width), bf16),
             pltpu.VMEM((slots, tile, width), bf16),
             pltpu.VMEM((2, bins, tile, tile), bf16),
@@ -181,7 +187,7 @@
         cost_estimate=pl.CostEstimate(
             flops=6 * 8 * 64 * 128**3, bytes_accessed=20 * 2**20, transcendentals=8 * 2**20
         ),
-    )(place, count, bin_bias, w_rows, w_wide, w_cols, *left_from, *right_from, teacher)
+    )(place, count, bin_bias, wide.T, wide, *left_from, *right_from, teacher)
 
 
 AXES = ("z", "core", "y", "x")
@@ -270,41 +276,16 @@
     return [shift(value, axis, s) for s in range(1, lax.axis_size(axis))]
 
 
-SCALARS = 16
-
-
-def split_rows(value):
-    body, tail = value[:-SCALARS], value[-SCALARS:]
-    high = tail.astype(jnp.bfloat16)
-    low = (tail - high.astype(jnp.float32)).astype(jnp.bfloat16)
-    return jnp.concatenate([body.astype(jnp.bfloat16), high, low])
-
-
-def join_rows(sent):
-    sent = sent.astype(jnp.float32)
-    body, high, low = sent[: -2 * SCALARS], sent[-2 * SCALARS : -SCALARS], sent[-SCALARS:]
-    return jnp.concatenate([body, high + low])
-
-
-def add_kernel(value, sent1, sent2, sent3, out, send):
-    total = value[...]
-    for sent in (sent1, sent2, sent3):
-        total = total + join_rows(sent[...])
-    out[...] = total
-    send[...] = split_rows(total)
-
-
-def add_sent(value, sent):
-    vmem = pl.BlockSpec(memory_space=pltpu.VMEM)
-    return pl.pallas_call(
-        add_kernel,
-        out_shape=[
-            jax.ShapeDtypeStruct(value.shape, jnp.float32),
-            jax.ShapeDtypeStruct(sent[0].shape, jnp.bfloat16),
-        ],
-        in_specs=[vmem] * 4,
-        out_specs=[vmem] * 2,
-    )(value, *sent)
+def after(value, *others):
+    return lax.optimization_barrier((value,) + others)[0]
+
+
+def low_parts(value, count):
+    parts = []
+    for _ in range(count):
+        parts.append(value.astype(jnp.bfloat16))
+        value = value - parts[-1].astype(jnp.float32)
+    return parts
 
 
 def per_device(
@@ -316,39 +297,43 @@
     left_wide = left_weight.astype(jnp.float32)
     right_wide = right_weight.astype(jnp.float32)
     info = jnp.concatenate([own_tiles.reshape(1, -1), block_count[None]], axis=1)
-    info_y = jnp.concatenate([info] + ring(info, "y"))
-    info_core = jnp.concatenate([info] + ring(info, "core"))
     left_local = jnp.dot(single, left_weight, preferred_element_type=jnp.float32).astype(
         jnp.bfloat16
     )
-    right_local = jnp.dot(single, right_weight, preferred_element_type=jnp.float32).astype(
-        jnp.bfloat16
-    )
     rows_dev, width = left_local.shape
     left_local = left_local.reshape(-1, tile, width)
-    right_local = right_local.reshape(-1, tile, width)
     here = jnp.stack([lax.axis_index(a) for a in AXES]).astype(jnp.int32)
     z, core, y = here[0], here[1], here[2]
-    picked = pick_tiles(info_y, here, [left_local] + ring(left_local, "x"))
+    left_near = [left_local] + ring(left_local, "x")
+    info_first = after(info, left_local)
+    right_local = jnp.dot(after(single, left_near[1]), right_weight, preferred_element_type=jnp.float32).astype(
+        jnp.bfloat16
+    )
+    right_local = right_local.reshape(-1, tile, width)
+    info_y = jnp.concatenate([info_first] + ring(info_first, "y"))
+    picked = pick_tiles(info_y, here, left_near)
     left_from = [picked[0]] + [shift(picked[s], "y", s) for s in (1, 2, 3)]
-    right_near = jnp.concatenate([right_local] + ring(right_local, "z"))
-    right_from = [right_near, shift(right_near, "core", 1)]
+    right_pair = jnp.concatenate([right_local, shift(right_local, "core", 1)])
+    right_pair = after(right_pair, *picked)
+    right_from = [right_pair] + ring(right_pair, "z")
     row, col = own_tiles[:, 0], own_tiles[:, 1]
     place = jnp.stack(
         [
             (y - row // 16 % 4) % 4,
-            (core - col // 64 % 2) % 2,
-            (z - col // 128 % 4) % 4 * TILES_DEV + col % TILES_DEV,
+            (z - col // 128 % 4) % 4,
+            (core - col // 64 % 2) % 2 * TILES_DEV + col % TILES_DEV,
         ],
         axis=1,
     )
     left_slots, right_slots, bins_part, cross_part = run_blocks(
         place, block_count, bin_weight, bin_bias, left_from, right_from, teacher[0]
     )
-    left_own, *left_far = fold_slots(0, info_y, here, [left_slots] + ring(left_slots, "y"))
-    right_own, *right_far = fold_slots(
-        1, info_core, here, [right_slots] + ring(right_slots, "core")
-    )
+    left_ring = ring(left_slots, "y")
+    info_last = after(info, right_slots)
+    info_core = jnp.concatenate([info_last] + ring(info_last, "core"))
+    right_ring = ring(right_slots, "core")
+    left_own, *left_far = fold_slots(0, info_y, here, [left_slots] + left_ring)
+    right_own, *right_far = fold_slots(1, info_core, here, [right_slots] + right_ring)
     left_rows_grad, right_rows_grad = left_own, right_own
     for s in (1, 2, 3):
         left_rows_grad = left_rows_grad + shift(left_far[s - 1], "x", s).astype(jnp.float32)
@@ -359,29 +344,36 @@
     part_left = jnp.dot(single_wide.T, left_rows_grad, precision=lax.Precision.HIGHEST)
     part_right = jnp.dot(single_wide.T, right_rows_grad, precision=lax.Precision.HIGHEST)
     depth = part_left.shape[0]
-    scalars = jnp.stack([jnp.sum(cross_part), block_count[0].astype(jnp.float32)])
-    scalars = jnp.pad(scalars[None], ((0, SCALARS - 1), (0, width - 2)))
-    part_bin = jnp.sum(bins_part, axis=1)
-    first = jnp.concatenate([part_left, part_bin, jnp.zeros_like(scalars)])
-    second = jnp.concatenate([part_right, jnp.zeros_like(part_bin), scalars])
-    low_core = core == 0
-    total = jnp.where(low_core, first, second) + shift(
-        jnp.where(low_core, second, first), "core", 1
-    )
-    send = split_rows(total)
-    for axis in ("z", "y", "x"):
-        total, send = add_sent(total, ring(send, axis))
-    other = shift(total, "core", 1)
-    first = jnp.where(low_core, total, other)
-    second = jnp.where(low_core, other, total)
+    rows_sum = 2 * depth + bins
+    chunk = rows_sum // devices + 1
+    last = rows_sum // chunk, rows_sum % chunk
+    bf16, f32 = jnp.bfloat16, jnp.float32
+    scalars = jnp.stack(low_parts(jnp.sum(cross_part), 3) + [block_count[0].astype(bf16)])
+    packed = jnp.concatenate(
+        [
+            part_left.astype(bf16),
+            part_right.astype(bf16),
+            jnp.sum(bins_part, axis=1).astype(bf16),
+            jnp.pad(scalars[None], ((0, chunk * devices - rows_sum - 1), (0, width - 4))),
+        ]
+    ).reshape(devices, chunk, width)
+    mine = jnp.sum(lax.all_to_all(packed, AXES, 0, 0).astype(f32), axis=0)
+    high, low = low_parts(mine, 2)
+    mine = jnp.concatenate([high, low[last[1] : last[1] + 1]])
+    totals = lax.all_to_all(
+        jnp.broadcast_to(mine[None], (devices, chunk + 1, width)), AXES, 0, 0
+    ).astype(f32)
+    scalars = totals[last[0], last[1]] + totals[last[0], chunk]
+    totals = totals[:, :chunk].reshape(-1, width)
     grad_single = (
         jnp.dot(left_rows_grad, left_wide.T, precision=lax.Precision.HIGHEST)
         + jnp.dot(right_rows_grad, right_wide.T, precision=lax.Precision.HIGHEST)
     ).astype(jnp.bfloat16)
-    grad_left = first[:depth] / devices
-    grad_right = second[:depth] / devices
-    grad_bin = first[depth : depth + bins].T / devices
-    loss_value = second[depth + bins, 0] / (second[depth + bins, 1] * (tile * tile))
+    grad_left = totals[:depth] / devices
+    grad_right = totals[depth : 2 * depth] / devices
+    grad_bin = totals[2 * depth : rows_sum].T / devices
+    cross_total = scalars[0] + scalars[1] + scalars[2]
+    loss_value = cross_total / (scalars[3] * (tile * tile))
     return (grad_single, grad_left, grad_right, grad_bin, loss_value)
 
 

time: 157 us -> 149 us (0.949)
  starting transfers between devices: 75 us -> 60.2 us
  waiting for transfers between devices: 33.5 us -> 40.8 us
  Pallas kernels: 23.8 us -> 26.6 us
  other arithmetic: 5.48 us -> 2.88 us
  local copies, waits for them, and re-layouts: 8.47 us -> 5.96 us
  between operations: 4.07 us -> 6.52 us
    ppermute x35 -> x24, starting transfers between devices: 75 us -> 47.7 us  [shift(): lax.ppermute(value, axis, [(i, (i + step) % size) for i in range(size)])]
    all_to_all x0 -> x2, waiting for transfers between devices: none -> 20.8 us  [the longest x1 10.8 us: per_device(): mine = jnp.sum(lax.all_to_all(packed, AXES, 0, 0).astype(f32), axis=0)]
    ppermute x35 -> x24, waiting for transfers between devices: 33.5 us -> 20 us  [shift(): lax.ppermute(value, axis, [(i, (i + step) % size) for i in range(size)])]
    all_to_all x0 -> x2, starting transfers between devices: none -> 12.5 us  [the longest x1 8.27 us: per_device(): mine = jnp.sum(lax.all_to_all(packed, AXES, 0, 0).astype(f32), axis=0)]
    pallas_call x1, Pallas kernels: 14.8 us -> 23.3 us  [run_blocks(): pl.pallas_call(blocks_kernel, out_shape=[piece] * 2 + [jax.ShapeDtypeStru...]
    pallas_call x3 -> x0, Pallas kernels: 5.74 us -> none  [add_sent(): pl.pallas_call(add_kernel, out_shape=[jax.ShapeDtypeStruct(value.shape, j...]
    broadcast_in_dim x5 -> x2, local copies, waits for them, and re-layouts: 2.75 us -> 0.83 us  [the longest x1 0.72 us: per_device(): jnp.broadcast_to(mine[None], (devices, chunk + 1, width))]
    unnamed x31 -> x12, local copies, waits for them, and re-layouts: 4.19 us -> 2.41 us
  transfers between devices with their start and end apart: 35 -> 26, of which waited for: 19 -> 11; matrix products, arithmetic and copies ran while one was open for 5% -> 4% of each run, Pallas kernels for 2% -> 2%
where the time goes in v5:
time: 149 us; the launch traced here: 148 us
  starting transfers between devices  60.2 us (40%)
  waiting for transfers between devices  40.8 us (27%)
  Pallas kernels  26.6 us (18%)
  between operations  6.52 us (4%)
  local copies, waits for them, and re-layouts  5.96 us (4%)
  matrix products  4.94 us (3%)
  other arithmetic  2.88 us (2%)
    ppermute x24, starting transfers between devices, shift(): lax.ppermute(value, axis, [(i, (i + step) % size) for i in range(size)])  47.7 us
    pallas_call x1, Pallas kernels, run_blocks(): pl.pallas_call(blocks_kernel, out_shape=[piece] * 2 + [jax.ShapeDtypeStru...  23.3 us
    ppermute x24, waiting for transfers between devices, shift(): lax.ppermute(value, axis, [(i, (i + step) % size) for i in range(size)])  20 us
    all_to_all x1, waiting for transfers between devices, per_device(): mine = jnp.sum(lax.all_to_all(packed, AXES, 0, 0).astype(f32), axis=0)  10.8 us
    all_to_all x1, waiting for transfers between devices, per_device(): lax.all_to_all(jnp.broadcast_to(mine[None], (devices, chunk + 1, width)),...  10 us
    all_to_all x1, starting transfers between devices, per_device(): mine = jnp.sum(lax.all_to_all(packed, AXES, 0, 0).astype(f32), axis=0)  8.27 us
    all_to_all x1, starting transfers between devices, per_device(): lax.all_to_all(jnp.broadcast_to(mine[None], (devices, chunk + 1, width)),...  4.2 us
  transfers between devices with their start and end apart: 26, of which 11 were waited for; matrix products, arithmetic and copies ran while one was open for 4% of the time, Pallas kernels for 2%

profile of v5, /device:TPU:1, one launch (start us, length us, event | category | flops | bytes accessed | tf_op | source)
XLA Modules:
  0.0 147.9 jit_solution(1983198918037734005)
XLA Ops:
  3.5 2.1 %collective-permute-start = (s32[1,17]{1,0:T(1,128)S(1)}, s32[1,17]{1,0:T(1,128)S(1)}, u32[]{:S(2)}, u32[]{:S(2)}) collective-permute-start(s32[1,17]{1,0:T(1,128)S(1)} %pad_add_fusion.3), channel_id=1, source_target_pairs={{0,4},{4,8},{8,12},{12,0},{1,5},{5,9},{9,13},{13,1},{2,6},{6,10},{... | collective-permute-start | bytes 212 | tf_op jit(solution)/shard_map/ppermute | solution.py:272
  5.6 2.6 %collective-permute-start.1 = (s32[1,17]{1,0:T(1,128)S(1)}, s32[1,17]{1,0:T(1,128)S(1)}, u32[]{:S(2)}, u32[]{:S(2)}) collective-permute-start(s32[1,17]{1,0:T(1,128)S(1)} %pad_add_fusion.3), channel_id=1, source_target_pairs={{0,8},{4,12},{8,0},{12,4},{1,9},{5,13},{9,1},{13,5},{2,10},{6,14},... | collective-permute-start | bytes 212 | tf_op jit(solution)/shard_map/ppermute | solution.py:272
  10.5 2.5 %collective-permute-start.4 = (bf16[4,128,128]{2,1,0:T(8,128)(2,1)S(1)}, bf16[4,128,128]{2,1,0:T(8,128)(2,1)S(1)}, u32[]{:S(2)}, u32[]{:S(2)}) collective-permute-start(bf16[4,128,128]{2,1,0:T(8,128)(2,1)S(1)} %bitcast.39), channel_id=1, source_target_pairs={{0,2},{1,3},{2,0},{3,1},{4,6},{5,7},{6,4},{7,5},{8,10},{9,11},{10,... | collective-permute-start | bytes 393224 | tf_op jit(solution)/shard_map/ppermute | solution.py:272
  17.3 2.4 %collective-permute-start.9 = (bf16[4,128,128]{2,1,0:T(8,128)(2,1)S(1)}, bf16[4,128,128]{2,1,0:T(8,128)(2,1)S(1)}, u32[]{:S(2)}, u32[]{:S(2)}) collective-permute-start(bf16[4,128,128]{2,1,0:T(8,128)(2,1)S(1)} %bitcast.46), channel_id=1, source_target_pairs={{0,16},{16,0},{1,17},{17,1},{2,18},{18,2},{3,19},{19,3},{4,20},{20... | collective-permute-start | bytes 393224 | tf_op jit(solution)/shard_map/ppermute | solution.py:272
  21.7 1.9 %collective-permute-start.8 = (bf16[8,128,128]{2,1,0:T(8,128)(2,1)S(1)}, bf16[8,128,128]{2,1,0:T(8,128)(2,1)S(1)}, u32[]{:S(2)}, u32[]{:S(2)}) collective-permute-start(bf16[8,128,128]{2,1,0:T(8,128)(2,1)S(1)} %get-tuple-element.29), channel_id=1, source_target_pairs={{0,12},{4,0},{8,4},{12,8},{1,13},{5,1},{9,5},{13,9},{2,14},{6,2},{... | collective-permute-start | bytes 786440 | tf_op jit(solution)/shard_map/ppermute | solution.py:272
  23.7 1.7 %collective-permute-start.10 = (bf16[8,128,128]{2,1,0:T(8,128)(2,1)S(1)}, bf16[8,128,128]{2,1,0:T(8,128)(2,1)S(1)}, u32[]{:S(2)}, u32[]{:S(2)}) collective-permute-start(bf16[8,128,128]{2,1,0:T(8,128)(2,1)S(1)} %pad_maximum_fusion.right0), channel_id=1, source_target_pairs={{0,32},{32,64},{64,96},{96,0},{1,33},{33,65},{65,97},{97,1},{2,34}... | collective-permute-start | bytes 786440 | tf_op jit(solution)/shard_map/ppermute | solution.py:272
  25.4 3.3 %collective-permute-start.11 = (bf16[8,128,128]{2,1,0:T(8,128)(2,1)S(1)}, bf16[8,128,128]{2,1,0:T(8,128)(2,1)S(1)}, u32[]{:S(2)}, u32[]{:S(2)}) collective-permute-start(bf16[8,128,128]{2,1,0:T(8,128)(2,1)S(1)} %pad_maximum_fusion.right0), channel_id=1, source_target_pairs={{0,64},{32,96},{64,0},{96,32},{1,65},{33,97},{65,1},{97,33},{2,66}... | collective-permute-start | bytes 786440 | tf_op jit(solution)/shard_map/ppermute | solution.py:272
  28.7 2.2 %collective-permute-done.6.left1 = bf16[8,128,128]{2,1,0:T(8,128)(2,1)S(1)} collective-permute-done((bf16[8,128,128]{2,1,0:T(8,128)(2,1)S(1)}, bf16[8,128,128]{2,1,0:T(8,128)(2,1)S(1)}, u32[]{:S(2)}, u32[]{:S(2)}) %collective-permute-start.6) | collective-permute-done | bytes 262176 | tf_op jit(solution)/shard_map/ppermute | solution.py:272
  30.9 3.8 %collective-permute-start.12 = (bf16[8,128,128]{2,1,0:T(8,128)(2,1)S(1)}, bf16[8,128,128]{2,1,0:T(8,128)(2,1)S(1)}, u32[]{:S(2)}, u32[]{:S(2)}) collective-permute-start(bf16[8,128,128]{2,1,0:T(8,128)(2,1)S(1)} %pad_maximum_fusion.right0), channel_id=1, source_target_pairs={{0,96},{32,0},{64,32},{96,64},{1,97},{33,1},{65,33},{97,65},{2,98}... | collective-permute-start | bytes 786440 | tf_op jit(solution)/shard_map/ppermute | solution.py:272
  35.1 2.4 %collective-permute-done.11.right2 = bf16[8,128,128]{2,1,0:T(8,128)(2,1)S(1)} collective-permute-done((bf16[8,128,128]{2,1,0:T(8,128)(2,1)S(1)}, bf16[8,128,128]{2,1,0:T(8,128)(2,1)S(1)}, u32[]{:S(2)}, u32[]{:S(2)}) %collective-permute-start.11) | collective-permute-done | bytes 262176 | tf_op jit(solution)/shard_map/ppermute | solution.py:272
  39.1 23.3 %shard_map.120 = (bf16[8,128,128]{2,1,0:T(8,128)(2,1)S(1)}, bf16[8,128,128]{2,1,0:T(8,128)(2,1)S(1)}, f32[64,8,128]{2,1,0:T(8,128)S(1)}, f32[8,128]{1,0:T(8,128)S(1)}) custom-call(s32[8,3]{1,0:T(8,128)S(1)} %pad_add_fusion.place, s32[1]{0:T(128)} %copy.44.count, f32[64]{0:T(128)S(1)} %copy-done.1, f32[64,128]{1,0:T(8,128)S(1)} %copy.38.w_turned, ...), custom_call_target="tpu_custom_call" | custom-call | flops 6442450944 | bytes 20971520 | tf_op jit(solution)/shard_map/pallas_call | solution.py:162
  62.6 2.6 %collective-permute-start.15 = (bf16[8,128,128]{2,1,0:T(8,128)(2,1)S(1)}, bf16[8,128,128]{2,1,0:T(8,128)(2,1)S(1)}, u32[]{:S(2)}, u32[]{:S(2)}) collective-permute-start(bf16[8,128,128]{2,1,0:T(8,128)(2,1)S(1)} %get-tuple-element.32.refs_0_), channel_id=1, source_target_pairs={{0,12},{4,0},{8,4},{12,8},{1,13},{5,1},{9,5},{13,9},{2,14},{6,2},{... | collective-permute-start | bytes 786440 | tf_op jit(solution)/shard_map/ppermute | solution.py:272
  67.1 8.6 %collective-permute-done.13.refs_1_ = bf16[8,128,128]{2,1,0:T(8,128)(2,1)S(1)} collective-permute-done((bf16[8,128,128]{2,1,0:T(8,128)(2,1)S(1)}, bf16[8,128,128]{2,1,0:T(8,128)(2,1)S(1)}, u32[]{:S(2)}, u32[]{:S(2)}) %collective-permute-start.13) | collective-permute-done | bytes 262176 | tf_op jit(solution)/shard_map/ppermute | solution.py:272
  76.7 1.3 shard_map.121
  78.1 8.5 %collective-permute-start.17 = (bf16[4,128,128]{2,1,0:T(8,128)(2,1)S(1)}, bf16[4,128,128]{2,1,0:T(8,128)(2,1)S(1)}, u32[]{:S(2)}, u32[]{:S(2)}) collective-permute-start(bf16[4,128,128]{2,1,0:T(8,128)(2,1)S(1)} %get-tuple-element.35), channel_id=1, source_target_pairs={{0,2},{1,3},{2,0},{3,1},{4,6},{5,7},{6,4},{7,5},{8,10},{9,11},{10,... | collective-permute-start | bytes 393224 | tf_op jit(solution)/shard_map/ppermute | solution.py:272
  86.6 2.0 %collective-permute-start.18 = (bf16[4,128,128]{2,1,0:T(8,128)(2,1)S(1)}, bf16[4,128,128]{2,1,0:T(8,128)(2,1)S(1)}, u32[]{:S(2)}, u32[]{:S(2)}) collective-permute-start(bf16[4,128,128]{2,1,0:T(8,128)(2,1)S(1)} %get-tuple-element.36), channel_id=1, source_target_pairs={{0,3},{1,0},{2,1},{3,2},{4,7},{5,4},{6,5},{7,6},{8,11},{9,8},{10,9... | collective-permute-start | bytes 393224 | tf_op jit(solution)/shard_map/ppermute | solution.py:272
  88.8 4.2 %collective-permute-start.19 = (s32[1,17]{1,0:T(1,128)S(1)}, s32[1,17]{1,0:T(1,128)S(1)}, u32[]{:S(2)}, u32[]{:S(2)}) collective-permute-start(s32[1,17]{1,0:T(1,128)S(1)} %pad_add_fusion.3), channel_id=1, source_target_pairs={{0,16},{16,0},{1,17},{17,1},{2,18},{18,2},{3,19},{19,3},{4,20},{20... | collective-permute-start | bytes 212 | tf_op jit(solution)/shard_map/ppermute | solution.py:272
  94.9 3.3 %collective-permute-start.22 = (bf16[4,128,128]{2,1,0:T(8,128)(2,1)S(1)}, bf16[4,128,128]{2,1,0:T(8,128)(2,1)S(1)}, u32[]{:S(2)}, u32[]{:S(2)}) collective-permute-start(bf16[4,128,128]{2,1,0:T(8,128)(2,1)S(1)} %get-tuple-element.41), channel_id=1, source_target_pairs={{0,64},{32,96},{64,0},{96,32},{1,65},{33,97},{65,1},{97,33},{2,66}... | collective-permute-start | bytes 393224 | tf_op jit(solution)/shard_map/ppermute | solution.py:272
  98.2 2.0 %collective-permute-start.23 = (bf16[4,128,128]{2,1,0:T(8,128)(2,1)S(1)}, bf16[4,128,128]{2,1,0:T(8,128)(2,1)S(1)}, u32[]{:S(2)}, u32[]{:S(2)}) collective-permute-start(bf16[4,128,128]{2,1,0:T(8,128)(2,1)S(1)} %get-tuple-element.42), channel_id=1, source_target_pairs={{0,96},{32,0},{64,32},{96,64},{1,97},{33,1},{65,33},{97,65},{2,98}... | collective-permute-start | bytes 393224 | tf_op jit(solution)/shard_map/ppermute | solution.py:272
  100.9 3.7 %collective-permute-done.22 = bf16[4,128,128]{2,1,0:T(8,128)(2,1)S(1)} collective-permute-done((bf16[4,128,128]{2,1,0:T(8,128)(2,1)S(1)}, bf16[4,128,128]{2,1,0:T(8,128)(2,1)S(1)}, u32[]{:S(2)}, u32[]{:S(2)}) %collective-permute-start.22) | collective-permute-done | bytes 131104 | tf_op jit(solution)/shard_map/ppermute | solution.py:272
  106.1 8.3 %all-to-all-start = ((bf16[128,7,128]{2,1,0:T(8,128)(2,1)}), bf16[128,7,128]{2,1,0:T(8,128)(2,1)S(1)}, u32[]{:S(2)}, u32[]{:S(2)}) async-start(bf16[128,7,128]{2,1,0:T(8,128)(2,1)} %reshape.51), calls=%async_computation | async-start | bytes 524288 | tf_op jit(solution)/shard_map/all_to_all | solution.py:360
  114.9 10.8 %all-to-all-done = bf16[128,7,128]{2,1,0:T(8,128)(2,1)S(1)} async-done(((bf16[128,7,128]{2,1,0:T(8,128)(2,1)}), bf16[128,7,128]{2,1,0:T(8,128)(2,1)S(1)}, u32[]{:S(2)}, u32[]{:S(2)}) %all-to-all-start) | async-done | bytes 229408 | tf_op jit(solution)/shard_map/all_to_all | solution.py:360
  126.6 4.2 %all-to-all-start.1 = ((bf16[128,8,128]{2,1,0:T(8,128)(2,1)}), bf16[128,8,128]{2,1,0:T(8,128)(2,1)S(1)}, u32[]{:S(2)}, u32[]{:S(2)}) async-start(bf16[128,8,128]{2,1,0:T(8,128)(2,1)} %broadcast_in_dim.14), calls=%async_computation.1 | async-start | bytes 524288 | tf_op jit(solution)/shard_map/all_to_all | solution.py:363
  132.0 10.0 %all-to-all-done.1 = bf16[128,8,128]{2,1,0:T(8,128)(2,1)S(1)} async-done(((bf16[128,8,128]{2,1,0:T(8,128)(2,1)}), bf16[128,8,128]{2,1,0:T(8,128)(2,1)S(1)}, u32[]{:S(2)}, u32[]{:S(2)}) %all-to-all-start.1) | async-done | bytes 262176 | tf_op jit(solution)/shard_map/all_to_all | solution.py:363
  (84 shorter events, 23.8 us)
Async XLA Ops:
  3.5 11.4 %collective-permute-start = (s32[1,17]{1,0:T(1,128)S(1)}, s32[1,17]{1,0:T(1,128)S(1)}, u32[]{:S(2)}, u32[]{:S(2)}) collective-permute-start(s32[1,17]{1,0:T(1,128)S(1)} %pad_add_fusion.3), channel_id=1, source_target_pairs={{0,4},{4,8},{8,12},{12,0},{1,5},{5,9},{9,13},{13,1},{2,6},{6,10},{... | collective-permute-start | bytes 212 | tf_op jit(solution)/shard_map/ppermute | solution.py:272
  5.6 10.5 %collective-permute-start.1 = (s32[1,17]{1,0:T(1,128)S(1)}, s32[1,17]{1,0:T(1,128)S(1)}, u32[]{:S(2)}, u32[]{:S(2)}) collective-permute-start(s32[1,17]{1,0:T(1,128)S(1)} %pad_add_fusion.3), channel_id=1, source_target_pairs={{0,8},{4,12},{8,0},{12,4},{1,9},{5,13},{9,1},{13,5},{2,10},{6,14},... | collective-permute-start | bytes 212 | tf_op jit(solution)/shard_map/ppermute | solution.py:272
  8.2 7.9 %collective-permute-start.2 = (s32[1,17]{1,0:T(1,128)S(1)}, s32[1,17]{1,0:T(1,128)S(1)}, u32[]{:S(2)}, u32[]{:S(2)}) collective-permute-start(s32[1,17]{1,0:T(1,128)S(1)} %pad_add_fusion.3), channel_id=1, source_target_pairs={{0,12},{4,0},{8,4},{12,8},{1,13},{5,1},{9,5},{13,9},{2,14},{6,2},{... | collective-permute-start | bytes 212 | tf_op jit(solution)/shard_map/ppermute | solution.py:272
  9.3 6.9 %collective-permute-start.3 = (bf16[4,128,128]{2,1,0:T(8,128)(2,1)S(1)}, bf16[4,128,128]{2,1,0:T(8,128)(2,1)S(1)}, u32[]{:S(2)}, u32[]{:S(2)}) collective-permute-start(bf16[4,128,128]{2,1,0:T(8,128)(2,1)S(1)} %bitcast.38), channel_id=1, source_target_pairs={{0,1},{1,2},{2,3},{3,0},{4,5},{5,6},{6,7},{7,4},{8,9},{9,10},{10,1... | collective-permute-start | bytes 393224 | tf_op jit(solution)/shard_map/ppermute | solution.py:272
  10.5 9.2 %collective-permute-start.4 = (bf16[4,128,128]{2,1,0:T(8,128)(2,1)S(1)}, bf16[4,128,128]{2,1,0:T(8,128)(2,1)S(1)}, u32[]{:S(2)}, u32[]{:S(2)}) collective-permute-start(bf16[4,128,128]{2,1,0:T(8,128)(2,1)S(1)} %bitcast.39), channel_id=1, source_target_pairs={{0,2},{1,3},{2,0},{3,1},{4,6},{5,7},{6,4},{7,5},{8,10},{9,11},{10,... | collective-permute-start | bytes 393224 | tf_op jit(solution)/shard_map/ppermute | solution.py:272
  17.3 6.3 %collective-permute-start.9 = (bf16[4,128,128]{2,1,0:T(8,128)(2,1)S(1)}, bf16[4,128,128]{2,1,0:T(8,128)(2,1)S(1)}, u32[]{:S(2)}, u32[]{:S(2)}) collective-permute-start(bf16[4,128,128]{2,1,0:T(8,128)(2,1)S(1)} %bitcast.46), channel_id=1, source_target_pairs={{0,16},{16,0},{1,17},{17,1},{2,18},{18,2},{3,19},{19,3},{4,20},{20... | collective-permute-start | bytes 393224 | tf_op jit(solution)/shard_map/ppermute | solution.py:272
  20.6 10.2 %collective-permute-start.6 = (bf16[8,128,128]{2,1,0:T(8,128)(2,1)S(1)}, bf16[8,128,128]{2,1,0:T(8,128)(2,1)S(1)}, u32[]{:S(2)}, u32[]{:S(2)}) collective-permute-start(bf16[8,128,128]{2,1,0:T(8,128)(2,1)S(1)} %get-tuple-element.27), channel_id=1, source_target_pairs={{0,4},{4,8},{8,12},{12,0},{1,5},{5,9},{9,13},{13,1},{2,6},{6,10},{... | collective-permute-start | bytes 786440 | tf_op jit(solution)/shard_map/ppermute | solution.py:272
  21.1 13.6 %collective-permute-start.7 = (bf16[8,128,128]{2,1,0:T(8,128)(2,1)S(1)}, bf16[8,128,128]{2,1,0:T(8,128)(2,1)S(1)}, u32[]{:S(2)}, u32[]{:S(2)}) collective-permute-start(bf16[8,128,128]{2,1,0:T(8,128)(2,1)S(1)} %get-tuple-element.28), channel_id=1, source_target_pairs={{0,8},{4,12},{8,0},{12,4},{1,9},{5,13},{9,1},{13,5},{2,10},{6,14},... | collective-permute-start | bytes 786440 | tf_op jit(solution)/shard_map/ppermute | solution.py:272
  21.7 13.4 %collective-permute-start.8 = (bf16[8,128,128]{2,1,0:T(8,128)(2,1)S(1)}, bf16[8,128,128]{2,1,0:T(8,128)(2,1)S(1)}, u32[]{:S(2)}, u32[]{:S(2)}) collective-permute-start(bf16[8,128,128]{2,1,0:T(8,128)(2,1)S(1)} %get-tuple-element.29), channel_id=1, source_target_pairs={{0,12},{4,0},{8,4},{12,8},{1,13},{5,1},{9,5},{13,9},{2,14},{6,2},{... | collective-permute-start | bytes 786440 | tf_op jit(solution)/shard_map/ppermute | solution.py:272
  23.7 11.5 %collective-permute-start.10 = (bf16[8,128,128]{2,1,0:T(8,128)(2,1)S(1)}, bf16[8,128,128]{2,1,0:T(8,128)(2,1)S(1)}, u32[]{:S(2)}, u32[]{:S(2)}) collective-permute-start(bf16[8,128,128]{2,1,0:T(8,128)(2,1)S(1)} %pad_maximum_fusion.right0), channel_id=1, source_target_pairs={{0,32},{32,64},{64,96},{96,0},{1,33},{33,65},{65,97},{97,1},{2,34}... | collective-permute-start | bytes 786440 | tf_op jit(solution)/shard_map/ppermute | solution.py:272
  25.4 12.1 %collective-permute-start.11 = (bf16[8,128,128]{2,1,0:T(8,128)(2,1)S(1)}, bf16[8,128,128]{2,1,0:T(8,128)(2,1)S(1)}, u32[]{:S(2)}, u32[]{:S(2)}) collective-permute-start(bf16[8,128,128]{2,1,0:T(8,128)(2,1)S(1)} %pad_maximum_fusion.right0), channel_id=1, source_target_pairs={{0,64},{32,96},{64,0},{96,32},{1,65},{33,97},{65,1},{97,33},{2,66}... | collective-permute-start | bytes 786440 | tf_op jit(solution)/shard_map/ppermute | solution.py:272
  30.9 7.6 %collective-permute-start.12 = (bf16[8,128,128]{2,1,0:T(8,128)(2,1)S(1)}, bf16[8,128,128]{2,1,0:T(8,128)(2,1)S(1)}, u32[]{:S(2)}, u32[]{:S(2)}) collective-permute-start(bf16[8,128,128]{2,1,0:T(8,128)(2,1)S(1)} %pad_maximum_fusion.right0), channel_id=1, source_target_pairs={{0,96},{32,0},{64,32},{96,64},{1,97},{33,1},{65,33},{97,65},{2,98}... | collective-permute-start | bytes 786440 | tf_op jit(solution)/shard_map/ppermute | solution.py:272
  62.5 13.2 %collective-permute-start.13 = (bf16[8,128,128]{2,1,0:T(8,128)(2,1)S(1)}, bf16[8,128,128]{2,1,0:T(8,128)(2,1)S(1)}, u32[]{:S(2)}, u32[]{:S(2)}) collective-permute-start(bf16[8,128,128]{2,1,0:T(8,128)(2,1)S(1)} %get-tuple-element.32.refs_0_), channel_id=1, source_target_pairs={{0,4},{4,8},{8,12},{12,0},{1,5},{5,9},{9,13},{13,1},{2,6},{6,10},{... | collective-permute-start | bytes 786440 | tf_op jit(solution)/shard_map/ppermute | solution.py:272
  62.5 13.1 %collective-permute-start.14 = (bf16[8,128,128]{2,1,0:T(8,128)(2,1)S(1)}, bf16[8,128,128]{2,1,0:T(8,128)(2,1)S(1)}, u32[]{:S(2)}, u32[]{:S(2)}) collective-permute-start(bf16[8,128,128]{2,1,0:T(8,128)(2,1)S(1)} %get-tuple-element.32.refs_0_), channel_id=1, source_target_pairs={{0,8},{4,12},{8,0},{12,4},{1,9},{5,13},{9,1},{13,5},{2,10},{6,14},... | collective-permute-start | bytes 786440 | tf_op jit(solution)/shard_map/ppermute | solution.py:272
  62.6 14.0 %collective-permute-start.15 = (bf16[8,128,128]{2,1,0:T(8,128)(2,1)S(1)}, bf16[8,128,128]{2,1,0:T(8,128)(2,1)S(1)}, u32[]{:S(2)}, u32[]{:S(2)}) collective-permute-start(bf16[8,128,128]{2,1,0:T(8,128)(2,1)S(1)} %get-tuple-element.32.refs_0_), channel_id=1, source_target_pairs={{0,12},{4,0},{8,4},{12,8},{1,13},{5,1},{9,5},{13,9},{2,14},{6,2},{... | collective-permute-start | bytes 786440 | tf_op jit(solution)/shard_map/ppermute | solution.py:272
  65.2 28.6 %collective-permute-start.20 = (bf16[8,128,128]{2,1,0:T(8,128)(2,1)S(1)}, bf16[8,128,128]{2,1,0:T(8,128)(2,1)S(1)}, u32[]{:S(2)}, u32[]{:S(2)}) collective-permute-start(bf16[8,128,128]{2,1,0:T(8,128)(2,1)S(1)} %get-tuple-element.37.refs_0_), channel_id=1, source_target_pairs={{0,16},{16,0},{1,17},{17,1},{2,18},{18,2},{3,19},{19,3},{4,20},{20... | collective-permute-start | bytes 786440 | tf_op jit(solution)/shard_map/ppermute | solution.py:272
  78.0 20.2 %collective-permute-start.16 = (bf16[4,128,128]{2,1,0:T(8,128)(2,1)S(1)}, bf16[4,128,128]{2,1,0:T(8,128)(2,1)S(1)}, u32[]{:S(2)}, u32[]{:S(2)}) collective-permute-start(bf16[4,128,128]{2,1,0:T(8,128)(2,1)S(1)} %get-tuple-element.34), channel_id=1, source_target_pairs={{0,1},{1,2},{2,3},{3,0},{4,5},{5,6},{6,7},{7,4},{8,9},{9,10},{10,1... | collective-permute-start | bytes 393224 | tf_op jit(solution)/shard_map/ppermute | solution.py:272
  78.1 22.1 %collective-permute-start.17 = (bf16[4,128,128]{2,1,0:T(8,128)(2,1)S(1)}, bf16[4,128,128]{2,1,0:T(8,128)(2,1)S(1)}, u32[]{:S(2)}, u32[]{:S(2)}) collective-permute-start(bf16[4,128,128]{2,1,0:T(8,128)(2,1)S(1)} %get-tuple-element.35), channel_id=1, source_target_pairs={{0,2},{1,3},{2,0},{3,1},{4,6},{5,7},{6,4},{7,5},{8,10},{9,11},{10,... | collective-permute-start | bytes 393224 | tf_op jit(solution)/shard_map/ppermute | solution.py:272
  86.6 13.6 %collective-permute-start.18 = (bf16[4,128,128]{2,1,0:T(8,128)(2,1)S(1)}, bf16[4,128,128]{2,1,0:T(8,128)(2,1)S(1)}, u32[]{:S(2)}, u32[]{:S(2)}) collective-permute-start(bf16[4,128,128]{2,1,0:T(8,128)(2,1)S(1)} %get-tuple-element.36), channel_id=1, source_target_pairs={{0,3},{1,0},{2,1},{3,2},{4,7},{5,4},{6,5},{7,6},{8,11},{9,8},{10,9... | collective-permute-start | bytes 393224 | tf_op jit(solution)/shard_map/ppermute | solution.py:272
  94.8 6.1 %collective-permute-start.21 = (bf16[4,128,128]{2,1,0:T(8,128)(2,1)S(1)}, bf16[4,128,128]{2,1,0:T(8,128)(2,1)S(1)}, u32[]{:S(2)}, u32[]{:S(2)}) collective-permute-start(bf16[4,128,128]{2,1,0:T(8,128)(2,1)S(1)} %get-tuple-element.40), channel_id=1, source_target_pairs={{0,32},{32,64},{64,96},{96,0},{1,33},{33,65},{65,97},{97,1},{2,34}... | collective-permute-start | bytes 393224 | tf_op jit(solution)/shard_map/ppermute | solution.py:272
  94.9 9.7 %collective-permute-start.22 = (bf16[4,128,128]{2,1,0:T(8,128)(2,1)S(1)}, bf16[4,128,128]{2,1,0:T(8,128)(2,1)S(1)}, u32[]{:S(2)}, u32[]{:S(2)}) collective-permute-start(bf16[4,128,128]{2,1,0:T(8,128)(2,1)S(1)} %get-tuple-element.41), channel_id=1, source_target_pairs={{0,64},{32,96},{64,0},{96,32},{1,65},{33,97},{65,1},{97,33},{2,66}... | collective-permute-start | bytes 393224 | tf_op jit(solution)/shard_map/ppermute | solution.py:272
  98.2 6.4 %collective-permute-start.23 = (bf16[4,128,128]{2,1,0:T(8,128)(2,1)S(1)}, bf16[4,128,128]{2,1,0:T(8,128)(2,1)S(1)}, u32[]{:S(2)}, u32[]{:S(2)}) collective-permute-start(bf16[4,128,128]{2,1,0:T(8,128)(2,1)S(1)} %get-tuple-element.42), channel_id=1, source_target_pairs={{0,96},{32,0},{64,32},{96,64},{1,97},{33,1},{65,33},{97,65},{2,98}... | collective-permute-start | bytes 393224 | tf_op jit(solution)/shard_map/ppermute | solution.py:272
  106.1 19.5 %all-to-all-start = ((bf16[128,7,128]{2,1,0:T(8,128)(2,1)}), bf16[128,7,128]{2,1,0:T(8,128)(2,1)S(1)}, u32[]{:S(2)}, u32[]{:S(2)}) async-start(bf16[128,7,128]{2,1,0:T(8,128)(2,1)} %reshape.51), calls=%async_computation | async-start | bytes 524288 | tf_op jit(solution)/shard_map/all_to_all | solution.py:360
  126.6 15.5 %all-to-all-start.1 = ((bf16[128,8,128]{2,1,0:T(8,128)(2,1)}), bf16[128,8,128]{2,1,0:T(8,128)(2,1)S(1)}, u32[]{:S(2)}, u32[]{:S(2)}) async-start(bf16[128,8,128]{2,1,0:T(8,128)(2,1)} %broadcast_in_dim.14), calls=%async_computation.1 | async-start | bytes 524288 | tf_op jit(solution)/shard_map/all_to_all | solution.py:363
  (6 other events, 231.4 us)

commit v6 on v5

--- a/solution.py
+++ b/solution.py
@@ -325,19 +325,21 @@
         ],
         axis=1,
     )
+    info_last = after(info, *picked)
+    info_core = jnp.concatenate([info_last] + ring(info_last, "core"))
+    place = after(place, info_core)
     left_slots, right_slots, bins_part, cross_part = run_blocks(
         place, block_count, bin_weight, bin_bias, left_from, right_from, teacher[0]
     )
     left_ring = ring(left_slots, "y")
-    info_last = after(info, right_slots)
-    info_core = jnp.concatenate([info_last] + ring(info_last, "core"))
     right_ring = ring(right_slots, "core")
-    left_own, *left_far = fold_slots(0, info_y, here, [left_slots] + left_ring)
-    right_own, *right_far = fold_slots(1, info_core, here, [right_slots] + right_ring)
-    left_rows_grad, right_rows_grad = left_own, right_own
+    right_rows_grad, *right_far = fold_slots(1, info_core, here, [right_slots] + right_ring)
+    right_far = [shift(right_far[s - 1], "z", s) for s in (1, 2, 3)]
+    left_ring = after(left_ring, *right_far)
+    left_rows_grad, *left_far = fold_slots(0, info_y, here, [left_slots] + left_ring)
     for s in (1, 2, 3):
         left_rows_grad = left_rows_grad + shift(left_far[s - 1], "x", s).astype(jnp.float32)
-        right_rows_grad = right_rows_grad + shift(right_far[s - 1], "z", s).astype(jnp.float32)
+        right_rows_grad = right_rows_grad + right_far[s - 1].astype(jnp.float32)
     left_rows_grad = left_rows_grad.reshape(rows_dev, width)
     right_rows_grad = right_rows_grad.reshape(rows_dev, width)
     single_wide = single.astype(jnp.float32)

time: 149 us -> 154 us (1.034); the launches traced: 148 us -> 150 us
  starting transfers between devices: 60.2 us -> 79.1 us
  Pallas kernels: 26.6 us -> 14.2 us
  waiting for transfers between devices: 40.8 us -> 36.8 us
    ppermute x24, starting transfers between devices: 47.7 us -> 67.6 us  [shift(): lax.ppermute(value, axis, [(i, (i + step) % size) for i in range(size)])]
    pallas_call x1, Pallas kernels: 23.3 us -> 11 us  [run_blocks(): pl.pallas_call(blocks_kernel, out_shape=[piece] * 2 + [jax.ShapeDtypeStru...]
    ppermute x24, waiting for transfers between devices: 20 us -> 16 us  [shift(): lax.ppermute(value, axis, [(i, (i + step) % size) for i in range(size)])]
  transfers between devices with their start and end apart: 26 -> 26, of which waited for: 11 -> 10; matrix products, arithmetic and copies ran while one was open for 4% -> 4% of each run, Pallas kernels for 2% -> 1%
where the time goes in v6:
time: 154 us; the launch traced here: 150 us
  starting transfers between devices  79.1 us (51%)
  waiting for transfers between devices  36.8 us (24%)
  Pallas kernels  14.2 us (9%)
  between operations  6.53 us (4%)
  local copies, waits for them, and re-layouts  5.97 us (4%)
  matrix products  4.98 us (3%)
  other arithmetic  2.89 us (2%)
    ppermute x24, starting transfers between devices, shift(): lax.ppermute(value, axis, [(i, (i + step) % size) for i in range(size)])  67.6 us
    ppermute x24, waiting for transfers between devices, shift(): lax.ppermute(value, axis, [(i, (i + step) % size) for i in range(size)])  16 us
    pallas_call x1, Pallas kernels, run_blocks(): pl.pallas_call(blocks_kernel, out_shape=[piece] * 2 + [jax.ShapeDtypeStru...  11 us
    all_to_all x1, waiting for transfers between devices, per_device(): mine = jnp.sum(lax.all_to_all(packed, AXES, 0, 0).astype(f32), axis=0)  10.8 us
    all_to_all x1, waiting for transfers between devices, per_device(): lax.all_to_all(jnp.broadcast_to(mine[None], (devices, chunk + 1, width)),...  10 us
    all_to_all x1, starting transfers between devices, per_device(): mine = jnp.sum(lax.all_to_all(packed, AXES, 0, 0).astype(f32), axis=0)  7.36 us
    all_to_all x1, starting transfers between devices, per_device(): lax.all_to_all(jnp.broadcast_to(mine[None], (devices, chunk + 1, width)),...  4.2 us
  transfers between devices with their start and end apart: 26, of which 10 were waited for; matrix products, arithmetic and copies ran while one was open for 4% of the time, Pallas kernels for 1%

profile of v6, /device:TPU:1, one launch (start us, length us, event | category | flops | bytes accessed | tf_op | source)
XLA Modules:
  0.0 150.5 jit_solution(344593706503048203)
XLA Ops:
  3.5 2.1 %collective-permute-start = (s32[1,17]{1,0:T(1,128)S(1)}, s32[1,17]{1,0:T(1,128)S(1)}, u32[]{:S(2)}, u32[]{:S(2)}) collective-permute-start(s32[1,17]{1,0:T(1,128)S(1)} %pad_add_fusion.3), channel_id=1, source_target_pairs={{0,4},{4,8},{8,12},{12,0},{1,5},{5,9},{9,13},{13,1},{2,6},{6,10},{... | collective-permute-start | bytes 212 | tf_op jit(solution)/shard_map/ppermute | solution.py:272
  5.6 2.6 %collective-permute-start.1 = (s32[1,17]{1,0:T(1,128)S(1)}, s32[1,17]{1,0:T(1,128)S(1)}, u32[]{:S(2)}, u32[]{:S(2)}) collective-permute-start(s32[1,17]{1,0:T(1,128)S(1)} %pad_add_fusion.3), channel_id=1, source_target_pairs={{0,8},{4,12},{8,0},{12,4},{1,9},{5,13},{9,1},{13,5},{2,10},{6,14},... | collective-permute-start | bytes 212 | tf_op jit(solution)/shard_map/ppermute | solution.py:272
  10.5 2.5 %collective-permute-start.4 = (bf16[4,128,128]{2,1,0:T(8,128)(2,1)S(1)}, bf16[4,128,128]{2,1,0:T(8,128)(2,1)S(1)}, u32[]{:S(2)}, u32[]{:S(2)}) collective-permute-start(bf16[4,128,128]{2,1,0:T(8,128)(2,1)S(1)} %bitcast.39), channel_id=1, source_target_pairs={{0,2},{1,3},{2,0},{3,1},{4,6},{5,7},{6,4},{7,5},{8,10},{9,11},{10,... | collective-permute-start | bytes 393224 | tf_op jit(solution)/shard_map/ppermute | solution.py:272
  17.2 2.5 %collective-permute-start.10 = (bf16[4,128,128]{2,1,0:T(8,128)(2,1)S(1)}, bf16[4,128,128]{2,1,0:T(8,128)(2,1)S(1)}, u32[]{:S(2)}, u32[]{:S(2)}) collective-permute-start(bf16[4,128,128]{2,1,0:T(8,128)(2,1)S(1)} %bitcast.46), channel_id=1, source_target_pairs={{0,16},{16,0},{1,17},{17,1},{2,18},{18,2},{3,19},{19,3},{4,20},{20... | collective-permute-start | bytes 393224 | tf_op jit(solution)/shard_map/ppermute | solution.py:272
  21.6 1.9 %collective-permute-start.9 = (bf16[8,128,128]{2,1,0:T(8,128)(2,1)S(1)}, bf16[8,128,128]{2,1,0:T(8,128)(2,1)S(1)}, u32[]{:S(2)}, u32[]{:S(2)}) collective-permute-start(bf16[8,128,128]{2,1,0:T(8,128)(2,1)S(1)} %get-tuple-element.33), channel_id=1, source_target_pairs={{0,12},{4,0},{8,4},{12,8},{1,13},{5,1},{9,5},{13,9},{2,14},{6,2},{... | collective-permute-start | bytes 786440 | tf_op jit(solution)/shard_map/ppermute | solution.py:272
  23.5 2.8 %collective-permute-start.6 = (s32[1,17]{1,0:T(1,128)S(1)}, s32[1,17]{1,0:T(1,128)S(1)}, u32[]{:S(2)}, u32[]{:S(2)}) collective-permute-start(s32[1,17]{1,0:T(1,128)S(1)} %pad_add_fusion.3), channel_id=1, source_target_pairs={{0,16},{16,0},{1,17},{17,1},{2,18},{18,2},{3,19},{19,3},{4,20},{20... | collective-permute-start | bytes 212 | tf_op jit(solution)/shard_map/ppermute | solution.py:272
  26.3 1.7 %collective-permute-start.11 = (bf16[8,128,128]{2,1,0:T(8,128)(2,1)S(1)}, bf16[8,128,128]{2,1,0:T(8,128)(2,1)S(1)}, u32[]{:S(2)}, u32[]{:S(2)}) collective-permute-start(bf16[8,128,128]{2,1,0:T(8,128)(2,1)S(1)} %pad_maximum_fusion.right0), channel_id=1, source_target_pairs={{0,32},{32,64},{64,96},{96,0},{1,33},{33,65},{65,97},{97,1},{2,34}... | collective-permute-start | bytes 786440 | tf_op jit(solution)/shard_map/ppermute | solution.py:272
  28.0 3.3 %collective-permute-start.12 = (bf16[8,128,128]{2,1,0:T(8,128)(2,1)S(1)}, bf16[8,128,128]{2,1,0:T(8,128)(2,1)S(1)}, u32[]{:S(2)}, u32[]{:S(2)}) collective-permute-start(bf16[8,128,128]{2,1,0:T(8,128)(2,1)S(1)} %pad_maximum_fusion.right0), channel_id=1, source_target_pairs={{0,64},{32,96},{64,0},{96,32},{1,65},{33,97},{65,1},{97,33},{2,66}... | collective-permute-start | bytes 786440 | tf_op jit(solution)/shard_map/ppermute | solution.py:272
  31.3 3.3 %collective-permute-start.13 = (bf16[8,128,128]{2,1,0:T(8,128)(2,1)S(1)}, bf16[8,128,128]{2,1,0:T(8,128)(2,1)S(1)}, u32[]{:S(2)}, u32[]{:S(2)}) collective-permute-start(bf16[8,128,128]{2,1,0:T(8,128)(2,1)S(1)} %pad_maximum_fusion.right0), channel_id=1, source_target_pairs={{0,96},{32,0},{64,32},{96,64},{1,97},{33,1},{65,33},{97,65},{2,98}... | collective-permute-start | bytes 786440 | tf_op jit(solution)/shard_map/ppermute | solution.py:272
  35.0 1.8 %collective-permute-done.11.right1 = bf16[8,128,128]{2,1,0:T(8,128)(2,1)S(1)} collective-permute-done((bf16[8,128,128]{2,1,0:T(8,128)(2,1)S(1)}, bf16[8,128,128]{2,1,0:T(8,128)(2,1)S(1)}, u32[]{:S(2)}, u32[]{:S(2)}) %collective-permute-start.11) | collective-permute-done | bytes 262176 | tf_op jit(solution)/shard_map/ppermute | solution.py:272
  36.8 6.6 %collective-permute-done.12.right2 = bf16[8,128,128]{2,1,0:T(8,128)(2,1)S(1)} collective-permute-done((bf16[8,128,128]{2,1,0:T(8,128)(2,1)S(1)}, bf16[8,128,128]{2,1,0:T(8,128)(2,1)S(1)}, u32[]{:S(2)}, u32[]{:S(2)}) %collective-permute-start.12) | collective-permute-done | bytes 262176 | tf_op jit(solution)/shard_map/ppermute | solution.py:272
  44.1 11.0 %shard_map.120 = (bf16[8,128,128]{2,1,0:T(8,128)(2,1)S(1)}, bf16[8,128,128]{2,1,0:T(8,128)(2,1)S(1)}, f32[64,8,128]{2,1,0:T(8,128)S(1)}, f32[8,128]{1,0:T(8,128)S(1)}) custom-call(s32[8,3]{1,0:T(8,128)S(1)} %pad_add_fusion.place, s32[1]{0:T(128)} %copy.44.count, f32[64]{0:T(128)S(1)} %copy-done.1, f32[64,128]{1,0:T(8,128)S(1)} %copy.38.w_turned, ...), custom_call_target="tpu_custom_call" | custom-call | flops 6442450944 | bytes 20971520 | tf_op jit(solution)/shard_map/pallas_call | solution.py:162
  55.2 18.4 %collective-permute-start.14 = (bf16[8,128,128]{2,1,0:T(8,128)(2,1)S(1)}, bf16[8,128,128]{2,1,0:T(8,128)(2,1)S(1)}, u32[]{:S(2)}, u32[]{:S(2)}) collective-permute-start(bf16[8,128,128]{2,1,0:T(8,128)(2,1)S(1)} %get-tuple-element.38.refs_0_), channel_id=1, source_target_pairs={{0,4},{4,8},{8,12},{12,0},{1,5},{5,9},{9,13},{13,1},{2,6},{6,10},{... | collective-permute-start | bytes 786440 | tf_op jit(solution)/shard_map/ppermute | solution.py:272
  73.6 6.3 %collective-permute-start.15 = (bf16[8,128,128]{2,1,0:T(8,128)(2,1)S(1)}, bf16[8,128,128]{2,1,0:T(8,128)(2,1)S(1)}, u32[]{:S(2)}, u32[]{:S(2)}) collective-permute-start(bf16[8,128,128]{2,1,0:T(8,128)(2,1)S(1)} %get-tuple-element.38.refs_0_), channel_id=1, source_target_pairs={{0,8},{4,12},{8,0},{12,4},{1,9},{5,13},{9,1},{13,5},{2,10},{6,14},... | collective-permute-start | bytes 786440 | tf_op jit(solution)/shard_map/ppermute | solution.py:272
  80.9 6.5 %collective-permute-start.18 = (bf16[4,128,128]{2,1,0:T(8,128)(2,1)S(1)}, bf16[4,128,128]{2,1,0:T(8,128)(2,1)S(1)}, u32[]{:S(2)}, u32[]{:S(2)}) collective-permute-start(bf16[4,128,128]{2,1,0:T(8,128)(2,1)S(1)} %get-tuple-element.40), channel_id=1, source_target_pairs={{0,32},{32,64},{64,96},{96,0},{1,33},{33,65},{65,97},{97,1},{2,34}... | collective-permute-start | bytes 393224 | tf_op jit(solution)/shard_map/ppermute | solution.py:272
  87.5 2.5 %collective-permute-start.20 = (bf16[4,128,128]{2,1,0:T(8,128)(2,1)S(1)}, bf16[4,128,128]{2,1,0:T(8,128)(2,1)S(1)}, u32[]{:S(2)}, u32[]{:S(2)}) collective-permute-start(bf16[4,128,128]{2,1,0:T(8,128)(2,1)S(1)} %get-tuple-element.42), channel_id=1, source_target_pairs={{0,96},{32,0},{64,32},{96,64},{1,97},{33,1},{65,33},{97,65},{2,98}... | collective-permute-start | bytes 393224 | tf_op jit(solution)/shard_map/ppermute | solution.py:272
  92.8 2.2 %collective-permute-done.20 = bf16[4,128,128]{2,1,0:T(8,128)(2,1)S(1)} collective-permute-done((bf16[4,128,128]{2,1,0:T(8,128)(2,1)S(1)}, bf16[4,128,128]{2,1,0:T(8,128)(2,1)S(1)}, u32[]{:S(2)}, u32[]{:S(2)}) %collective-permute-start.20) | collective-permute-done | bytes 131104 | tf_op jit(solution)/shard_map/ppermute | solution.py:272
  96.3 4.1 %collective-permute-start.21 = (bf16[4,128,128]{2,1,0:T(8,128)(2,1)S(1)}, bf16[4,128,128]{2,1,0:T(8,128)(2,1)S(1)}, u32[]{:S(2)}, u32[]{:S(2)}) collective-permute-start(bf16[4,128,128]{2,1,0:T(8,128)(2,1)S(1)} %get-tuple-element.47), channel_id=1, source_target_pairs={{0,1},{1,2},{2,3},{3,0},{4,5},{5,6},{6,7},{7,4},{8,9},{9,10},{10,1... | collective-permute-start | bytes 393224 | tf_op jit(solution)/shard_map/ppermute | solution.py:272
  100.4 2.1 %collective-permute-start.22 = (bf16[4,128,128]{2,1,0:T(8,128)(2,1)S(1)}, bf16[4,128,128]{2,1,0:T(8,128)(2,1)S(1)}, u32[]{:S(2)}, u32[]{:S(2)}) collective-permute-start(bf16[4,128,128]{2,1,0:T(8,128)(2,1)S(1)} %get-tuple-element.48), channel_id=1, source_target_pairs={{0,2},{1,3},{2,0},{3,1},{4,6},{5,7},{6,4},{7,5},{8,10},{9,11},{10,... | collective-permute-start | bytes 393224 | tf_op jit(solution)/shard_map/ppermute | solution.py:272
  103.8 3.6 %collective-permute-done.22 = bf16[4,128,128]{2,1,0:T(8,128)(2,1)S(1)} collective-permute-done((bf16[4,128,128]{2,1,0:T(8,128)(2,1)S(1)}, bf16[4,128,128]{2,1,0:T(8,128)(2,1)S(1)}, u32[]{:S(2)}, u32[]{:S(2)}) %collective-permute-start.22) | collective-permute-done | bytes 131104 | tf_op jit(solution)/shard_map/ppermute | solution.py:272
  109.7 7.4 %all-to-all-start = ((bf16[128,7,128]{2,1,0:T(8,128)(2,1)}), bf16[128,7,128]{2,1,0:T(8,128)(2,1)S(1)}, u32[]{:S(2)}, u32[]{:S(2)}) async-start(bf16[128,7,128]{2,1,0:T(8,128)(2,1)} %reshape.51), calls=%async_computation | async-start | bytes 524288 | tf_op jit(solution)/shard_map/all_to_all | solution.py:362
  117.5 10.8 %all-to-all-done = bf16[128,7,128]{2,1,0:T(8,128)(2,1)S(1)} async-done(((bf16[128,7,128]{2,1,0:T(8,128)(2,1)}), bf16[128,7,128]{2,1,0:T(8,128)(2,1)S(1)}, u32[]{:S(2)}, u32[]{:S(2)}) %all-to-all-start) | async-done | bytes 229408 | tf_op jit(solution)/shard_map/all_to_all | solution.py:362
  129.2 4.2 %all-to-all-start.1 = ((bf16[128,8,128]{2,1,0:T(8,128)(2,1)}), bf16[128,8,128]{2,1,0:T(8,128)(2,1)S(1)}, u32[]{:S(2)}, u32[]{:S(2)}) async-start(bf16[128,8,128]{2,1,0:T(8,128)(2,1)} %broadcast_in_dim.14), calls=%async_computation.1 | async-start | bytes 524288 | tf_op jit(solution)/shard_map/all_to_all | solution.py:365
  134.7 10.0 %all-to-all-done.1 = bf16[128,8,128]{2,1,0:T(8,128)(2,1)S(1)} async-done(((bf16[128,8,128]{2,1,0:T(8,128)(2,1)}), bf16[128,8,128]{2,1,0:T(8,128)(2,1)S(1)}, u32[]{:S(2)}, u32[]{:S(2)}) %all-to-all-start.1) | async-done | bytes 262176 | tf_op jit(solution)/shard_map/all_to_all | solution.py:365
  (84 shorter events, 23.7 us)
Async XLA Ops:
  3.5 11.3 %collective-permute-start = (s32[1,17]{1,0:T(1,128)S(1)}, s32[1,17]{1,0:T(1,128)S(1)}, u32[]{:S(2)}, u32[]{:S(2)}) collective-permute-start(s32[1,17]{1,0:T(1,128)S(1)} %pad_add_fusion.3), channel_id=1, source_target_pairs={{0,4},{4,8},{8,12},{12,0},{1,5},{5,9},{9,13},{13,1},{2,6},{6,10},{... | collective-permute-start | bytes 212 | tf_op jit(solution)/shard_map/ppermute | solution.py:272
  5.6 10.4 %collective-permute-start.1 = (s32[1,17]{1,0:T(1,128)S(1)}, s32[1,17]{1,0:T(1,128)S(1)}, u32[]{:S(2)}, u32[]{:S(2)}) collective-permute-start(s32[1,17]{1,0:T(1,128)S(1)} %pad_add_fusion.3), channel_id=1, source_target_pairs={{0,8},{4,12},{8,0},{12,4},{1,9},{5,13},{9,1},{13,5},{2,10},{6,14},... | collective-permute-start | bytes 212 | tf_op jit(solution)/shard_map/ppermute | solution.py:272
  8.2 7.8 %collective-permute-start.2 = (s32[1,17]{1,0:T(1,128)S(1)}, s32[1,17]{1,0:T(1,128)S(1)}, u32[]{:S(2)}, u32[]{:S(2)}) collective-permute-start(s32[1,17]{1,0:T(1,128)S(1)} %pad_add_fusion.3), channel_id=1, source_target_pairs={{0,12},{4,0},{8,4},{12,8},{1,13},{5,1},{9,5},{13,9},{2,14},{6,2},{... | collective-permute-start | bytes 212 | tf_op jit(solution)/shard_map/ppermute | solution.py:272
  9.3 6.7 %collective-permute-start.3 = (bf16[4,128,128]{2,1,0:T(8,128)(2,1)S(1)}, bf16[4,128,128]{2,1,0:T(8,128)(2,1)S(1)}, u32[]{:S(2)}, u32[]{:S(2)}) collective-permute-start(bf16[4,128,128]{2,1,0:T(8,128)(2,1)S(1)} %bitcast.38), channel_id=1, source_target_pairs={{0,1},{1,2},{2,3},{3,0},{4,5},{5,6},{6,7},{7,4},{8,9},{9,10},{10,1... | collective-permute-start | bytes 393224 | tf_op jit(solution)/shard_map/ppermute | solution.py:272
  10.5 9.1 %collective-permute-start.4 = (bf16[4,128,128]{2,1,0:T(8,128)(2,1)S(1)}, bf16[4,128,128]{2,1,0:T(8,128)(2,1)S(1)}, u32[]{:S(2)}, u32[]{:S(2)}) collective-permute-start(bf16[4,128,128]{2,1,0:T(8,128)(2,1)S(1)} %bitcast.39), channel_id=1, source_target_pairs={{0,2},{1,3},{2,0},{3,1},{4,6},{5,7},{6,4},{7,5},{8,10},{9,11},{10,... | collective-permute-start | bytes 393224 | tf_op jit(solution)/shard_map/ppermute | solution.py:272
  17.2 9.1 %collective-permute-start.10 = (bf16[4,128,128]{2,1,0:T(8,128)(2,1)S(1)}, bf16[4,128,128]{2,1,0:T(8,128)(2,1)S(1)}, u32[]{:S(2)}, u32[]{:S(2)}) collective-permute-start(bf16[4,128,128]{2,1,0:T(8,128)(2,1)S(1)} %bitcast.46), channel_id=1, source_target_pairs={{0,16},{16,0},{1,17},{17,1},{2,18},{18,2},{3,19},{19,3},{4,20},{20... | collective-permute-start | bytes 393224 | tf_op jit(solution)/shard_map/ppermute | solution.py:272
  20.5 10.8 %collective-permute-start.7 = (bf16[8,128,128]{2,1,0:T(8,128)(2,1)S(1)}, bf16[8,128,128]{2,1,0:T(8,128)(2,1)S(1)}, u32[]{:S(2)}, u32[]{:S(2)}) collective-permute-start(bf16[8,128,128]{2,1,0:T(8,128)(2,1)S(1)} %get-tuple-element.31), channel_id=1, source_target_pairs={{0,4},{4,8},{8,12},{12,0},{1,5},{5,9},{9,13},{13,1},{2,6},{6,10},{... | collective-permute-start | bytes 786440 | tf_op jit(solution)/shard_map/ppermute | solution.py:272
  21.0 13.8 %collective-permute-start.8 = (bf16[8,128,128]{2,1,0:T(8,128)(2,1)S(1)}, bf16[8,128,128]{2,1,0:T(8,128)(2,1)S(1)}, u32[]{:S(2)}, u32[]{:S(2)}) collective-permute-start(bf16[8,128,128]{2,1,0:T(8,128)(2,1)S(1)} %get-tuple-element.32), channel_id=1, source_target_pairs={{0,8},{4,12},{8,0},{12,4},{1,9},{5,13},{9,1},{13,5},{2,10},{6,14},... | collective-permute-start | bytes 786440 | tf_op jit(solution)/shard_map/ppermute | solution.py:272
  21.6 13.4 %collective-permute-start.9 = (bf16[8,128,128]{2,1,0:T(8,128)(2,1)S(1)}, bf16[8,128,128]{2,1,0:T(8,128)(2,1)S(1)}, u32[]{:S(2)}, u32[]{:S(2)}) collective-permute-start(bf16[8,128,128]{2,1,0:T(8,128)(2,1)S(1)} %get-tuple-element.33), channel_id=1, source_target_pairs={{0,12},{4,0},{8,4},{12,8},{1,13},{5,1},{9,5},{13,9},{2,14},{6,2},{... | collective-permute-start | bytes 786440 | tf_op jit(solution)/shard_map/ppermute | solution.py:272
  26.3 10.5 %collective-permute-start.11 = (bf16[8,128,128]{2,1,0:T(8,128)(2,1)S(1)}, bf16[8,128,128]{2,1,0:T(8,128)(2,1)S(1)}, u32[]{:S(2)}, u32[]{:S(2)}) collective-permute-start(bf16[8,128,128]{2,1,0:T(8,128)(2,1)S(1)} %pad_maximum_fusion.right0), channel_id=1, source_target_pairs={{0,32},{32,64},{64,96},{96,0},{1,33},{33,65},{65,97},{97,1},{2,34}... | collective-permute-start | bytes 786440 | tf_op jit(solution)/shard_map/ppermute | solution.py:272
  28.0 15.4 %collective-permute-start.12 = (bf16[8,128,128]{2,1,0:T(8,128)(2,1)S(1)}, bf16[8,128,128]{2,1,0:T(8,128)(2,1)S(1)}, u32[]{:S(2)}, u32[]{:S(2)}) collective-permute-start(bf16[8,128,128]{2,1,0:T(8,128)(2,1)S(1)} %pad_maximum_fusion.right0), channel_id=1, source_target_pairs={{0,64},{32,96},{64,0},{96,32},{1,65},{33,97},{65,1},{97,33},{2,66}... | collective-permute-start | bytes 786440 | tf_op jit(solution)/shard_map/ppermute | solution.py:272
  31.3 12.1 %collective-permute-start.13 = (bf16[8,128,128]{2,1,0:T(8,128)(2,1)S(1)}, bf16[8,128,128]{2,1,0:T(8,128)(2,1)S(1)}, u32[]{:S(2)}, u32[]{:S(2)}) collective-permute-start(bf16[8,128,128]{2,1,0:T(8,128)(2,1)S(1)} %pad_maximum_fusion.right0), channel_id=1, source_target_pairs={{0,96},{32,0},{64,32},{96,64},{1,97},{33,1},{65,33},{97,65},{2,98}... | collective-permute-start | bytes 786440 | tf_op jit(solution)/shard_map/ppermute | solution.py:272
  55.1 24.8 %collective-permute-start.17 = (bf16[8,128,128]{2,1,0:T(8,128)(2,1)S(1)}, bf16[8,128,128]{2,1,0:T(8,128)(2,1)S(1)}, u32[]{:S(2)}, u32[]{:S(2)}) collective-permute-start(bf16[8,128,128]{2,1,0:T(8,128)(2,1)S(1)} %get-tuple-element.39.refs_0_), channel_id=1, source_target_pairs={{0,16},{16,0},{1,17},{17,1},{2,18},{18,2},{3,19},{19,3},{4,20},{20... | collective-permute-start | bytes 786440 | tf_op jit(solution)/shard_map/ppermute | solution.py:272
  55.2 32.3 %collective-permute-start.14 = (bf16[8,128,128]{2,1,0:T(8,128)(2,1)S(1)}, bf16[8,128,128]{2,1,0:T(8,128)(2,1)S(1)}, u32[]{:S(2)}, u32[]{:S(2)}) collective-permute-start(bf16[8,128,128]{2,1,0:T(8,128)(2,1)S(1)} %get-tuple-element.38.refs_0_), channel_id=1, source_target_pairs={{0,4},{4,8},{8,12},{12,0},{1,5},{5,9},{9,13},{13,1},{2,6},{6,10},{... | collective-permute-start | bytes 786440 | tf_op jit(solution)/shard_map/ppermute | solution.py:272
  73.6 18.7 %collective-permute-start.15 = (bf16[8,128,128]{2,1,0:T(8,128)(2,1)S(1)}, bf16[8,128,128]{2,1,0:T(8,128)(2,1)S(1)}, u32[]{:S(2)}, u32[]{:S(2)}) collective-permute-start(bf16[8,128,128]{2,1,0:T(8,128)(2,1)S(1)} %get-tuple-element.38.refs_0_), channel_id=1, source_target_pairs={{0,8},{4,12},{8,0},{12,4},{1,9},{5,13},{9,1},{13,5},{2,10},{6,14},... | collective-permute-start | bytes 786440 | tf_op jit(solution)/shard_map/ppermute | solution.py:272
  79.9 12.4 %collective-permute-start.16 = (bf16[8,128,128]{2,1,0:T(8,128)(2,1)S(1)}, bf16[8,128,128]{2,1,0:T(8,128)(2,1)S(1)}, u32[]{:S(2)}, u32[]{:S(2)}) collective-permute-start(bf16[8,128,128]{2,1,0:T(8,128)(2,1)S(1)} %get-tuple-element.38.refs_0_), channel_id=1, source_target_pairs={{0,12},{4,0},{8,4},{12,8},{1,13},{5,1},{9,5},{13,9},{2,14},{6,2},{... | collective-permute-start | bytes 786440 | tf_op jit(solution)/shard_map/ppermute | solution.py:272
  80.9 11.4 %collective-permute-start.18 = (bf16[4,128,128]{2,1,0:T(8,128)(2,1)S(1)}, bf16[4,128,128]{2,1,0:T(8,128)(2,1)S(1)}, u32[]{:S(2)}, u32[]{:S(2)}) collective-permute-start(bf16[4,128,128]{2,1,0:T(8,128)(2,1)S(1)} %get-tuple-element.40), channel_id=1, source_target_pairs={{0,32},{32,64},{64,96},{96,0},{1,33},{33,65},{65,97},{97,1},{2,34}... | collective-permute-start | bytes 393224 | tf_op jit(solution)/shard_map/ppermute | solution.py:272
  87.5 5.3 %collective-permute-start.19 = (bf16[4,128,128]{2,1,0:T(8,128)(2,1)S(1)}, bf16[4,128,128]{2,1,0:T(8,128)(2,1)S(1)}, u32[]{:S(2)}, u32[]{:S(2)}) collective-permute-start(bf16[4,128,128]{2,1,0:T(8,128)(2,1)S(1)} %get-tuple-element.41), channel_id=1, source_target_pairs={{0,64},{32,96},{64,0},{96,32},{1,65},{33,97},{65,1},{97,33},{2,66}... | collective-permute-start | bytes 393224 | tf_op jit(solution)/shard_map/ppermute | solution.py:272
  87.5 7.5 %collective-permute-start.20 = (bf16[4,128,128]{2,1,0:T(8,128)(2,1)S(1)}, bf16[4,128,128]{2,1,0:T(8,128)(2,1)S(1)}, u32[]{:S(2)}, u32[]{:S(2)}) collective-permute-start(bf16[4,128,128]{2,1,0:T(8,128)(2,1)S(1)} %get-tuple-element.42), channel_id=1, source_target_pairs={{0,96},{32,0},{64,32},{96,64},{1,97},{33,1},{65,33},{97,65},{2,98}... | collective-permute-start | bytes 393224 | tf_op jit(solution)/shard_map/ppermute | solution.py:272
  96.3 7.4 %collective-permute-start.21 = (bf16[4,128,128]{2,1,0:T(8,128)(2,1)S(1)}, bf16[4,128,128]{2,1,0:T(8,128)(2,1)S(1)}, u32[]{:S(2)}, u32[]{:S(2)}) collective-permute-start(bf16[4,128,128]{2,1,0:T(8,128)(2,1)S(1)} %get-tuple-element.47), channel_id=1, source_target_pairs={{0,1},{1,2},{2,3},{3,0},{4,5},{5,6},{6,7},{7,4},{8,9},{9,10},{10,1... | collective-permute-start | bytes 393224 | tf_op jit(solution)/shard_map/ppermute | solution.py:272
  100.4 6.9 %collective-permute-start.22 = (bf16[4,128,128]{2,1,0:T(8,128)(2,1)S(1)}, bf16[4,128,128]{2,1,0:T(8,128)(2,1)S(1)}, u32[]{:S(2)}, u32[]{:S(2)}) collective-permute-start(bf16[4,128,128]{2,1,0:T(8,128)(2,1)S(1)} %get-tuple-element.48), channel_id=1, source_target_pairs={{0,2},{1,3},{2,0},{3,1},{4,6},{5,7},{6,4},{7,5},{8,10},{9,11},{10,... | collective-permute-start | bytes 393224 | tf_op jit(solution)/shard_map/ppermute | solution.py:272
  102.6 5.5 %collective-permute-start.23 = (bf16[4,128,128]{2,1,0:T(8,128)(2,1)S(1)}, bf16[4,128,128]{2,1,0:T(8,128)(2,1)S(1)}, u32[]{:S(2)}, u32[]{:S(2)}) collective-permute-start(bf16[4,128,128]{2,1,0:T(8,128)(2,1)S(1)} %get-tuple-element.49), channel_id=1, source_target_pairs={{0,3},{1,0},{2,1},{3,2},{4,7},{5,4},{6,5},{7,6},{8,11},{9,8},{10,9... | collective-permute-start | bytes 393224 | tf_op jit(solution)/shard_map/ppermute | solution.py:272
  109.7 18.6 %all-to-all-start = ((bf16[128,7,128]{2,1,0:T(8,128)(2,1)}), bf16[128,7,128]{2,1,0:T(8,128)(2,1)S(1)}, u32[]{:S(2)}, u32[]{:S(2)}) async-start(bf16[128,7,128]{2,1,0:T(8,128)(2,1)} %reshape.51), calls=%async_computation | async-start | bytes 524288 | tf_op jit(solution)/shard_map/all_to_all | solution.py:362
  129.2 15.5 %all-to-all-start.1 = ((bf16[128,8,128]{2,1,0:T(8,128)(2,1)}), bf16[128,8,128]{2,1,0:T(8,128)(2,1)S(1)}, u32[]{:S(2)}, u32[]{:S(2)}) async-start(bf16[128,8,128]{2,1,0:T(8,128)(2,1)} %broadcast_in_dim.14), calls=%async_computation.1 | async-start | bytes 524288 | tf_op jit(solution)/shard_map/all_to_all | solution.py:365
  (6 other events, 233.5 us)
